TPU v7x, 512 devices: a whole 4x4x16 slice. The times are simulated.
512 devices in a mesh: frame: 8 (over z_lo, core), seq: 64 (over y, z_hi, x).
Axes of the slice: x: 4, y: 4, z: 16 (z_hi: 4, z_lo: 4; z = z_hi * 4 + z_lo), core: 2. Of those that a mesh axis runs over, the one named last changes fastest.
Arguments:
- queries: bfloat16 [64, 1024, 3072], P('frame', 'seq'), may hold values from -140 to 140
- keys: bfloat16 [64, 1024, 3072], P('frame', 'seq'), may hold values from -6 to 6
- values: bfloat16 [64, 1024, 3072], P('frame', 'seq'), may hold values from -6 to 6
- ref_keys: bfloat16 [1536, 3072], P(('frame', 'seq')), may hold values from -6 to 6
- ref_values: bfloat16 [1536, 3072], P(('frame', 'seq')), may hold values from -6 to 6
Outputs:
- attended: bfloat16 [64, 1024, 3072], P('frame', 'seq')
All inputs are finite; a program needn't handle non-finite values.
Results may differ from a plain program's by a relative error of at most 0.0055.
Values may be sent and summed in bfloat16 or wider, within the bound.
No kernel may reach another device: no remote copies, remote signals or barrier semaphores. Data moves between devices by JAX's collectives and lax.ppermute only.
A program may use at most 64 MiB of HBM per device.

v0:
```python
from functools import partial
import math

import jax
import jax.numpy as jnp
from jax import lax
from jax.sharding import PartitionSpec as P

HD = 128


def head_major(tensor, frames_dev, rows_dev, head_groups, group_width):
    shaped = tensor.reshape(frames_dev, rows_dev, head_groups, group_width).transpose(0, 2, 1, 3)
    return shaped.reshape(frames_dev * head_groups, rows_dev, group_width)


def spread_heads(tensor, frames_dev, head_groups, group_width):
    rows_here = tensor.shape[0]
    split_up = tensor.reshape(rows_here, head_groups, group_width).transpose(1, 0, 2)
    return jnp.tile(split_up, (frames_dev, 1, 1))


def spatial_head(operands, block_rows, scaling):
    query_head, key_head, value_head, ref_key_head, ref_value_head = operands
    frame_len = query_head.shape[0]
    query_blocks = query_head.reshape(frame_len // block_rows, block_rows, query_head.shape[1])
    all_keys = jnp.concatenate([key_head, ref_key_head], axis=0)
    all_values = jnp.concatenate([value_head, ref_value_head], axis=0)

    def one_block(query_block):
        scores = (
            jnp.einsum("qd,kd->qk", query_block, all_keys, preferred_element_type=jnp.float32)
            * scaling
        )
        highest = jnp.max(scores, axis=1, keepdims=True)
        weights = jnp.exp(scores - highest)
        totals = jnp.sum(weights, axis=1, keepdims=True)
        numerator = jnp.dot(
            weights.astype(jnp.bfloat16), all_values, preferred_element_type=jnp.float32
        )
        return (numerator / totals).astype(jnp.bfloat16)

    return lax.map(one_block, query_blocks).reshape(frame_len, query_head.shape[1])


def local(queries, keys, values, ref_keys, ref_values):
    frames_dev, rows_dev, width = queries.shape
    seq_count = lax.axis_size("seq")
    head_groups = seq_count // frames_dev
    group_width = width // head_groups
    heads_dev = group_width // HD
    heads_all = width // HD
    scaling = 1.0 / math.sqrt(HD)
    head_query, head_key, head_value = (
        lax.all_to_all(
            head_major(queries, frames_dev, rows_dev, head_groups, group_width),
            "seq",
            split_axis=0,
            concat_axis=1,
            tiled=True,
        ),
        lax.all_to_all(
            head_major(keys, frames_dev, rows_dev, head_groups, group_width),
            "seq",
            split_axis=0,
            concat_axis=1,
            tiled=True,
        ),
        lax.all_to_all(
            head_major(values, frames_dev, rows_dev, head_groups, group_width),
            "seq",
            split_axis=0,
            concat_axis=1,
            tiled=True,
        ),
    )
    ref_key_all, ref_value_all = (
        lax.all_gather(ref_keys, "frame", axis=0, tiled=True),
        lax.all_gather(ref_values, "frame", axis=0, tiled=True),
    )
    ref_key_group, ref_value_group = (
        lax.all_to_all(
            spread_heads(ref_key_all, frames_dev, head_groups, group_width),
            "seq",
            split_axis=0,
            concat_axis=1,
            tiled=True,
        ),
        lax.all_to_all(
            spread_heads(ref_value_all, frames_dev, head_groups, group_width),
            "seq",
            split_axis=0,
            concat_axis=1,
            tiled=True,
        ),
    )

    def by_head(tensor):
        length = tensor.shape[1]
        return tensor.reshape(length, heads_dev, HD).transpose(1, 0, 2)

    frame_len = head_query.shape[1]
    block_rows = min(512, frame_len)
    spatial_heads = lax.map(
        partial(spatial_head, block_rows=block_rows, scaling=scaling),
        (
            by_head(head_query),
            by_head(head_key),
            by_head(head_value),
            by_head(ref_key_group),
            by_head(ref_value_group),
        ),
    )
    spatial_rows = spatial_heads.transpose(1, 0, 2).reshape(1, frame_len, group_width)
    spatial_back = lax.all_to_all(spatial_rows, "seq", split_axis=1, concat_axis=0, tiled=True)
    spatial = spatial_back.reshape(frames_dev, head_groups, rows_dev, group_width).transpose(
        0, 2, 1, 3
    )
    spatial = spatial.reshape(frames_dev, rows_dev, width)
    pixel_query, pixel_key, pixel_value = (
        lax.all_to_all(queries, "frame", split_axis=1, concat_axis=0, tiled=True),
        lax.all_to_all(keys, "frame", split_axis=1, concat_axis=0, tiled=True),
        lax.all_to_all(values, "frame", split_axis=1, concat_axis=0, tiled=True),
    )
    frames_all = pixel_query.shape[0]
    pixels_dev = pixel_query.shape[1]

    def by_pixel(tensor):
        return tensor.reshape(frames_all, pixels_dev, heads_all, HD)

    scores = (
        jnp.einsum(
            "fphd,gphd->phfg",
            by_pixel(pixel_query),
            by_pixel(pixel_key),
            preferred_element_type=jnp.float32,
        )
        * scaling
    )
    highest = jnp.max(scores, axis=-1, keepdims=True)
    weights = jnp.exp(scores - highest)
    totals = jnp.sum(weights, axis=-1, keepdims=True)
    numerator = jnp.einsum(
        "phfg,gphd->fphd",
        weights.astype(jnp.bfloat16),
        by_pixel(pixel_value),
        preferred_element_type=jnp.float32,
    )
    temporal_pixels = (numerator / jnp.transpose(totals, (2, 0, 1, 3))).astype(jnp.bfloat16)
    temporal_pixels = temporal_pixels.reshape(frames_all, pixels_dev, width)
    temporal = lax.all_to_all(temporal_pixels, "frame", split_axis=0, concat_axis=1, tiled=True)
    return (spatial.astype(jnp.float32) + temporal.astype(jnp.float32)).astype(jnp.bfloat16)


def solution(mesh):
    return jax.shard_map(
        local,
        mesh=mesh,
        in_specs=(
            P("frame", "seq", None),
            P("frame", "seq", None),
            P("frame", "seq", None),
            P(("frame", "seq"), None),
            P(("frame", "seq"), None),
        ),
        out_specs=P("frame", "seq", None),
        check_vma=False,
    )
```

profile of v0, /device:TPU:32, one launch (start us, length us, event | category | flops | bytes accessed | tf_op | source)
XLA Modules:
  0.0 498.5 jit_solution(104447328543442279)
XLA Ops:
  2.5 8.9 %all-to-all-start.7 = ((bf16[8,16,3072]{2,0,1:T(8,128)(2,1)}), bf16[8,16,3072]{2,0,1:T(8,128)(2,1)S(1)}, u32[]{:S(2)}, u32[]{:S(2)}) async-start(bf16[8,16,3072]{2,0,1:T(8,128)(2,1)} %copy.65), calls=%async_computation.7 | async-start | bytes 1572864 | tf_op jit(solution)/shard_map/all_to_all | solution.py:122
  12.8 16.2 %all-to-all-done.7 = bf16[8,16,3072]{2,0,1:T(8,128)(2,1)S(1)} async-done(((bf16[8,16,3072]{2,0,1:T(8,128)(2,1)}), bf16[8,16,3072]{2,0,1:T(8,128)(2,1)S(1)}, u32[]{:S(2)}, u32[]{:S(2)}) %all-to-all-start.7) | async-done | bytes 786464 | tf_op jit(solution)/shard_map/all_to_all | solution.py:122
  29.0 7.0 %all-to-all-start.6 = ((bf16[8,16,3072]{2,0,1:T(8,128)(2,1)}), bf16[8,16,3072]{2,0,1:T(8,128)(2,1)S(1)}, u32[]{:S(2)}, u32[]{:S(2)}) async-start(bf16[8,16,3072]{2,0,1:T(8,128)(2,1)} %copy.63), calls=%async_computation.6 | async-start | bytes 1572864 | tf_op jit(solution)/shard_map/all_to_all | solution.py:121
  37.3 16.1 %all-to-all-done.6 = bf16[8,16,3072]{2,0,1:T(8,128)(2,1)S(1)} async-done(((bf16[8,16,3072]{2,0,1:T(8,128)(2,1)}), bf16[8,16,3072]{2,0,1:T(8,128)(2,1)S(1)}, u32[]{:S(2)}, u32[]{:S(2)}) %all-to-all-start.6) | async-done | bytes 786464 | tf_op jit(solution)/shard_map/all_to_all | solution.py:121
  53.4 7.0 %all-to-all-start.8 = ((bf16[8,16,3072]{2,0,1:T(8,128)(2,1)}), bf16[8,16,3072]{2,0,1:T(8,128)(2,1)S(1)}, u32[]{:S(2)}, u32[]{:S(2)}) async-start(bf16[8,16,3072]{2,0,1:T(8,128)(2,1)} %copy.69), calls=%async_computation.8 | async-start | bytes 1572864 | tf_op jit(solution)/shard_map/all_to_all | solution.py:123
  61.6 16.3 %all-to-all-done.8 = bf16[8,16,3072]{2,0,1:T(8,128)(2,1)S(1)} async-done(((bf16[8,16,3072]{2,0,1:T(8,128)(2,1)}), bf16[8,16,3072]{2,0,1:T(8,128)(2,1)S(1)}, u32[]{:S(2)}, u32[]{:S(2)}) %all-to-all-start.8) | async-done | bytes 786464 | tf_op jit(solution)/shard_map/all_to_all | solution.py:123
  78.8 15.8 %all-to-all-start = ((bf16[64,16,384]{2,1,0:T(8,128)(2,1)}), bf16[64,16,384]{2,1,0:T(8,128)(2,1)S(1)}, u32[]{:S(2)}, u32[]{:S(2)}) async-start(bf16[64,16,384]{2,1,0:T(8,128)(2,1)} %bitcast.147), calls=%async_computation | async-start | bytes 1572864 | tf_op jit(solution)/shard_map/all_to_all | solution.py:55
  95.8 41.1 %all-to-all-done = bf16[64,16,384]{2,1,0:T(8,128)(2,1)S(1)} async-done(((bf16[64,16,384]{2,1,0:T(8,128)(2,1)}), bf16[64,16,384]{2,1,0:T(8,128)(2,1)S(1)}, u32[]{:S(2)}, u32[]{:S(2)}) %all-to-all-start) | async-done | bytes 786464 | tf_op jit(solution)/shard_map/all_to_all | solution.py:55
  136.9 9.7 %all-to-all-start.1 = ((bf16[64,16,384]{2,1,0:T(8,128)(2,1)}), bf16[64,16,384]{2,1,0:T(8,128)(2,1)S(1)}, u32[]{:S(2)}, u32[]{:S(2)}) async-start(bf16[64,16,384]{2,1,0:T(8,128)(2,1)} %bitcast.12), calls=%async_computation.1 | async-start | bytes 1572864 | tf_op jit(solution)/shard_map/all_to_all | solution.py:62
  147.9 28.4 %all-to-all-done.1 = bf16[64,16,384]{2,1,0:T(8,128)(2,1)S(1)} async-done(((bf16[64,16,384]{2,1,0:T(8,128)(2,1)}), bf16[64,16,384]{2,1,0:T(8,128)(2,1)S(1)}, u32[]{:S(2)}, u32[]{:S(2)}) %all-to-all-start.1) | async-done | bytes 786464 | tf_op jit(solution)/shard_map/all_to_all | solution.py:62
  176.3 19.1 %all-to-all-start.3 = ((bf16[64,16,384]{2,1,0:T(8,128)(2,1)}), bf16[64,16,384]{2,1,0:T(8,128)(2,1)S(1)}, u32[]{:S(2)}, u32[]{:S(2)}) async-start(bf16[64,16,384]{2,1,0:T(8,128)(2,1)} %bitcast.19), calls=%async_computation.3 | async-start | bytes 1572864 | tf_op jit(solution)/shard_map/all_to_all | solution.py:69
  195.4 33.8 %all-gather = bf16[8,3,3072]{2,1,0:T(4,128)(2,1)S(1)} all-gather(bf16[1,3,3072]{2,1,0:T(4,128)(2,1)S(1)} %bitcast.161), channel_id=1, replica_groups=mesh['frame'=8,'seq'=64] {'frame'}, dimensions={0}, use_global_device_ids=true | all-gather | bytes 165888 | tf_op jit(solution)/shard_map/all_gather | solution.py:78
  230.7 14.5 %all-to-all-start.2 = ((bf16[64,24,384]{2,1,0:T(8,128)(2,1)}), bf16[64,24,384]{2,1,0:T(8,128)(2,1)S(1)}, u32[]{:S(2)}, u32[]{:S(2)}) async-start(bf16[64,24,384]{2,1,0:T(8,128)(2,1)} %bitcast.16), calls=%async_computation.2 | async-start | bytes 2359296 | tf_op jit(solution)/shard_map/all_to_all | solution.py:82
  245.2 62.7 %all-gather.1 = bf16[8,3,3072]{2,1,0:T(4,128)(2,1)S(1)} all-gather(bf16[1,3,3072]{2,1,0:T(4,128)(2,1)S(1)} %bitcast.162), channel_id=1, replica_groups=mesh['frame'=8,'seq'=64] {'frame'}, dimensions={0}, use_global_device_ids=true | all-gather | bytes 165888 | tf_op jit(solution)/shard_map/all_gather | solution.py:79
  309.3 15.4 %all-to-all-start.4 = ((bf16[64,24,384]{2,1,0:T(8,128)(2,1)}), bf16[64,24,384]{2,1,0:T(8,128)(2,1)}, u32[]{:S(2)}, u32[]{:S(2)}) async-start(bf16[64,24,384]{2,1,0:T(8,128)(2,1)} %bitcast.23), calls=%async_computation.4 | async-start | bytes 2359296 | tf_op jit(solution)/shard_map/all_to_all | solution.py:89
  335.6 46.2 %all-to-all-done.4 = bf16[64,24,384]{2,1,0:T(8,128)(2,1)} async-done(((bf16[64,24,384]{2,1,0:T(8,128)(2,1)}), bf16[64,24,384]{2,1,0:T(8,128)(2,1)}, u32[]{:S(2)}, u32[]{:S(2)}) %all-to-all-start.4) | async-done | bytes 1179680 | tf_op jit(solution)/shard_map/all_to_all | solution.py:89
  381.8 7.7 %all-to-all-start.9 = ((bf16[64,2,3072]{2,1,0:T(2,128)(2,1)}), bf16[64,2,3072]{2,1,0:T(2,128)(2,1)}, u32[]{:S(2)}, u32[]{:S(2)}) async-start(bf16[64,2,3072]{2,1,0:T(2,128)(2,1)} %reshape.136), calls=%async_computation.9 | async-start | bytes 1572864 | tf_op jit(solution)/shard_map/all_to_all | solution.py:151
  394.0 28.8 %while.21 = (s32[]{:T(128)}, bf16[3,1024,128]{1,2,0:T(8,128)(2,1)}, bf16[3,1024,128]{2,1,0:T(8,128)(2,1)}, bf16[3,1024,128]{2,1,0:T(8,128)(2,1)}, bf16[3,1536,12...) while((s32[]{:T(128)}, bf16[3,1024,128]{1,2,0:T(8,128)(2,1)}, ...), condition=%wide.region_5.6_spmd, body=%wide.region_0.5_spmd.sunk | while | flops 681704448 | bytes 24127752 | solution.py:104
  397.2 5.5 %while.22 = (s32[]{:T(128)}, bf16[2,512,128]{2,1,0:T(8,128)(2,1)S(1)}, bf16[2,512,128]{2,1,0:T(8,128)(2,1)S(1)}, bf16[2560,128]{1,0:T(8,128)(2,1)S(1)}, bf16[2560,128]{1,0:T(8,128)(2,1)S(1)}, /*index=5*/s32[]{:T(128)}) while((s32[]{:T(128)}, bf16[2,512,128]{2,1,0:T(8,128)(2,1)S(1)}, bf16[2,512,128]{2,1,0:T(8,128)(2,1)S(1)}, ...), condition=%wide.region_4.4_spmd, body=%wide.region_1.3_spmd.sunk | while | flops 679083008 | bytes 17311828 | solution.py:43
  406.8 5.5 %while.22 = (s32[]{:T(128)}, bf16[2,512,128]{2,1,0:T(8,128)(2,1)S(1)}, bf16[2,512,128]{2,1,0:T(8,128)(2,1)S(1)}, bf16[2560,128]{1,0:T(8,128)(2,1)S(1)}, bf16[2560,128]{1,0:T(8,128)(2,1)S(1)}, /*index=5*/s32[]{:T(128)}) while((s32[]{:T(128)}, bf16[2,512,128]{2,1,0:T(8,128)(2,1)S(1)}, bf16[2,512,128]{2,1,0:T(8,128)(2,1)S(1)}, ...), condition=%wide.region_4.4_spmd, body=%wide.region_1.3_spmd.sunk | while | flops 679083008 | bytes 17311828 | solution.py:43
  416.4 5.5 %while.22 = (s32[]{:T(128)}, bf16[2,512,128]{2,1,0:T(8,128)(2,1)S(1)}, bf16[2,512,128]{2,1,0:T(8,128)(2,1)S(1)}, bf16[2560,128]{1,0:T(8,128)(2,1)S(1)}, bf16[2560,128]{1,0:T(8,128)(2,1)S(1)}, /*index=5*/s32[]{:T(128)}) while((s32[]{:T(128)}, bf16[2,512,128]{2,1,0:T(8,128)(2,1)S(1)}, bf16[2,512,128]{2,1,0:T(8,128)(2,1)S(1)}, ...), condition=%wide.region_4.4_spmd, body=%wide.region_1.3_spmd.sunk | while | flops 679083008 | bytes 17311828 | solution.py:43
  427.4 5.4 %reduce = bf16[1024,384]{1,0:T(8,128)(2,1)S(1)} reduce(bf16[1024,1,384]{2,1,0:T(2,128)(2,1)S(1)} %bitcast.132, bf16[]{:T(256)} %broadcast.16), dimensions={1}, to_apply=%bitcast.105.reduce_sub_computation | reduce | bytes 1572866
  433.9 10.5 %all-to-all-start.5 = ((bf16[64,2,3072]{2,1,0:T(2,128)(2,1)}), bf16[64,2,3072]{2,1,0:T(2,128)(2,1)}, u32[]{:S(2)}, u32[]{:S(2)}) async-start(bf16[64,2,3072]{2,1,0:T(2,128)(2,1)} %reshape.137), calls=%async_computation.5 | async-start | bytes 1572864 | tf_op jit(solution)/shard_map/all_to_all | solution.py:115
  445.9 45.4 %all-to-all-done.5 = bf16[64,2,3072]{2,1,0:T(2,128)(2,1)} async-done(((bf16[64,2,3072]{2,1,0:T(2,128)(2,1)}), bf16[64,2,3072]{2,1,0:T(2,128)(2,1)}, u32[]{:S(2)}, u32[]{:S(2)}) %all-to-all-start.5) | async-done | bytes 786464 | tf_op jit(solution)/shard_map/all_to_all | solution.py:115
  (125 shorter events, 70.7 us)
Async XLA Ops:
  0.0 11.5 %copy-start.4 = (bf16[8,16,3072]{2,1,0:T(8,128)(2,1)S(1)}, bf16[8,16,3072]{2,1,0:T(8,128)(2,1)}, u32[]{:S(2)}) copy-start(bf16[8,16,3072]{2,1,0:T(8,128)(2,1)} %param.9) | copy-start | bytes 2359300
  2.5 26.4 %all-to-all-start.7 = ((bf16[8,16,3072]{2,0,1:T(8,128)(2,1)}), bf16[8,16,3072]{2,0,1:T(8,128)(2,1)S(1)}, u32[]{:S(2)}, u32[]{:S(2)}) async-start(bf16[8,16,3072]{2,0,1:T(8,128)(2,1)} %copy.65), calls=%async_computation.7 | async-start | bytes 1572864 | tf_op jit(solution)/shard_map/all_to_all | solution.py:122
  11.5 24.5 %copy-start.6 = (bf16[8,16,3072]{2,1,0:T(8,128)(2,1)S(1)}, bf16[8,16,3072]{2,1,0:T(8,128)(2,1)}, u32[]{:S(2)}) copy-start(bf16[8,16,3072]{2,1,0:T(8,128)(2,1)} %param.11) | copy-start | bytes 2359300
  29.0 8.3 %copy-start.7 = (bf16[8,16,3072]{2,0,1:T(8,128)(2,1)}, bf16[8,16,3072]{2,0,1:T(8,128)(2,1)S(1)}, u32[]{:S(2)}) copy-start(bf16[8,16,3072]{2,0,1:T(8,128)(2,1)S(1)} %all-to-all-done.7) | copy-start | bytes 2359300
  29.0 24.5 %all-to-all-start.6 = ((bf16[8,16,3072]{2,0,1:T(8,128)(2,1)}), bf16[8,16,3072]{2,0,1:T(8,128)(2,1)S(1)}, u32[]{:S(2)}, u32[]{:S(2)}) async-start(bf16[8,16,3072]{2,0,1:T(8,128)(2,1)} %copy.63), calls=%async_computation.6 | async-start | bytes 1572864 | tf_op jit(solution)/shard_map/all_to_all | solution.py:121
  53.4 7.1 %copy-start.9 = (bf16[8,16,3072]{2,0,1:T(8,128)(2,1)}, bf16[8,16,3072]{2,0,1:T(8,128)(2,1)S(1)}, u32[]{:S(2)}) copy-start(bf16[8,16,3072]{2,0,1:T(8,128)(2,1)S(1)} %all-to-all-done.6) | copy-start | bytes 2359300
  53.4 24.5 %all-to-all-start.8 = ((bf16[8,16,3072]{2,0,1:T(8,128)(2,1)}), bf16[8,16,3072]{2,0,1:T(8,128)(2,1)S(1)}, u32[]{:S(2)}, u32[]{:S(2)}) async-start(bf16[8,16,3072]{2,0,1:T(8,128)(2,1)} %copy.69), calls=%async_computation.8 | async-start | bytes 1572864 | tf_op jit(solution)/shard_map/all_to_all | solution.py:123
  60.6 34.0 %copy-start.5 = (bf16[8,16,3072]{2,1,0:T(8,128)(2,1)S(1)}, bf16[8,16,3072]{2,1,0:T(8,128)(2,1)}, u32[]{:S(2)}) copy-start(bf16[8,16,3072]{2,1,0:T(8,128)(2,1)} %param.10) | copy-start | bytes 2359300
  78.8 58.1 %all-to-all-start = ((bf16[64,16,384]{2,1,0:T(8,128)(2,1)}), bf16[64,16,384]{2,1,0:T(8,128)(2,1)S(1)}, u32[]{:S(2)}, u32[]{:S(2)}) async-start(bf16[64,16,384]{2,1,0:T(8,128)(2,1)} %bitcast.147), calls=%async_computation | async-start | bytes 1572864 | tf_op jit(solution)/shard_map/all_to_all | solution.py:55
  136.9 39.4 %all-to-all-start.1 = ((bf16[64,16,384]{2,1,0:T(8,128)(2,1)}), bf16[64,16,384]{2,1,0:T(8,128)(2,1)S(1)}, u32[]{:S(2)}, u32[]{:S(2)}) async-start(bf16[64,16,384]{2,1,0:T(8,128)(2,1)} %bitcast.12), calls=%async_computation.1 | async-start | bytes 1572864 | tf_op jit(solution)/shard_map/all_to_all | solution.py:62
  146.8 48.5 %copy-start.13 = (bf16[3,3072]{1,0:T(4,128)(2,1)S(1)}, bf16[3,3072]{1,0:T(4,128)(2,1)}, u32[]{:S(2)}) copy-start(bf16[3,3072]{1,0:T(4,128)(2,1)} %param.12) | copy-start | bytes 55300
  176.3 54.4 %copy-start = (bf16[64,16,384]{2,1,0:T(8,128)(2,1)}, bf16[64,16,384]{2,1,0:T(8,128)(2,1)S(1)}, u32[]{:S(2)}) copy-start(bf16[64,16,384]{2,1,0:T(8,128)(2,1)S(1)} %all-to-all-done.1) | copy-start | bytes 2359300
  176.3 53.1 %all-to-all-start.3 = ((bf16[64,16,384]{2,1,0:T(8,128)(2,1)}), bf16[64,16,384]{2,1,0:T(8,128)(2,1)S(1)}, u32[]{:S(2)}, u32[]{:S(2)}) async-start(bf16[64,16,384]{2,1,0:T(8,128)(2,1)} %bitcast.19), calls=%async_computation.3 | async-start | bytes 1572864 | tf_op jit(solution)/shard_map/all_to_all | solution.py:69
  229.4 15.9 %copy-start.14 = (bf16[3,3072]{1,0:T(4,128)(2,1)S(1)}, bf16[3,3072]{1,0:T(4,128)(2,1)}, u32[]{:S(2)}) copy-start(bf16[3,3072]{1,0:T(4,128)(2,1)} %param.13) | copy-start | bytes 55300
  229.4 1.3 copy-start.2
  230.7 77.4 %all-to-all-start.2 = ((bf16[64,24,384]{2,1,0:T(8,128)(2,1)}), bf16[64,24,384]{2,1,0:T(8,128)(2,1)S(1)}, u32[]{:S(2)}, u32[]{:S(2)}) async-start(bf16[64,24,384]{2,1,0:T(8,128)(2,1)} %bitcast.16), calls=%async_computation.2 | async-start | bytes 2359296 | tf_op jit(solution)/shard_map/all_to_all | solution.py:82
  308.1 16.6 %copy-start.8 = (bf16[8,16,3072]{2,0,1:T(8,128)(2,1)S(1)}, bf16[8,16,3072]{2,0,1:T(8,128)(2,1)}, u32[]{:S(2)}) copy-start(bf16[8,16,3072]{2,0,1:T(8,128)(2,1)} %copy-done.7) | copy-start | bytes 2359300
  309.3 72.5 %all-to-all-start.4 = ((bf16[64,24,384]{2,1,0:T(8,128)(2,1)}), bf16[64,24,384]{2,1,0:T(8,128)(2,1)}, u32[]{:S(2)}, u32[]{:S(2)}) async-start(bf16[64,24,384]{2,1,0:T(8,128)(2,1)} %bitcast.23), calls=%async_computation.4 | async-start | bytes 2359296 | tf_op jit(solution)/shard_map/all_to_all | solution.py:89
  324.7 1.1 copy-start.10
  325.8 1.1 copy-start.12
  330.8 1.4 copy-start.1
  332.4 1.4 copy-start.3
  381.8 52.1 %all-to-all-start.9 = ((bf16[64,2,3072]{2,1,0:T(2,128)(2,1)}), bf16[64,2,3072]{2,1,0:T(2,128)(2,1)}, u32[]{:S(2)}, u32[]{:S(2)}) async-start(bf16[64,2,3072]{2,1,0:T(2,128)(2,1)} %reshape.136), calls=%async_computation.9 | async-start | bytes 1572864 | tf_op jit(solution)/shard_map/all_to_all | solution.py:151
  433.9 57.3 %all-to-all-start.5 = ((bf16[64,2,3072]{2,1,0:T(2,128)(2,1)}), bf16[64,2,3072]{2,1,0:T(2,128)(2,1)}, u32[]{:S(2)}, u32[]{:S(2)}) async-start(bf16[64,2,3072]{2,1,0:T(2,128)(2,1)} %reshape.137), calls=%async_computation.5 | async-start | bytes 1572864 | tf_op jit(solution)/shard_map/all_to_all | solution.py:115
  (1 other events, 0.9 us)
where the time goes:
time: 500 us; the launch traced here: 498 us
  waiting for transfers between devices  210 us (42%)
  starting transfers between devices  116 us (23%)
  blocking collectives  96.5 us (19%)
  local copies, waits for them, and re-layouts  49 us (10%)
  other arithmetic  14.4 us (3%)
  matrix products  12.7 us (3%)
    all_gather x1, blocking collectives, local(): lax.all_gather(ref_values, 'frame', axis=0, tiled=True)  62.7 us
    all_to_all x1, waiting for transfers between devices, local(): lax.all_to_all(spread_heads(ref_value_all, frames_dev, head_groups, group...  46.2 us
    all_to_all x1, waiting for transfers between devices, local(): lax.all_to_all(spatial_rows, 'seq', split_axis=1, concat_axis=0, tiled=True)  45.4 us
    all_to_all x1, waiting for transfers between devices, local(): lax.all_to_all(head_major(queries, frames_dev, rows_dev, head_groups, gro...  41.1 us
    all_gather x1, blocking collectives, local(): lax.all_gather(ref_keys, 'frame', axis=0, tiled=True)  33.8 us
    all_to_all x1, waiting for transfers between devices, local(): lax.all_to_all(head_major(keys, frames_dev, rows_dev, head_groups, group_...  28.4 us
    all_to_all x1, starting transfers between devices, local(): lax.all_to_all(head_major(values, frames_dev, rows_dev, head_groups, grou...  19.1 us
    all_to_all x1, waiting for transfers between devices, local(): lax.all_to_all(values, 'frame', split_axis=1, concat_axis=0, tiled=True)  16.3 us
  transfers between devices with their start and end apart: 10, of which 7 were waited for; matrix products, arithmetic and copies ran while one was open for 12% of the time, Pallas kernels for 0%

commit v1 on v0

v1 whole, which is shorter than its diff:
```python
import math

import jax
import jax.numpy as jnp
from jax import lax
from jax.experimental import pallas as pl
from jax.experimental.pallas import tpu as pltpu
from jax.sharding import Mesh, PartitionSpec as P

HD = 128
LOG2E = 1.4426950408889634
Z = ("zl1", "zl0", "zh")
YX = ("y", "x")
VMEM = pl.BlockSpec(memory_space=pltpu.VMEM)


def head_of(z_index, slot):
    zl1, zl0, zh = z_index // 8, (z_index // 4) % 2, z_index % 4
    pair = zh * 2 + zl1
    return pair * 3 + (1 if slot == 2 else 2 * zl0)


def frame_of(z_index, j, slot):
    zl0 = (z_index // 4) % 2
    return 4 * zl0 + j if slot == 2 else 2 * j + slot


def pack_kernel(q_ref, k_ref, v_ref, out_ref):
    for z in range(16):
        for j in range(4):
            for slot in range(3):
                frame = frame_of(z, j, slot)
                head = head_of(z, slot)
                for t, ref in enumerate((q_ref, k_ref, v_ref)):
                    out_ref[z, j, t, slot] = ref[frame, :, head * HD : (head + 1) * HD]


def pack_refs_kernel(key_ref, value_ref, out_ref):
    for z in range(16):
        for ab, slot in enumerate((0, 2)):
            head = head_of(z, slot)
            for t, ref in enumerate((key_ref, value_ref)):
                out_ref[z, t, ab] = ref[:, head * HD : (head + 1) * HD]


def unpack_kernel(in_ref, out_ref):
    for z in range(16):
        for j in range(4):
            for slot in range(3):
                frame = frame_of(z, j, slot)
                head = head_of(z, slot)
                out_ref[frame, :, head * HD : (head + 1) * HD] = in_ref[z, j, slot]


def spatial_kernel(x_ref, ref_ref, out_ref):
    frame_len = x_ref.shape[0] * 16
    ref_len = ref_ref.shape[0] * ref_ref.shape[3]
    groups = 16
    rows = groups * 16
    scale = LOG2E / math.sqrt(HD)
    nt = (((1,), (1,)), ((), ()))
    for slot in range(3):
        ab = 1 if slot == 2 else 0
        own_k = x_ref[:, 1, slot].reshape(frame_len, HD)
        own_v = x_ref[:, 2, slot].reshape(frame_len, HD)
        ref_k = ref_ref[:, 0, ab].reshape(ref_len, HD)
        ref_v = ref_ref[:, 1, ab].reshape(ref_len, HD)
        for block in range(x_ref.shape[0] // groups):
            at = slice(block * groups, (block + 1) * groups)
            query = x_ref[at, 0, slot].reshape(rows, HD)
            own = lax.dot_general(query, own_k, nt, preferred_element_type=jnp.float32)
            ref = lax.dot_general(query, ref_k, nt, preferred_element_type=jnp.float32)
            highest = jnp.maximum(
                jnp.max(own, axis=1, keepdims=True), jnp.max(ref, axis=1, keepdims=True)
            )
            own = jnp.exp2((own - highest) * scale)
            ref = jnp.exp2((ref - highest) * scale)
            totals = jnp.sum(own, axis=1, keepdims=True) + jnp.sum(ref, axis=1, keepdims=True)
            numerator = jnp.dot(
                own.astype(jnp.bfloat16), own_v, preferred_element_type=jnp.float32
            ) + jnp.dot(ref.astype(jnp.bfloat16), ref_v, preferred_element_type=jnp.float32)
            out_ref[at, slot] = (numerator / totals).astype(jnp.bfloat16).reshape(groups, 16, HD)


def call(kernel, out_shape, *args, flops=0):
    size = sum(a.size * 2 for a in args) + 2 * math.prod(out_shape)
    return pl.pallas_call(
        kernel,
        out_shape=jax.ShapeDtypeStruct(out_shape, jnp.bfloat16),
        in_specs=[VMEM] * len(args),
        out_specs=VMEM,
        compiler_params=pltpu.CompilerParams(vmem_limit_bytes=48 * 1024 * 1024),
        cost_estimate=pl.CostEstimate(flops=flops, bytes_accessed=size, transcendentals=0),
    )(*args)


def temporal_attention(query, key, value):
    scores = jnp.einsum("ftd,gtd->tfg", query, key, preferred_element_type=jnp.float32)
    scores = scores * (1.0 / math.sqrt(HD))
    highest = jnp.max(scores, axis=-1, keepdims=True)
    weights = jnp.exp(scores - highest)
    totals = jnp.sum(weights, axis=-1, keepdims=True)
    numerator = jnp.einsum(
        "tfg,gtd->ftd", weights.astype(jnp.bfloat16), value, preferred_element_type=jnp.float32
    )
    return (numerator / jnp.transpose(totals, (1, 0, 2))).astype(jnp.bfloat16)


def swap(tensor, mask):
    return lax.ppermute(tensor, ("zl0", "core"), [(i, i ^ mask) for i in range(4)])


def local(queries, keys, values, ref_keys, ref_values):
    core = lax.axis_index("core")
    quarter = lax.axis_index("zl0") * 2 + core

    refs = call(pack_refs_kernel, (16, 2, 2, 3, HD), ref_keys, ref_values)
    refs = lax.all_to_all(refs, Z, split_axis=0, concat_axis=0, tiled=True)
    packed = call(pack_kernel, (16, 4, 3, 3, 16, HD), queries, keys, values)
    refs, packed = lax.optimization_barrier((refs, packed))
    refs = refs.transpose(1, 2, 0, 3, 4).reshape(1, 2, 2, 48, HD)
    refs = lax.all_gather(refs, ("core", "y", "x"), axis=0, tiled=True)

    spread = lax.all_to_all(packed, Z, split_axis=0, concat_axis=0, tiled=True)
    spread = spread.reshape(4, 4, 4, 3, 3, 16, HD)

    by_frame = spread.transpose(0, 2, 1, 3, 4, 5, 6).reshape(16, 4, 3, 3, 16, HD)
    by_frame = lax.all_to_all(by_frame, YX, split_axis=0, concat_axis=0, tiled=True)
    by_frame = by_frame.reshape(64, 3, 3, 16, HD)
    spatial = call(
        spatial_kernel, (64, 3, 16, HD), by_frame, refs, flops=4 * 3 * 1024 * 2560 * HD
    )
    spatial = lax.all_to_all(
        spatial.reshape(16, 4, 3, 16, HD), YX, split_axis=0, concat_axis=0, tiled=True
    ).reshape(4, 4, 4, 3, 16, HD)

    first = spread[..., :2, :, :]
    mine = lax.dynamic_slice_in_dim(first, 2 * core, 2, axis=1)
    other = swap(lax.dynamic_slice_in_dim(first, 2 - 2 * core, 2, axis=1), 1)
    both = jnp.stack((mine, other))
    both = both.transpose(4, 0, 1, 3, 5, 2, 6, 7).reshape(3, 64, 32, HD)
    result = temporal_attention(both[0], both[1], both[2])
    result = result.reshape(2, 4, 4, 2, 2, 16, HD)
    mine, other = result[0], swap(result[1], 1)
    is_first = core == 0
    halves = (jnp.where(is_first, mine, other), jnp.where(is_first, other, mine))
    own_head = jnp.concatenate(halves, axis=3).transpose(0, 1, 3, 2, 4, 5)

    middle = spread[..., 2, :, :]
    parts = []
    for mask in range(4):
        part = lax.dynamic_index_in_dim(middle, quarter ^ mask, axis=1, keepdims=False)
        parts.append(swap(part, mask) if mask else part)
    four = jnp.stack(parts)
    four = four.transpose(3, 0, 1, 2, 4, 5).reshape(3, 64, 16, HD)
    result = temporal_attention(four[0], four[1], four[2]).reshape(4, 4, 4, 16, HD)
    parts = jnp.stack([swap(result[mask], mask) if mask else result[0] for mask in range(4)])
    middle_head = jnp.stack(
        [lax.dynamic_index_in_dim(parts, quarter ^ zh, axis=0, keepdims=False) for zh in range(4)],
        axis=2,
    )

    temporal = jnp.concatenate((own_head, middle_head[:, :, :, None]), axis=3)
    attended = (spatial.astype(jnp.float32) + temporal.astype(jnp.float32)).astype(jnp.bfloat16)
    attended = attended.transpose(0, 2, 1, 3, 4, 5).reshape(16, 4, 3, 16, HD)
    attended = lax.all_to_all(attended, Z, split_axis=0, concat_axis=0, tiled=True)
    return call(unpack_kernel, queries.shape, attended)


def solution(mesh):
    split = Mesh(mesh.devices.reshape(2, 2, 2, 4, 4, 4), ("zl1", "zl0", "core", "y", "zh", "x"))
    rows = P(("zl1", "zl0", "core"), ("y", "zh", "x"), None)
    refs = P(("zl1", "zl0", "core", "y", "zh", "x"), None)
    return jax.shard_map(
        local,
        mesh=split,
        in_specs=(rows, rows, rows, refs, refs),
        out_specs=rows,
        check_vma=False,
    )
```

time: 500 us -> 322 us (0.64)
  starting transfers between devices: 116 us -> 55.9 us
  waiting for transfers between devices: 210 us -> 160 us
  blocking collectives: 96.5 us -> 53.8 us
  local copies, waits for them, and re-layouts: 49 us -> 15.3 us
  Pallas kernels: 0 us -> 15.5 us
  between operations: 0.44 us -> 13.8 us
  matrix products: 12.7 us -> 1.58 us
  other arithmetic: 14.4 us -> 4.37 us
    all_gather x2 -> x0, blocking collectives: 96.5 us -> none  [the longest x1 62.7 us: local(): lax.all_gather(ref_values, 'frame', axis=0, tiled=True)]
    all_to_all x10 -> x4, waiting for transfers between devices: 210 us -> 119 us  [the longest x1 101 us: local(): spread = lax.all_to_all(packed, Z, split_axis=0, concat_axis=0, tiled=True)]
    all_to_all x10 -> x4, starting transfers between devices: 116 us -> 32.7 us  [the longest x1 15.2 us: local(): refs = lax.all_to_all(refs, Z, split_axis=0, concat_axis=0, tiled=True)]
    all_to_all x0 -> x1, blocking collectives: none -> 53.8 us  [local(): lax.all_to_all(attended, Z, split_axis=0, concat_axis=0, tiled=True)]
    all_gather x0 -> x1, waiting for transfers between devices: none -> 36.5 us  [local(): refs = lax.all_gather(refs, ('core', 'y', 'x'), axis=0, tiled=True)]
    ppermute x0 -> x8, starting transfers between devices: none -> 23.2 us  [swap(): lax.ppermute(tensor, ('zl0', 'core'), [(i, i ^ mask) for i in range(4)])]
    pallas_call x0 -> x4, Pallas kernels: none -> 15.5 us  [call(): pl.pallas_call(kernel, out_shape=jax.ShapeDtypeStruct(out_shape, jnp.bflo...]
    dot_general x14 -> x4, matrix products: 12.7 us -> 1.58 us  [the longest x2 0.88 us: temporal_attention(): jnp.einsum('tfg,gtd->ftd', weights.astype(jnp.bfloat16), value, preferred...]
  transfers between devices with their start and end apart: 10 -> 13, of which waited for: 7 -> 7; matrix products, arithmetic and copies ran while one was open for 12% -> 4% of each run, Pallas kernels for 0% -> 1%
where the time goes in v1:
time: 322 us; the launch traced here: 321 us
  waiting for transfers between devices  160 us (50%)
  starting transfers between devices  55.9 us (17%)
  blocking collectives  53.8 us (17%)
  Pallas kernels  15.5 us (5%)
  local copies, waits for them, and re-layouts  15.3 us (5%)
  between operations  13.8 us (4%)
  other arithmetic  4.37 us (1%)
    all_to_all x1, waiting for transfers between devices, local(): spread = lax.all_to_all(packed, Z, split_axis=0, concat_axis=0, tiled=True)  101 us
    all_to_all x1, blocking collectives, local(): lax.all_to_all(attended, Z, split_axis=0, concat_axis=0, tiled=True)  53.8 us
    all_gather x1, waiting for transfers between devices, local(): refs = lax.all_gather(refs, ('core', 'y', 'x'), axis=0, tiled=True)  36.5 us
    ppermute x8, starting transfers between devices, swap(): lax.ppermute(tensor, ('zl0', 'core'), [(i, i ^ mask) for i in range(4)])  23.2 us
    pallas_call x4, Pallas kernels, call(): pl.pallas_call(kernel, out_shape=jax.ShapeDtypeStruct(out_shape, jnp.bflo...  15.5 us
    all_to_all x1, starting transfers between devices, local(): refs = lax.all_to_all(refs, Z, split_axis=0, concat_axis=0, tiled=True)  15.2 us
    all_to_all x1, waiting for transfers between devices, local(): lax.all_to_all(spatial.reshape(16, 4, 3, 16, HD), YX, split_axis=0, conca...  11 us
    all_to_all x1, starting transfers between devices, local(): lax.all_to_all(by_frame, YX, split_axis=0, concat_axis=0, tiled=True)  7.07 us
  transfers between devices with their start and end apart: 13, of which 7 were waited for; matrix products, arithmetic and copies ran while one was open for 4% of the time, Pallas kernels for 1%

profile of v1, /device:TPU:32, one launch (start us, length us, event | category | flops | bytes accessed | tf_op | source)
XLA Modules:
  0.0 320.5 jit_solution(6157232070746343191)
XLA Ops:
  8.7 15.2 %all-to-all-start = ((bf16[16,2,2,3,128]{4,2,3,1,0:T(2,128)(2,1)}), bf16[16,2,2,3,128]{4,2,3,1,0:T(2,128)(2,1)S(1)}, u32[]{:S(2)}, u32[]{:S(2)}) async-start(bf16[16,2,2,3,128]{4,2,3,1,0:T(2,128)(2,1)} %copy.40), calls=%async_computation | async-start | bytes 98304 | tf_op jit(solution)/shard_map/all_to_all | solution.py:118
  27.3 1.8 shard_map.56
  29.2 6.6 %all-to-all-done = bf16[16,2,2,3,128]{4,2,3,1,0:T(2,128)(2,1)S(1)} async-done(((bf16[16,2,2,3,128]{4,2,3,1,0:T(2,128)(2,1)}), bf16[16,2,2,3,128]{4,2,3,1,0:T(2,128)(2,1)S(1)}, u32[]{:S(2)}, u32[]{:S(2)}) %all-to-all-start) | async-done | bytes 49184 | tf_op jit(solution)/shard_map/all_to_all | solution.py:118
  35.7 5.5 %all-to-all-start.1 = ((bf16[16,4,3,3,16,128]{5,4,3,2,1,0:T(8,128)(2,1)}), bf16[16,4,3,3,16,128]{5,4,3,2,1,0:T(8,128)(2,1)S(1)}, u32[]{:S(2)}, u32[]{:S(2)}) async-start(bf16[16,4,3,3,16,128]{5,4,3,2,1,0:T(8,128)(2,1)} %shard_map.56), calls=%async_computation.1 | async-start | bytes 4718592 | tf_op jit(solution)/shard_map/all_to_all | solution.py:124
  41.3 100.9 %all-to-all-done.1 = bf16[16,4,3,3,16,128]{5,4,3,2,1,0:T(8,128)(2,1)S(1)} async-done(((bf16[16,4,3,3,16,128]{5,4,3,2,1,0:T(8,128)(2,1)}), bf16[16,4,3,3,16,128]{5,4,3,2,1,0:T(8,128)(2,1)S(1)}, u32[]{:S(2)}, u32[]{:S(2)}) %all-to-all-start.1) | async-done | bytes 2359328 | tf_op jit(solution)/shard_map/all_to_all | solution.py:124
  143.2 1.9 collective-permute-start.2
  145.1 7.4 %collective-permute-start.3 = (bf16[4,4,3,16,128]{4,3,2,1,0:T(8,128)(2,1)}, bf16[4,4,3,16,128]{4,3,2,1,0:T(8,128)(2,1)}, u32[]{:S(2)}, u32[]{:S(2)}) collective-permute-start(bf16[4,4,3,16,128]{4,3,2,1,0:T(8,128)(2,1)} %get-tuple-element.18), channel_id=1, source_target_pairs={{0,128},{64,192},{128,0},{192,64},{1,129},{65,193},{129,1},{193,65... | collective-permute-start | bytes 589832 | tf_op jit(solution)/shard_map/ppermute | solution.py:110
  152.5 2.0 collective-permute-start.4
  156.7 2.0 collective-permute-start
  158.8 2.0 copy.41
  160.8 7.1 %all-to-all-start.2 = ((bf16[16,4,3,3,16,128]{5,4,3,2,1,0:T(8,128)(2,1)}), bf16[16,4,3,3,16,128]{5,4,3,2,1,0:T(8,128)(2,1)S(1)}, u32[]{:S(2)}, u32[]{:S(2)}) async-start(bf16[16,4,3,3,16,128]{5,4,3,2,1,0:T(8,128)(2,1)} %bitcast.98), calls=%async_computation.2 | async-start | bytes 4718592 | tf_op jit(solution)/shard_map/all_to_all | solution.py:128
  170.5 2.0 collective-permute-start.5
  172.5 3.7 %collective-permute-start.6 = (bf16[4,4,16,128]{3,1,0,2:T(4,128)(2,1)S(1)}, bf16[4,4,16,128]{3,1,0,2:T(4,128)(2,1)S(1)}, u32[]{:S(2)}, u32[]{:S(2)}) collective-permute-start(bf16[4,4,16,128]{3,1,0,2:T(4,128)(2,1)S(1)} %bitcast.114), channel_id=1, source_target_pairs={{0,128},{64,192},{128,0},{192,64},{1,129},{65,193},{129,1},{193,65... | collective-permute-start | bytes 196616 | tf_op jit(solution)/shard_map/ppermute | solution.py:110
  176.2 2.2 collective-permute-start.7
  179.0 3.3 %collective-permute-done.7 = bf16[4,4,16,128]{3,1,0,2:T(4,128)(2,1)} collective-permute-done((bf16[4,4,16,128]{3,1,0,2:T(4,128)(2,1)S(1)}, bf16[4,4,16,128]{3,1,0,2:T(4,128)(2,1)}, u32[]{:S(2)}, u32[]{:S(2)}) %collective-permute-start.7) | collective-permute-done | bytes 65568 | tf_op jit(solution)/shard_map/ppermute | solution.py:110
  183.5 1.3 maximum_bitcast_fusion
  188.2 36.5 %all-gather.2.cloned.1.call-done.ref_ref = bf16[32,2,2,48,128]{4,3,2,1,0:T(8,128)(2,1)} async-done(((bf16[1,2,2,48,128]{4,3,2,1,0:T(8,128)(2,1)}), bf16[32,2,2,48,128]{4,3,2,1,0:T(8,128)(2,1)}) %all-gather.2.cloned.1.call-update) | async-done | bytes 1572880 | tf_op jit(solution)/shard_map/all_gather | solution.py:122
  224.7 1.4 copy-done.5
  226.1 12.6 %shard_map.57 = bf16[64,3,16,128]{3,2,1,0:T(8,128)(2,1)} custom-call(bf16[64,3,3,16,128]{4,3,2,1,0:T(8,128)(2,1)S(1)} %bitcast.94, bf16[32,2,2,48,128]{4,3,2,1,0:T(8,128)(2,1)S(1)} %copy-done.5), custom_call_target="tpu_custom_call" | custom-call | flops 4026531840 | bytes 4718592 | tf_op jit(solution)/shard_map/pallas_call | solution.py:87
  238.7 4.9 %all-to-all-start.3 = ((bf16[16,4,3,16,128]{4,3,2,1,0:T(8,128)(2,1)}), bf16[16,4,3,16,128]{4,3,2,1,0:T(8,128)(2,1)S(1)}, u32[]{:S(2)}, u32[]{:S(2)}) async-start(bf16[16,4,3,16,128]{4,3,2,1,0:T(8,128)(2,1)} %bitcast.6), calls=%async_computation.3 | async-start | bytes 1572864 | tf_op jit(solution)/shard_map/all_to_all | solution.py:133
  243.8 1.9 collective-permute-start.1
  245.8 1.4 collective-permute-done.1
  247.4 11.0 %all-to-all-done.3 = bf16[16,4,3,16,128]{4,3,2,1,0:T(8,128)(2,1)S(1)} async-done(((bf16[16,4,3,16,128]{4,3,2,1,0:T(8,128)(2,1)}), bf16[16,4,3,16,128]{4,3,2,1,0:T(8,128)(2,1)S(1)}, u32[]{:S(2)}, u32[]{:S(2)}) %all-to-all-start.3) | async-done | bytes 786464 | tf_op jit(solution)/shard_map/all_to_all | solution.py:133
  258.8 53.8 %all_to_all.25.in_ref = bf16[16,4,3,16,128]{4,3,2,1,0:T(8,128)(2,1)S(1)} all-to-all(bf16[16,4,3,16,128]{4,3,2,1,0:T(8,128)(2,1)S(1)} %bitcast.99), channel_id=1, replica_groups=mesh['zl1'=2,'zl0'=2,'core'=2,'y'=4,'zh'=4,'x'=4] {'zl1','zl0','zh'}, dimensions={0} | all-to-all | bytes 1572864 | tf_op jit(solution)/shard_map/all_to_all | solution.py:166
  (56 shorter events, 18.2 us)
Async XLA Ops:
  6.5 0.7 copy-start.3
  7.3 0.7 copy-start.4
  8.7 27.0 %all-to-all-start = ((bf16[16,2,2,3,128]{4,2,3,1,0:T(2,128)(2,1)}), bf16[16,2,2,3,128]{4,2,3,1,0:T(2,128)(2,1)S(1)}, u32[]{:S(2)}, u32[]{:S(2)}) async-start(bf16[16,2,2,3,128]{4,2,3,1,0:T(2,128)(2,1)} %copy.40), calls=%async_computation | async-start | bytes 98304 | tf_op jit(solution)/shard_map/all_to_all | solution.py:118
  23.9 1.1 copy-start
  25.1 1.1 copy-start.1
  26.2 1.1 copy-start.2
  35.7 106.5 %all-to-all-start.1 = ((bf16[16,4,3,3,16,128]{5,4,3,2,1,0:T(8,128)(2,1)}), bf16[16,4,3,3,16,128]{5,4,3,2,1,0:T(8,128)(2,1)S(1)}, u32[]{:S(2)}, u32[]{:S(2)}) async-start(bf16[16,4,3,3,16,128]{5,4,3,2,1,0:T(8,128)(2,1)} %shard_map.56), calls=%async_computation.1 | async-start | bytes 4718592 | tf_op jit(solution)/shard_map/all_to_all | solution.py:124
  41.2 183.5 %all-gather.2.cloned.1.call-start = ((), (), s32[]{:S(2)}) async-start(), calls=%async_computation.5 | async-start | bytes 1622016 | tf_op jit(solution)/shard_map/all_gather | solution.py:122
  143.2 24.7 %collective-permute-start.2 = (bf16[4,4,3,16,128]{4,3,2,1,0:T(8,128)(2,1)}, bf16[4,4,3,16,128]{4,3,2,1,0:T(8,128)(2,1)}, u32[]{:S(2)}, u32[]{:S(2)}) collective-permute-start(bf16[4,4,3,16,128]{4,3,2,1,0:T(8,128)(2,1)} %get-tuple-element.19), channel_id=1, source_target_pairs={{0,64},{64,0},{128,192},{192,128},{1,65},{65,1},{129,193},{193,129... | collective-permute-start | bytes 589832 | tf_op jit(solution)/shard_map/ppermute | solution.py:110
  145.1 22.7 %collective-permute-start.3 = (bf16[4,4,3,16,128]{4,3,2,1,0:T(8,128)(2,1)}, bf16[4,4,3,16,128]{4,3,2,1,0:T(8,128)(2,1)}, u32[]{:S(2)}, u32[]{:S(2)}) collective-permute-start(bf16[4,4,3,16,128]{4,3,2,1,0:T(8,128)(2,1)} %get-tuple-element.18), channel_id=1, source_target_pairs={{0,128},{64,192},{128,0},{192,64},{1,129},{65,193},{129,1},{193,65... | collective-permute-start | bytes 589832 | tf_op jit(solution)/shard_map/ppermute | solution.py:110
  152.5 15.3 %collective-permute-start.4 = (bf16[4,4,3,16,128]{4,3,2,1,0:T(8,128)(2,1)S(1)}, bf16[4,4,3,16,128]{4,3,2,1,0:T(8,128)(2,1)}, u32[]{:S(2)}, u32[]{:S(2)}) collective-permute-start(bf16[4,4,3,16,128]{4,3,2,1,0:T(8,128)(2,1)S(1)} %get-tuple-element.20), channel_id=1, source_target_pairs={{0,192},{64,128},{128,64},{192,0},{1,193},{65,129},{129,65},{193,1... | collective-permute-start | bytes 589832 | tf_op jit(solution)/shard_map/ppermute | solution.py:110
  156.7 26.8 %collective-permute-start = (bf16[4,2,4,3,2,16,128]{6,5,4,3,2,1,0:T(8,128)(2,1)}, bf16[4,2,4,3,2,16,128]{6,5,4,3,2,1,0:T(8,128)(2,1)}, u32[]{:S(2)}, u32[]{:S(2)}) collective-permute-start(bf16[4,2,4,3,2,16,128]{6,5,4,3,2,1,0:T(8,128)(2,1)} %get-tuple-element.13), channel_id=1, source_target_pairs={{0,64},{64,0},{128,192},{192,128},{1,65},{65,1},{129,193},{193,129... | collective-permute-start | bytes 2359304 | tf_op jit(solution)/shard_map/ppermute | solution.py:110
  160.8 63.9 %all-to-all-start.2 = ((bf16[16,4,3,3,16,128]{5,4,3,2,1,0:T(8,128)(2,1)}), bf16[16,4,3,3,16,128]{5,4,3,2,1,0:T(8,128)(2,1)S(1)}, u32[]{:S(2)}, u32[]{:S(2)}) async-start(bf16[16,4,3,3,16,128]{5,4,3,2,1,0:T(8,128)(2,1)} %bitcast.98), calls=%async_computation.2 | async-start | bytes 4718592 | tf_op jit(solution)/shard_map/all_to_all | solution.py:128
  170.5 7.9 %collective-permute-start.5 = (bf16[4,4,16,128]{3,1,0,2:T(4,128)(2,1)S(1)}, bf16[4,4,16,128]{3,1,0,2:T(4,128)(2,1)S(1)}, u32[]{:S(2)}, u32[]{:S(2)}) collective-permute-start(bf16[4,4,16,128]{3,1,0,2:T(4,128)(2,1)S(1)} %bitcast.116), channel_id=1, source_target_pairs={{0,64},{64,0},{128,192},{192,128},{1,65},{65,1},{129,193},{193,129... | collective-permute-start | bytes 196616 | tf_op jit(solution)/shard_map/ppermute | solution.py:110
  172.5 6.5 %collective-permute-start.6 = (bf16[4,4,16,128]{3,1,0,2:T(4,128)(2,1)S(1)}, bf16[4,4,16,128]{3,1,0,2:T(4,128)(2,1)S(1)}, u32[]{:S(2)}, u32[]{:S(2)}) collective-permute-start(bf16[4,4,16,128]{3,1,0,2:T(4,128)(2,1)S(1)} %bitcast.114), channel_id=1, source_target_pairs={{0,128},{64,192},{128,0},{192,64},{1,129},{65,193},{129,1},{193,65... | collective-permute-start | bytes 196616 | tf_op jit(solution)/shard_map/ppermute | solution.py:110
  176.2 6.1 %collective-permute-start.7 = (bf16[4,4,16,128]{3,1,0,2:T(4,128)(2,1)S(1)}, bf16[4,4,16,128]{3,1,0,2:T(4,128)(2,1)}, u32[]{:S(2)}, u32[]{:S(2)}) collective-permute-start(bf16[4,4,16,128]{3,1,0,2:T(4,128)(2,1)S(1)} %bitcast.112), channel_id=1, source_target_pairs={{0,192},{64,128},{128,64},{192,0},{1,193},{65,129},{129,65},{193,1... | collective-permute-start | bytes 196616 | tf_op jit(solution)/shard_map/ppermute | solution.py:110
  224.7 1.4 copy-start.5
  238.7 19.7 %all-to-all-start.3 = ((bf16[16,4,3,16,128]{4,3,2,1,0:T(8,128)(2,1)}), bf16[16,4,3,16,128]{4,3,2,1,0:T(8,128)(2,1)S(1)}, u32[]{:S(2)}, u32[]{:S(2)}) async-start(bf16[16,4,3,16,128]{4,3,2,1,0:T(8,128)(2,1)} %bitcast.6), calls=%async_computation.3 | async-start | bytes 1572864 | tf_op jit(solution)/shard_map/all_to_all | solution.py:133
  243.8 3.4 %collective-permute-start.1 = (bf16[4,4,2,2,16,128]{5,4,2,3,1,0:T(8,128)(2,1)S(1)}, bf16[4,4,2,2,16,128]{5,4,2,3,1,0:T(8,128)(2,1)S(1)}, u32[]{:S(2)}, u32[]{:S(2)}) collective-permute-start(bf16[4,4,2,2,16,128]{5,4,2,3,1,0:T(8,128)(2,1)S(1)} %copy.48), channel_id=1, source_target_pairs={{0,64},{64,0},{128,192},{192,128},{1,65},{65,1},{129,193},{193,129... | collective-permute-start | bytes 786440 | tf_op jit(solution)/shard_map/ppermute | solution.py:110
Sparse Core Ops, SparseCore 0:
  155.4 69.2 all-gather.1

commit v2 on v1

v2 whole, which is shorter than its diff:
```python
import math

import jax
import jax.numpy as jnp
from jax import lax
from jax.experimental import pallas as pl
from jax.experimental.pallas import tpu as pltpu
from jax.sharding import Mesh, PartitionSpec as P

HD = 128
LOG2E = 1.4426950408889634
Z = ("zl1", "zl0", "zh")
YX = ("y", "x")
VMEM = pl.BlockSpec(memory_space=pltpu.VMEM)
FIRST_ROWS = 4 * 3 * 16 + 16


def head_of(z_index, middle):
    zl1, zl0, zh = z_index // 8, (z_index // 4) % 2, z_index % 4
    pair = zh * 2 + zl1
    return pair * 3 + (1 if middle else 2 * zl0)


def frame_of(z_index, j, slot):
    zl0 = (z_index // 4) % 2
    return 4 * zl0 + j if slot == 2 else 2 * j + slot


def columns(head):
    return slice(head * HD, (head + 1) * HD)


def pack_first_kernel(q_ref, k_ref, v_ref, ref_key_ref, ref_value_ref, out_ref):
    for z in range(16):
        for j in range(4):
            for t, ref in enumerate((q_ref, k_ref, v_ref)):
                at = (j * 3 + t) * 16
                out_ref[z, at : at + 16] = ref[frame_of(z, j, 2), :, columns(head_of(z, True))]
        for t, ref in enumerate((ref_key_ref, ref_value_ref)):
            for middle in range(2):
                at = 192 + (t * 2 + middle) * 4
                out_ref[z, at : at + 3] = ref[:, columns(head_of(z, middle))]


def pack_second_kernel(q_ref, k_ref, v_ref, out_ref):
    for z in range(16):
        for j in range(4):
            for slot in range(2):
                for t, ref in enumerate((q_ref, k_ref, v_ref)):
                    out_ref[z, j, t, slot] = ref[frame_of(z, j, slot), :, columns(head_of(z, False))]


def split_first_kernel(in_ref, refs_ref, *frame_refs):
    y, x = lax.axis_index("y"), lax.axis_index("x")
    for z in range(16):
        for t in range(2):
            for middle in range(2):
                at = 192 + (t * 2 + middle) * 4
                refs_ref[0, t, middle, z * 3 : z * 3 + 3] = in_ref[z, at : at + 3]
    for k, frame_ref in enumerate(frame_refs):
        zl = lax.rem(y + k, 4)
        for m in range(4):
            j = lax.rem(x + m, 4)
            for zh in range(4):
                for t in range(3):
                    at = pl.multiple_of((j * 3 + t) * 16, 16)
                    frame_ref[m, zh, t] = in_ref[zl * 4 + zh, pl.ds(at, 16)]


def split_second_kernel(in_ref, first_ref, frame_ref, mine_ref, other_ref):
    core = lax.axis_index("core")
    for zl in range(4):
        for j in range(4):
            for zh in range(4):
                frame_ref[zl * 4 + j, zh] = in_ref[zl, zh, j]
            for half in range(2):
                for ref, zh in ((mine_ref, 2 * core + half), (other_ref, 2 - 2 * core + half)):
                    for t in range(3):
                        for slot in range(2):
                            ref[t, slot, zl * 4 + j, half] = in_ref[zl, zh, j, t, slot]
                        at = (j * 3 + t) * 16
                        ref[t, 2, zl * 4 + j, half] = first_ref[zl * 4 + zh, at : at + 16]


def attend(query, own_k, own_v, ref_k, ref_v):
    scale = LOG2E / math.sqrt(HD)
    nt = (((1,), (1,)), ((), ()))
    own = lax.dot_general(query, own_k, nt, preferred_element_type=jnp.float32)
    ref = lax.dot_general(query, ref_k, nt, preferred_element_type=jnp.float32)
    highest = jnp.maximum(jnp.max(own, axis=1, keepdims=True), jnp.max(ref, axis=1, keepdims=True))
    own = jnp.exp2((own - highest) * scale)
    ref = jnp.exp2((ref - highest) * scale)
    totals = jnp.sum(own, axis=1, keepdims=True) + jnp.sum(ref, axis=1, keepdims=True)
    numerator = jnp.dot(own.astype(jnp.bfloat16), own_v, preferred_element_type=jnp.float32)
    numerator += jnp.dot(ref.astype(jnp.bfloat16), ref_v, preferred_element_type=jnp.float32)
    return (numerator / totals).astype(jnp.bfloat16)


def spatial_first_kernel(*refs):
    *parts, ref_ref, out_ref = refs
    y, x = lax.axis_index("y"), lax.axis_index("x")
    own_k = jnp.concatenate([part[:, :, 1].reshape(256, HD) for part in parts])
    own_v = jnp.concatenate([part[:, :, 2].reshape(256, HD) for part in parts])
    ref_k = ref_ref[:, 0, 1].reshape(-1, HD)
    ref_v = ref_ref[:, 1, 1].reshape(-1, HD)
    for m, part in enumerate(parts):
        result = attend(part[:, :, 0].reshape(256, HD), own_k, own_v, ref_k, ref_v)
        result = result.reshape(4, 4, 16, HD)
        for k in range(4):
            out_ref[lax.rem(y + 4 - k, 4) * 4 + lax.rem(x + 4 - m, 4)] = result[k]


def spatial_second_kernel(x_ref, ref_ref, first_ref, out_ref):
    out_ref[:, :, 2] = first_ref[...]
    ref_k = ref_ref[:, 0, 0].reshape(-1, HD)
    ref_v = ref_ref[:, 1, 0].reshape(-1, HD)
    for slot in range(2):
        own_k = x_ref[:, :, 1, slot].reshape(1024, HD)
        own_v = x_ref[:, :, 2, slot].reshape(1024, HD)
        for block in range(4):
            at = slice(block * 4, block * 4 + 4)
            result = attend(x_ref[at, :, 0, slot].reshape(256, HD), own_k, own_v, ref_k, ref_v)
            out_ref[at, :, slot] = result.reshape(4, 4, 16, HD)


def sum_kernel(spatial_ref, mine_ref, other_ref, out_ref):
    core = lax.axis_index("core")
    for zl in range(4):
        for j in range(4):
            for half in range(2):
                for ref, first in ((mine_ref, 2 * core), (other_ref, 2 - 2 * core)):
                    zh = first + half
                    both = spatial_ref[zl * 4 + j, zh].astype(jnp.float32)
                    both += ref[:, zl * 4 + j, half].astype(jnp.float32)
                    out_ref[zl, zh, j] = both.astype(jnp.bfloat16)


def unpack_kernel(in_ref, out_ref):
    for z in range(16):
        for j in range(4):
            for slot in range(3):
                out_ref[frame_of(z, j, slot), :, columns(head_of(z, slot == 2))] = in_ref[z, j, slot]


def call(kernel, out_shapes, *args, flops=0):
    several = isinstance(out_shapes, list)
    shapes = [jax.ShapeDtypeStruct(s, jnp.bfloat16) for s in (out_shapes if several else [out_shapes])]
    size = sum(a.size * 2 for a in args) + sum(2 * math.prod(s.shape) for s in shapes)
    return pl.pallas_call(
        kernel,
        out_shape=shapes if several else shapes[0],
        in_specs=[VMEM] * len(args),
        out_specs=[VMEM] * len(shapes) if several else VMEM,
        compiler_params=pltpu.CompilerParams(vmem_limit_bytes=48 * 1024 * 1024),
        cost_estimate=pl.CostEstimate(flops=flops, bytes_accessed=size, transcendentals=0),
    )(*args)


def temporal_attention(query, key, value):
    scores = jnp.einsum("ftd,gtd->tfg", query, key, preferred_element_type=jnp.float32)
    scores = scores * (1.0 / math.sqrt(HD))
    highest = jnp.max(scores, axis=-1, keepdims=True)
    weights = jnp.exp(scores - highest)
    totals = jnp.sum(weights, axis=-1, keepdims=True)
    numerator = jnp.einsum(
        "tfg,gtd->ftd", weights.astype(jnp.bfloat16), value, preferred_element_type=jnp.float32
    )
    return (numerator / jnp.transpose(totals, (1, 0, 2))).astype(jnp.bfloat16)


def swap(tensor, mask):
    return lax.ppermute(tensor, ("zl0", "core"), [(i, i ^ mask) for i in range(4)])


def shift(tensor, axis, step):
    return lax.ppermute(tensor, axis, [(i, (i + step) % 4) for i in range(4)])


def gather_refs(refs):
    refs = jnp.concatenate((refs, lax.ppermute(refs, "core", [(0, 1), (1, 0)])))
    for axis in YX:
        refs = jnp.concatenate([refs] + [shift(refs, axis, step) for step in (1, 3, 2)])
    return refs


def local(queries, keys, values, ref_keys, ref_values):
    first = call(
        pack_first_kernel, (16, FIRST_ROWS, HD), queries, keys, values, ref_keys, ref_values
    )
    first = lax.all_to_all(first, Z, split_axis=0, concat_axis=0, tiled=True)
    second = call(pack_second_kernel, (16, 4, 3, 2, 16, HD), queries, keys, values)
    first, second = lax.optimization_barrier((first, second))
    second = lax.all_to_all(second, Z, split_axis=0, concat_axis=0, tiled=True)

    refs, *parts = call(
        split_first_kernel, [(1, 2, 2, 48, HD)] + [(4, 4, 3, 16, HD)] * 4, first
    )
    parts = [parts[0]] + [shift(parts[step], "y", step) for step in (1, 2, 3)]
    parts = [jnp.stack([part[m] for part in parts]) for m in range(4)]
    parts = [parts[0]] + [shift(parts[step], "x", step) for step in (1, 2, 3)]
    refs = gather_refs(refs)
    middle = call(
        spatial_first_kernel, (16, 4, 16, HD), *parts, refs, flops=4 * 1024 * 2560 * HD
    )

    second, middle, refs = lax.optimization_barrier((second, middle, refs))
    by_frame, mine, other = call(
        split_second_kernel,
        [(16, 4, 3, 2, 16, HD), (3, 3, 16, 2, 16, HD), (3, 3, 16, 2, 16, HD)],
        second.reshape(4, 4, 4, 3, 2, 16, HD),
        first,
    )

    by_frame = lax.all_to_all(by_frame, YX, split_axis=0, concat_axis=0, tiled=True)
    spatial = call(
        spatial_second_kernel,
        (16, 4, 3, 16, HD),
        by_frame,
        refs,
        middle,
        flops=8 * 1024 * 2560 * HD,
    )
    spatial = lax.all_to_all(spatial, YX, split_axis=0, concat_axis=0, tiled=True)

    got = swap(other, 1)
    own_head = jnp.stack((mine[:, :2], got[:, :2]), axis=1).reshape(3, 64, 32, HD)
    own_head = temporal_attention(own_head[0], own_head[1], own_head[2])
    own_head = own_head.reshape(2, 2, 16, 2, 16, HD)
    zl0 = lax.axis_index("zl0")
    middle = jnp.stack((mine[:, 2], got[:, 2]), axis=1)
    send = lax.dynamic_index_in_dim(middle, 1 - zl0, axis=3, keepdims=False)
    keep = lax.dynamic_index_in_dim(middle, zl0, axis=3, keepdims=False)
    middle = jnp.stack((keep, swap(send, 2)), axis=1).reshape(3, 64, 16, HD)
    middle = temporal_attention(middle[0], middle[1], middle[2])
    keep, send = middle[:32], middle[32:]
    got = swap(send, 2)
    middle = jnp.stack(
        (jnp.where(zl0 == 0, keep, got), jnp.where(zl0 == 0, got, keep)), axis=1
    ).reshape(2, 1, 16, 2, 16, HD)
    temporal = jnp.concatenate((own_head, middle), axis=1)
    mine, other = temporal[0], swap(temporal[1], 1)

    attended = call(sum_kernel, (4, 4, 4, 3, 16, HD), spatial, mine, other)
    attended = attended.reshape(16, 4, 3, 16, HD)
    attended = lax.all_to_all(attended, Z, split_axis=0, concat_axis=0, tiled=True)
    return call(unpack_kernel, queries.shape, attended)


def solution(mesh):
    split = Mesh(mesh.devices.reshape(2, 2, 2, 4, 4, 4), ("zl1", "zl0", "core", "y", "zh", "x"))
    rows = P(("zl1", "zl0", "core"), ("y", "zh", "x"), None)
    refs = P(("zl1", "zl0", "core", "y", "zh", "x"), None)
    return jax.shard_map(
        local,
        mesh=split,
        in_specs=(rows, rows, rows, refs, refs),
        out_specs=rows,
        check_vma=False,
    )
```

time: 322 us -> 261 us (0.81)
  waiting for transfers between devices: 160 us -> 86.1 us
  starting transfers between devices: 55.9 us -> 87.1 us
  between operations: 13.8 us -> 0.57 us
  Pallas kernels: 15.5 us -> 19.9 us
  other arithmetic: 4.37 us -> 0.83 us
    all_to_all x3, waiting for transfers between devices: 119 us -> 51.4 us  [the longest x1 40.4 us: local(): first = lax.all_to_all(first, Z, split_axis=0, concat_axis=0, tiled=True)]
    ppermute x0 -> x13, starting transfers between devices: none -> 42.7 us  [the longest x12 40.8 us: shift(): return lax.ppermute(tensor, axis, [(i, (i + step) % 4) for i in range(4)])]
    all_gather x1 -> x0, waiting for transfers between devices: 36.5 us -> none  [local(): refs = lax.all_gather(refs, ('core', 'y', 'x'), axis=0, tiled=True)]
    ppermute x0 -> x13, waiting for transfers between devices: none -> 20.4 us  [the longest x12 20.4 us: shift(): return lax.ppermute(tensor, axis, [(i, (i + step) % 4) for i in range(4)])]
    ppermute x8 -> x4, starting transfers between devices: 23.2 us -> 10.7 us  [swap(): lax.ppermute(tensor, ('zl0', 'core'), [(i, i ^ mask) for i in range(4)])]
    all_to_all x1, waiting for transfers between devices: 0.01 us -> 6.8 us  [local(): lax.all_to_all(by_frame, YX, split_axis=0, concat_axis=0, tiled=True)]
    pallas_call x4 -> x8, Pallas kernels: 15.5 us -> 19.9 us  [call(): pl.pallas_call(kernel, out_shape=shapes if several else shapes[0], in_spe...]
    ppermute x8 -> x4, waiting for transfers between devices: 5.28 us -> 7.51 us  [swap(): lax.ppermute(tensor, ('zl0', 'core'), [(i, i ^ mask) for i in range(4)])]
  transfers between devices with their start and end apart: 13 -> 21, of which waited for: 7 -> 12; matrix products, arithmetic and copies ran while one was open for 4% -> 3% of each run, Pallas kernels for 1% -> 5%
where the time goes in v2:
time: 261 us; the launch traced here: 260 us
  starting transfers between devices  87.1 us (33%)
  waiting for transfers between devices  86.1 us (33%)
  blocking collectives  51.1 us (20%)
  Pallas kernels  19.9 us (8%)
  local copies, waits for them, and re-layouts  12.3 us (5%)
    all_to_all x1, blocking collectives, local(): lax.all_to_all(attended, Z, split_axis=0, concat_axis=0, tiled=True)  51.1 us
    ppermute x12, starting transfers between devices, shift(): return lax.ppermute(tensor, axis, [(i, (i + step) % 4) for i in range(4)])  40.8 us
    all_to_all x1, waiting for transfers between devices, local(): first = lax.all_to_all(first, Z, split_axis=0, concat_axis=0, tiled=True)  40.4 us
    ppermute x12, waiting for transfers between devices, shift(): return lax.ppermute(tensor, axis, [(i, (i + step) % 4) for i in range(4)])  20.4 us
    pallas_call x8, Pallas kernels, call(): pl.pallas_call(kernel, out_shape=shapes if several else shapes[0], in_spe...  19.9 us
    all_to_all x1, starting transfers between devices, local(): first = lax.all_to_all(first, Z, split_axis=0, concat_axis=0, tiled=True)  15.3 us
    ppermute x4, starting transfers between devices, swap(): lax.ppermute(tensor, ('zl0', 'core'), [(i, i ^ mask) for i in range(4)])  10.7 us
    all_to_all x1, waiting for transfers between devices, local(): lax.all_to_all(spatial, YX, split_axis=0, concat_axis=0, tiled=True)  10.2 us
  transfers between devices with their start and end apart: 21, of which 12 were waited for; matrix products, arithmetic and copies ran while one was open for 3% of the time, Pallas kernels for 5%

profile of v2, /device:TPU:32, one launch (start us, length us, event | category | flops | bytes accessed | tf_op | source)
XLA Modules:
  0.0 259.8 jit_solution(5811688681335088242)
XLA Ops:
  6.0 15.3 %all-to-all-start = ((bf16[16,208,128]{2,1,0:T(8,128)(2,1)}), bf16[16,208,128]{2,1,0:T(8,128)(2,1)S(1)}, u32[]{:S(2)}, u32[]{:S(2)}) async-start(bf16[16,208,128]{2,1,0:T(8,128)(2,1)} %shard_map.55), calls=%async_computation | async-start | bytes 1703936 | tf_op jit(solution)/shard_map/all_to_all | solution.py:190
  22.8 40.4 %all-to-all-done.in_ref.first_ref = bf16[16,208,128]{2,1,0:T(8,128)(2,1)S(1)} async-done(((bf16[16,208,128]{2,1,0:T(8,128)(2,1)}), bf16[16,208,128]{2,1,0:T(8,128)(2,1)S(1)}, u32[]{:S(2)}, u32[]{:S(2)}) %all-to-all-start) | async-done | bytes 852000 | tf_op jit(solution)/shard_map/all_to_all | solution.py:190
  63.2 7.6 %all-to-all-start.1 = ((bf16[16,4,3,2,16,128]{5,4,3,2,1,0:T(8,128)(2,1)}), bf16[16,4,3,2,16,128]{5,4,3,2,1,0:T(8,128)(2,1)S(1)}, u32[]{:S(2)}, u32[]{:S(2)}) async-start(bf16[16,4,3,2,16,128]{5,4,3,2,1,0:T(8,128)(2,1)} %shard_map.56), calls=%async_computation.1 | async-start | bytes 3145728 | tf_op jit(solution)/shard_map/all_to_all | solution.py:193
  72.8 4.9 %collective-permute-start.2 = (bf16[4,4,3,16,128]{4,3,2,1,0:T(8,128)(2,1)S(1)}, bf16[4,4,3,16,128]{4,3,2,1,0:T(8,128)(2,1)S(1)}, u32[]{:S(2)}, u32[]{:S(2)}) collective-permute-start(bf16[4,4,3,16,128]{4,3,2,1,0:T(8,128)(2,1)S(1)} %get-tuple-element.23), channel_id=1, source_target_pairs={{0,48},{16,0},{32,16},{48,32},{1,49},{17,1},{33,17},{49,33},{2,50}... | collective-permute-start | bytes 589832 | tf_op jit(solution)/shard_map/ppermute | solution.py:176
  83.3 3.8 %collective-permute-start.7 = (bf16[2,2,2,48,128]{4,3,2,1,0:T(8,128)(2,1)S(1)}, bf16[2,2,2,48,128]{4,3,2,1,0:T(8,128)(2,1)S(1)}, u32[]{:S(2)}, u32[]{:S(2)}) collective-permute-start(bf16[2,2,2,48,128]{4,3,2,1,0:T(8,128)(2,1)S(1)} %get-tuple-element.67), channel_id=1, source_target_pairs={{0,16},{16,32},{32,48},{48,0},{1,17},{17,33},{33,49},{49,1},{2,18}... | collective-permute-start | bytes 294920 | tf_op jit(solution)/shard_map/ppermute | solution.py:176
  90.3 4.2 %collective-permute-done.7 = bf16[2,2,2,48,128]{4,3,2,1,0:T(8,128)(2,1)S(1)} collective-permute-done((bf16[2,2,2,48,128]{4,3,2,1,0:T(8,128)(2,1)S(1)}, bf16[2,2,2,48,128]{4,3,2,1,0:T(8,128)(2,1)S(1)}, u32[]{:S(2)}, u32[]{:S(2)}) %collective-permute-start.7) | collective-permute-done | bytes 98336 | tf_op jit(solution)/shard_map/ppermute | solution.py:176
  97.2 5.5 %collective-permute-done.9 = bf16[2,2,2,48,128]{4,3,2,1,0:T(8,128)(2,1)S(1)} collective-permute-done((bf16[2,2,2,48,128]{4,3,2,1,0:T(8,128)(2,1)S(1)}, bf16[2,2,2,48,128]{4,3,2,1,0:T(8,128)(2,1)S(1)}, u32[]{:S(2)}, u32[]{:S(2)}) %collective-permute-start.9) | collective-permute-done | bytes 98336 | tf_op jit(solution)/shard_map/ppermute | solution.py:176
  102.7 3.4 %collective-permute-start.10 = (bf16[8,2,2,48,128]{4,3,2,1,0:T(8,128)(2,1)S(1)}, bf16[8,2,2,48,128]{4,3,2,1,0:T(8,128)(2,1)S(1)}, u32[]{:S(2)}, u32[]{:S(2)}) collective-permute-start(bf16[8,2,2,48,128]{4,3,2,1,0:T(8,128)(2,1)S(1)} %get-tuple-element.59), channel_id=1, source_target_pairs={{0,1},{1,2},{2,3},{3,0},{4,5},{5,6},{6,7},{7,4},{8,9},{9,10},{10,1... | collective-permute-start | bytes 1179656 | tf_op jit(solution)/shard_map/ppermute | solution.py:176
  106.1 3.7 %collective-permute-start.11 = (bf16[8,2,2,48,128]{4,3,2,1,0:T(8,128)(2,1)S(1)}, bf16[8,2,2,48,128]{4,3,2,1,0:T(8,128)(2,1)S(1)}, u32[]{:S(2)}, u32[]{:S(2)}) collective-permute-start(bf16[8,2,2,48,128]{4,3,2,1,0:T(8,128)(2,1)S(1)} %get-tuple-element.59), channel_id=1, source_target_pairs={{0,3},{1,0},{2,1},{3,2},{4,7},{5,4},{6,5},{7,6},{8,11},{9,8},{10,9... | collective-permute-start | bytes 1179656 | tf_op jit(solution)/shard_map/ppermute | solution.py:176
  109.7 3.7 %collective-permute-start.12 = (bf16[8,2,2,48,128]{4,3,2,1,0:T(8,128)(2,1)S(1)}, bf16[8,2,2,48,128]{4,3,2,1,0:T(8,128)(2,1)S(1)}, u32[]{:S(2)}, u32[]{:S(2)}) collective-permute-start(bf16[8,2,2,48,128]{4,3,2,1,0:T(8,128)(2,1)S(1)} %get-tuple-element.59), channel_id=1, source_target_pairs={{0,2},{1,3},{2,0},{3,1},{4,6},{5,7},{6,4},{7,5},{8,10},{9,11},{10,... | collective-permute-start | bytes 1179656 | tf_op jit(solution)/shard_map/ppermute | solution.py:176
  116.1 3.9 %collective-permute-start.4 = (bf16[4,4,3,16,128]{4,3,2,1,0:T(8,128)(2,1)S(1)}, bf16[4,4,3,16,128]{4,3,2,1,0:T(8,128)(2,1)S(1)}, u32[]{:S(2)}, u32[]{:S(2)}) collective-permute-start(bf16[4,4,3,16,128]{4,3,2,1,0:T(8,128)(2,1)S(1)} %pad_maximum_fusion.4), channel_id=1, source_target_pairs={{0,2},{1,3},{2,0},{3,1},{4,6},{5,7},{6,4},{7,5},{8,10},{9,11},{10,... | collective-permute-start | bytes 589832 | tf_op jit(solution)/shard_map/ppermute | solution.py:176
  120.2 3.7 %collective-permute-start.5 = (bf16[4,4,3,16,128]{4,3,2,1,0:T(8,128)(2,1)S(1)}, bf16[4,4,3,16,128]{4,3,2,1,0:T(8,128)(2,1)S(1)}, u32[]{:S(2)}, u32[]{:S(2)}) collective-permute-start(bf16[4,4,3,16,128]{4,3,2,1,0:T(8,128)(2,1)S(1)} %pad_maximum_fusion.5), channel_id=1, source_target_pairs={{0,3},{1,0},{2,1},{3,2},{4,7},{5,4},{6,5},{7,6},{8,11},{9,8},{10,9... | collective-permute-start | bytes 589832 | tf_op jit(solution)/shard_map/ppermute | solution.py:176
  123.9 3.8 %collective-permute-done.11 = bf16[8,2,2,48,128]{4,3,2,1,0:T(8,128)(2,1)S(1)} collective-permute-done((bf16[8,2,2,48,128]{4,3,2,1,0:T(8,128)(2,1)S(1)}, bf16[8,2,2,48,128]{4,3,2,1,0:T(8,128)(2,1)S(1)}, u32[]{:S(2)}, u32[]{:S(2)}) %collective-permute-start.11) | collective-permute-done | bytes 393248 | tf_op jit(solution)/shard_map/ppermute | solution.py:176
  130.2 3.6 %collective-permute-done.4.refs_2_ = bf16[4,4,3,16,128]{4,3,2,1,0:T(8,128)(2,1)S(1)} collective-permute-done((bf16[4,4,3,16,128]{4,3,2,1,0:T(8,128)(2,1)S(1)}, bf16[4,4,3,16,128]{4,3,2,1,0:T(8,128)(2,1)S(1)}, u32[]{:S(2)}, u32[]{:S(2)}) %collective-permute-start.4) | collective-permute-done | bytes 196640 | tf_op jit(solution)/shard_map/ppermute | solution.py:176
  134.8 4.0 %shard_map.58.first_ref = bf16[16,4,16,128]{3,2,1,0:T(8,128)(2,1)S(1)} custom-call(bf16[4,4,3,16,128]{4,3,2,1,0:T(8,128)(2,1)S(1)} %pad_maximum_fusion.2.refs_0_, bf16[4,4,3,16,128]{4,3,2,1,0:T(8,128)(2,1)S(1)} %collective-permute-done.3.refs_1_, bf16[4,4,3,16,128]{4,3,2,1,0:T(8,128)(2,1)S(1)} %collective-permute-done.4.refs_2_, ...), custom_call_target="tpu_custom_call" | custom-call | flops 1342177280 | bytes 2621440 | tf_op jit(solution)/shard_map/pallas_call | solution.py:149
  147.2 7.0 %all-to-all-start.2 = ((bf16[16,4,3,2,16,128]{5,4,3,2,1,0:T(8,128)(2,1)}), bf16[16,4,3,2,16,128]{5,4,3,2,1,0:T(8,128)(2,1)S(1)}, u32[]{:S(2)}, u32[]{:S(2)}) async-start(bf16[16,4,3,2,16,128]{5,4,3,2,1,0:T(8,128)(2,1)} %get-tuple-element.26), calls=%async_computation.2 | async-start | bytes 3145728 | tf_op jit(solution)/shard_map/all_to_all | solution.py:214
  155.5 3.4 %collective-permute-start.14 = (bf16[3,2,16,16,128]{4,3,2,1,0:T(8,128)(2,1)S(1)}, bf16[3,2,16,16,128]{4,3,2,1,0:T(8,128)(2,1)S(1)}, u32[]{:S(2)}, u32[]{:S(2)}) collective-permute-start(bf16[3,2,16,16,128]{4,3,2,1,0:T(8,128)(2,1)S(1)} %get-tuple-element.39), channel_id=1, source_target_pairs={{0,128},{64,192},{128,0},{192,64},{1,129},{65,193},{129,1},{193,65... | collective-permute-start | bytes 1179656 | tf_op jit(solution)/shard_map/ppermute | solution.py:172
  162.8 5.8 %collective-permute-done.14 = bf16[3,2,16,16,128]{4,3,2,1,0:T(8,128)(2,1)S(1)} collective-permute-done((bf16[3,2,16,16,128]{4,3,2,1,0:T(8,128)(2,1)S(1)}, bf16[3,2,16,16,128]{4,3,2,1,0:T(8,128)(2,1)S(1)}, u32[]{:S(2)}, u32[]{:S(2)}) %collective-permute-start.14) | collective-permute-done | bytes 393248 | tf_op jit(solution)/shard_map/ppermute | solution.py:172
  170.4 3.5 %collective-permute-start.15 = (bf16[32,16,128]{2,0,1:T(8,128)(2,1)}, bf16[32,16,128]{2,0,1:T(8,128)(2,1)S(1)}, u32[]{:S(2)}, u32[]{:S(2)}) collective-permute-start(bf16[32,16,128]{2,0,1:T(8,128)(2,1)} %slice.149), channel_id=1, source_target_pairs={{0,128},{64,192},{128,0},{192,64},{1,129},{65,193},{129,1},{193,65... | collective-permute-start | bytes 393224 | tf_op jit(solution)/shard_map/ppermute | solution.py:172
  174.0 6.8 %all-to-all-done.2.x_ref = bf16[16,4,3,2,16,128]{5,4,3,2,1,0:T(8,128)(2,1)S(1)} async-done(((bf16[16,4,3,2,16,128]{5,4,3,2,1,0:T(8,128)(2,1)}), bf16[16,4,3,2,16,128]{5,4,3,2,1,0:T(8,128)(2,1)S(1)}, u32[]{:S(2)}, u32[]{:S(2)}) %all-to-all-start.2) | async-done | bytes 1572896 | tf_op jit(solution)/shard_map/all_to_all | solution.py:214
  180.8 8.6 %shard_map.60 = bf16[16,4,3,16,128]{4,3,2,1,0:T(8,128)(2,1)} custom-call(bf16[16,4,3,2,16,128]{5,4,3,2,1,0:T(8,128)(2,1)S(1)} %all-to-all-done.2.x_ref, bf16[32,2,2,48,128]{4,3,2,1,0:T(8,128)(2,1)S(1)} %copy-done.9, bf16[16,4,16,128]{3,2,1,0:T(8,128)(2,1)S(1)} %shard_map.58.first_ref), custom_call_target="tpu_custom_call" | custom-call | flops 2684354560 | bytes 4194304 | tf_op jit(solution)/shard_map/pallas_call | solution.py:149
  189.4 3.7 %all-to-all-start.3 = ((bf16[16,4,3,16,128]{4,3,2,1,0:T(8,128)(2,1)}), bf16[16,4,3,16,128]{4,3,2,1,0:T(8,128)(2,1)S(1)}, u32[]{:S(2)}, u32[]{:S(2)}) async-start(bf16[16,4,3,16,128]{4,3,2,1,0:T(8,128)(2,1)} %shard_map.60), calls=%async_computation.3 | async-start | bytes 1572864 | tf_op jit(solution)/shard_map/all_to_all | solution.py:223
  197.2 10.2 %all-to-all-done.3.spatial_ref = bf16[16,4,3,16,128]{4,3,2,1,0:T(8,128)(2,1)S(1)} async-done(((bf16[16,4,3,16,128]{4,3,2,1,0:T(8,128)(2,1)}), bf16[16,4,3,16,128]{4,3,2,1,0:T(8,128)(2,1)S(1)}, u32[]{:S(2)}, u32[]{:S(2)}) %all-to-all-start.3) | async-done | bytes 786464 | tf_op jit(solution)/shard_map/all_to_all | solution.py:223
  207.6 51.1 %all_to_all.25.in_ref = bf16[16,4,3,16,128]{4,3,2,1,0:T(8,128)(2,1)S(1)} all-to-all(bf16[16,4,3,16,128]{4,3,2,1,0:T(8,128)(2,1)S(1)} %bitcast.49), channel_id=1, replica_groups=mesh['zl1'=2,'zl0'=2,'core'=2,'y'=4,'zh'=4,'x'=4] {'zl1','zl0','zh'}, dimensions={0} | all-to-all | bytes 1572864 | tf_op jit(solution)/shard_map/all_to_all | solution.py:245
  (94 shorter events, 47.4 us)
Async XLA Ops:
  4.9 16.4 %copy-start.5 = (bf16[8,16,3072]{2,1,0:T(8,128)(2,1)S(1)}, bf16[8,16,3072]{2,1,0:T(8,128)(2,1)}, u32[]{:S(2)}) copy-start(bf16[8,16,3072]{2,1,0:T(8,128)(2,1)} %v_ref.3) | copy-start | bytes 2359300
  6.0 15.4 %copy-start.1 = (bf16[8,16,3072]{2,1,0:T(8,128)(2,1)S(1)}, bf16[8,16,3072]{2,1,0:T(8,128)(2,1)}, u32[]{:S(2)}) copy-start(bf16[8,16,3072]{2,1,0:T(8,128)(2,1)} %q_ref.3) | copy-start | bytes 2359300
  6.0 15.4 %copy-start.3 = (bf16[8,16,3072]{2,1,0:T(8,128)(2,1)S(1)}, bf16[8,16,3072]{2,1,0:T(8,128)(2,1)}, u32[]{:S(2)}) copy-start(bf16[8,16,3072]{2,1,0:T(8,128)(2,1)} %k_ref.3) | copy-start | bytes 2359300
  6.0 57.2 %all-to-all-start = ((bf16[16,208,128]{2,1,0:T(8,128)(2,1)}), bf16[16,208,128]{2,1,0:T(8,128)(2,1)S(1)}, u32[]{:S(2)}, u32[]{:S(2)}) async-start(bf16[16,208,128]{2,1,0:T(8,128)(2,1)} %shard_map.55), calls=%async_computation | async-start | bytes 1703936 | tf_op jit(solution)/shard_map/all_to_all | solution.py:190
  63.2 77.6 %all-to-all-start.1 = ((bf16[16,4,3,2,16,128]{5,4,3,2,1,0:T(8,128)(2,1)}), bf16[16,4,3,2,16,128]{5,4,3,2,1,0:T(8,128)(2,1)S(1)}, u32[]{:S(2)}, u32[]{:S(2)}) async-start(bf16[16,4,3,2,16,128]{5,4,3,2,1,0:T(8,128)(2,1)} %shard_map.56), calls=%async_computation.1 | async-start | bytes 3145728 | tf_op jit(solution)/shard_map/all_to_all | solution.py:193
  70.9 12.3 %collective-permute-start.6 = (bf16[1,2,2,48,128]{4,3,2,1,0:T(8,128)(2,1)S(1)}, bf16[1,2,2,48,128]{4,3,2,1,0:T(8,128)(2,1)S(1)}, u32[]{:S(2)}, u32[]{:S(2)}) collective-permute-start(bf16[1,2,2,48,128]{4,3,2,1,0:T(8,128)(2,1)S(1)} %get-tuple-element.24), channel_id=1, source_target_pairs={{0,64},{64,0},{1,65},{65,1},{2,66},{66,2},{3,67},{67,3},{4,68},{68... | collective-permute-start | bytes 147464 | tf_op jit(solution)/shard_map/ppermute | solution.py:180
  72.8 36.9 %collective-permute-start.2 = (bf16[4,4,3,16,128]{4,3,2,1,0:T(8,128)(2,1)S(1)}, bf16[4,4,3,16,128]{4,3,2,1,0:T(8,128)(2,1)S(1)}, u32[]{:S(2)}, u32[]{:S(2)}) collective-permute-start(bf16[4,4,3,16,128]{4,3,2,1,0:T(8,128)(2,1)S(1)} %get-tuple-element.23), channel_id=1, source_target_pairs={{0,48},{16,0},{32,16},{48,32},{1,49},{17,1},{33,17},{49,33},{2,50}... | collective-permute-start | bytes 589832 | tf_op jit(solution)/shard_map/ppermute | solution.py:176
  77.8 35.7 %collective-permute-start.1 = (bf16[4,4,3,16,128]{4,3,2,1,0:T(8,128)(2,1)S(1)}, bf16[4,4,3,16,128]{4,3,2,1,0:T(8,128)(2,1)S(1)}, u32[]{:S(2)}, u32[]{:S(2)}) collective-permute-start(bf16[4,4,3,16,128]{4,3,2,1,0:T(8,128)(2,1)S(1)} %get-tuple-element.22), channel_id=1, source_target_pairs={{0,32},{16,48},{32,0},{48,16},{1,33},{17,49},{33,1},{49,17},{2,34}... | collective-permute-start | bytes 589832 | tf_op jit(solution)/shard_map/ppermute | solution.py:176
  80.3 33.2 %collective-permute-start = (bf16[4,4,3,16,128]{4,3,2,1,0:T(8,128)(2,1)S(1)}, bf16[4,4,3,16,128]{4,3,2,1,0:T(8,128)(2,1)S(1)}, u32[]{:S(2)}, u32[]{:S(2)}) collective-permute-start(bf16[4,4,3,16,128]{4,3,2,1,0:T(8,128)(2,1)S(1)} %get-tuple-element.21), channel_id=1, source_target_pairs={{0,16},{16,32},{32,48},{48,0},{1,17},{17,33},{33,49},{49,1},{2,18}... | collective-permute-start | bytes 589832 | tf_op jit(solution)/shard_map/ppermute | solution.py:176
  83.3 11.3 %collective-permute-start.7 = (bf16[2,2,2,48,128]{4,3,2,1,0:T(8,128)(2,1)S(1)}, bf16[2,2,2,48,128]{4,3,2,1,0:T(8,128)(2,1)S(1)}, u32[]{:S(2)}, u32[]{:S(2)}) collective-permute-start(bf16[2,2,2,48,128]{4,3,2,1,0:T(8,128)(2,1)S(1)} %get-tuple-element.67), channel_id=1, source_target_pairs={{0,16},{16,32},{32,48},{48,0},{1,17},{17,33},{33,49},{49,1},{2,18}... | collective-permute-start | bytes 294920 | tf_op jit(solution)/shard_map/ppermute | solution.py:176
  87.1 10.0 %collective-permute-start.8 = (bf16[2,2,2,48,128]{4,3,2,1,0:T(8,128)(2,1)S(1)}, bf16[2,2,2,48,128]{4,3,2,1,0:T(8,128)(2,1)S(1)}, u32[]{:S(2)}, u32[]{:S(2)}) collective-permute-start(bf16[2,2,2,48,128]{4,3,2,1,0:T(8,128)(2,1)S(1)} %get-tuple-element.67), channel_id=1, source_target_pairs={{0,48},{16,0},{32,16},{48,32},{1,49},{17,1},{33,17},{49,33},{2,50}... | collective-permute-start | bytes 294920 | tf_op jit(solution)/shard_map/ppermute | solution.py:176
  94.5 8.1 %collective-permute-start.9 = (bf16[2,2,2,48,128]{4,3,2,1,0:T(8,128)(2,1)S(1)}, bf16[2,2,2,48,128]{4,3,2,1,0:T(8,128)(2,1)S(1)}, u32[]{:S(2)}, u32[]{:S(2)}) collective-permute-start(bf16[2,2,2,48,128]{4,3,2,1,0:T(8,128)(2,1)S(1)} %get-tuple-element.67), channel_id=1, source_target_pairs={{0,32},{16,48},{32,0},{48,16},{1,33},{17,49},{33,1},{49,17},{2,34}... | collective-permute-start | bytes 294920 | tf_op jit(solution)/shard_map/ppermute | solution.py:176
  102.7 17.5 %collective-permute-start.10 = (bf16[8,2,2,48,128]{4,3,2,1,0:T(8,128)(2,1)S(1)}, bf16[8,2,2,48,128]{4,3,2,1,0:T(8,128)(2,1)S(1)}, u32[]{:S(2)}, u32[]{:S(2)}) collective-permute-start(bf16[8,2,2,48,128]{4,3,2,1,0:T(8,128)(2,1)S(1)} %get-tuple-element.59), channel_id=1, source_target_pairs={{0,1},{1,2},{2,3},{3,0},{4,5},{5,6},{6,7},{7,4},{8,9},{9,10},{10,1... | collective-permute-start | bytes 1179656 | tf_op jit(solution)/shard_map/ppermute | solution.py:176
  106.1 21.6 %collective-permute-start.11 = (bf16[8,2,2,48,128]{4,3,2,1,0:T(8,128)(2,1)S(1)}, bf16[8,2,2,48,128]{4,3,2,1,0:T(8,128)(2,1)S(1)}, u32[]{:S(2)}, u32[]{:S(2)}) collective-permute-start(bf16[8,2,2,48,128]{4,3,2,1,0:T(8,128)(2,1)S(1)} %get-tuple-element.59), channel_id=1, source_target_pairs={{0,3},{1,0},{2,1},{3,2},{4,7},{5,4},{6,5},{7,6},{8,11},{9,8},{10,9... | collective-permute-start | bytes 1179656 | tf_op jit(solution)/shard_map/ppermute | solution.py:176
  109.7 18.0 %collective-permute-start.12 = (bf16[8,2,2,48,128]{4,3,2,1,0:T(8,128)(2,1)S(1)}, bf16[8,2,2,48,128]{4,3,2,1,0:T(8,128)(2,1)S(1)}, u32[]{:S(2)}, u32[]{:S(2)}) collective-permute-start(bf16[8,2,2,48,128]{4,3,2,1,0:T(8,128)(2,1)S(1)} %get-tuple-element.59), channel_id=1, source_target_pairs={{0,2},{1,3},{2,0},{3,1},{4,6},{5,7},{6,4},{7,5},{8,10},{9,11},{10,... | collective-permute-start | bytes 1179656 | tf_op jit(solution)/shard_map/ppermute | solution.py:176
  113.6 16.6 %collective-permute-start.3 = (bf16[4,4,3,16,128]{4,3,2,1,0:T(8,128)(2,1)S(1)}, bf16[4,4,3,16,128]{4,3,2,1,0:T(8,128)(2,1)S(1)}, u32[]{:S(2)}, u32[]{:S(2)}) collective-permute-start(bf16[4,4,3,16,128]{4,3,2,1,0:T(8,128)(2,1)S(1)} %pad_maximum_fusion.3), channel_id=1, source_target_pairs={{0,1},{1,2},{2,3},{3,0},{4,5},{5,6},{6,7},{7,4},{8,9},{9,10},{10,1... | collective-permute-start | bytes 589832 | tf_op jit(solution)/shard_map/ppermute | solution.py:176
  116.1 17.7 %collective-permute-start.4 = (bf16[4,4,3,16,128]{4,3,2,1,0:T(8,128)(2,1)S(1)}, bf16[4,4,3,16,128]{4,3,2,1,0:T(8,128)(2,1)S(1)}, u32[]{:S(2)}, u32[]{:S(2)}) collective-permute-start(bf16[4,4,3,16,128]{4,3,2,1,0:T(8,128)(2,1)S(1)} %pad_maximum_fusion.4), channel_id=1, source_target_pairs={{0,2},{1,3},{2,0},{3,1},{4,6},{5,7},{6,4},{7,5},{8,10},{9,11},{10,... | collective-permute-start | bytes 589832 | tf_op jit(solution)/shard_map/ppermute | solution.py:176
  120.2 14.6 %collective-permute-start.5 = (bf16[4,4,3,16,128]{4,3,2,1,0:T(8,128)(2,1)S(1)}, bf16[4,4,3,16,128]{4,3,2,1,0:T(8,128)(2,1)S(1)}, u32[]{:S(2)}, u32[]{:S(2)}) collective-permute-start(bf16[4,4,3,16,128]{4,3,2,1,0:T(8,128)(2,1)S(1)} %pad_maximum_fusion.5), channel_id=1, source_target_pairs={{0,3},{1,0},{2,1},{3,2},{4,7},{5,4},{6,5},{7,6},{8,11},{9,8},{10,9... | collective-permute-start | bytes 589832 | tf_op jit(solution)/shard_map/ppermute | solution.py:176
  145.3 9.1 %collective-permute-start.13 = (bf16[3,3,16,2,16,128]{5,4,3,2,1,0:T(8,128)(2,1)}, bf16[3,3,16,2,16,128]{5,4,3,2,1,0:T(8,128)(2,1)}, u32[]{:S(2)}, u32[]{:S(2)}) collective-permute-start(bf16[3,3,16,2,16,128]{5,4,3,2,1,0:T(8,128)(2,1)} %get-tuple-element.30), channel_id=1, source_target_pairs={{0,64},{64,0},{128,192},{192,128},{1,65},{65,1},{129,193},{193,129... | collective-permute-start | bytes 3538952 | tf_op jit(solution)/shard_map/ppermute | solution.py:172
  147.2 33.6 %all-to-all-start.2 = ((bf16[16,4,3,2,16,128]{5,4,3,2,1,0:T(8,128)(2,1)}), bf16[16,4,3,2,16,128]{5,4,3,2,1,0:T(8,128)(2,1)S(1)}, u32[]{:S(2)}, u32[]{:S(2)}) async-start(bf16[16,4,3,2,16,128]{5,4,3,2,1,0:T(8,128)(2,1)} %get-tuple-element.26), calls=%async_computation.2 | async-start | bytes 3145728 | tf_op jit(solution)/shard_map/all_to_all | solution.py:214
  155.5 13.1 %collective-permute-start.14 = (bf16[3,2,16,16,128]{4,3,2,1,0:T(8,128)(2,1)S(1)}, bf16[3,2,16,16,128]{4,3,2,1,0:T(8,128)(2,1)S(1)}, u32[]{:S(2)}, u32[]{:S(2)}) collective-permute-start(bf16[3,2,16,16,128]{4,3,2,1,0:T(8,128)(2,1)S(1)} %get-tuple-element.39), channel_id=1, source_target_pairs={{0,128},{64,192},{128,0},{192,64},{1,129},{65,193},{129,1},{193,65... | collective-permute-start | bytes 1179656 | tf_op jit(solution)/shard_map/ppermute | solution.py:172
  170.4 22.7 %collective-permute-start.15 = (bf16[32,16,128]{2,0,1:T(8,128)(2,1)}, bf16[32,16,128]{2,0,1:T(8,128)(2,1)S(1)}, u32[]{:S(2)}, u32[]{:S(2)}) collective-permute-start(bf16[32,16,128]{2,0,1:T(8,128)(2,1)} %slice.149), channel_id=1, source_target_pairs={{0,128},{64,192},{128,0},{192,64},{1,129},{65,193},{129,1},{193,65... | collective-permute-start | bytes 393224 | tf_op jit(solution)/shard_map/ppermute | solution.py:172
  189.4 18.0 %all-to-all-start.3 = ((bf16[16,4,3,16,128]{4,3,2,1,0:T(8,128)(2,1)}), bf16[16,4,3,16,128]{4,3,2,1,0:T(8,128)(2,1)S(1)}, u32[]{:S(2)}, u32[]{:S(2)}) async-start(bf16[16,4,3,16,128]{4,3,2,1,0:T(8,128)(2,1)} %shard_map.60), calls=%async_computation.3 | async-start | bytes 1572864 | tf_op jit(solution)/shard_map/all_to_all | solution.py:223
  193.5 3.6 %collective-permute-start.16 = (bf16[3,16,2,16,128]{4,3,2,1,0:T(8,128)(2,1)S(1)}, bf16[3,16,2,16,128]{4,3,2,1,0:T(8,128)(2,1)S(1)}, u32[]{:S(2)}, u32[]{:S(2)}) collective-permute-start(bf16[3,16,2,16,128]{4,3,2,1,0:T(8,128)(2,1)S(1)} %get-tuple-element.34), channel_id=1, source_target_pairs={{0,64},{64,0},{128,192},{192,128},{1,65},{65,1},{129,193},{193,129... | collective-permute-start | bytes 1179656 | tf_op jit(solution)/shard_map/ppermute | solution.py:172
  (11 other events, 27.2 us)

commit v3 on v2

v3 whole, which is shorter than its diff:
```python
import math

import jax
import jax.numpy as jnp
from jax import lax
from jax.experimental import pallas as pl
from jax.experimental.pallas import tpu as pltpu
from jax.sharding import Mesh, PartitionSpec as P

HD = 128
LOG2E = 1.4426950408889634
Z = ("zl1", "zl0", "zh")
YX = ("y", "x")
VMEM = pl.BlockSpec(memory_space=pltpu.VMEM)
HBM = pl.BlockSpec(memory_space=pltpu.HBM)


def head_of(z_index, middle):
    zl1, zl0, zh = z_index // 8, (z_index // 4) % 2, z_index % 4
    pair = zh * 2 + zl1
    return pair * 3 + (1 if middle else 2 * zl0)


def frame_of(z_index, j, slot):
    zl0 = (z_index // 4) % 2
    return 4 * zl0 + j if slot == 2 else 2 * j + slot


def columns(head):
    return slice(head * HD, (head + 1) * HD)


def pack_first_kernel(q_ref, k_ref, v_ref, ref_key_ref, ref_value_ref, out_ref, key_rows, value_rows, sems):
    copies = [
        pltpu.make_async_copy(ref_key_ref, key_rows, sems.at[48]),
        pltpu.make_async_copy(ref_value_ref, value_rows, sems.at[49]),
    ]
    for z in range(16):
        for t, ref in enumerate((q_ref, k_ref, v_ref)):
            frames = pl.ds(frame_of(z, 0, 2), 4)
            source = ref.at[frames, :, pl.ds(head_of(z, True) * HD, HD)]
            target = out_ref.at[z, pl.ds(t * 4, 4)]
            copies.append(pltpu.make_async_copy(source, target, sems.at[z * 3 + t]))
    for copy in copies:
        copy.start()
    for copy in copies[:2]:
        copy.wait()
    for z in range(16):
        for t, ref in enumerate((key_rows, value_rows)):
            for middle in range(2):
                at = (t * 2 + middle) * 4
                out_ref[z, 12, at : at + 3] = ref[:, columns(head_of(z, middle))]
    for copy in copies[2:]:
        copy.wait()


def pack_second_kernel(q_ref, k_ref, v_ref, out_ref):
    for z in range(16):
        for j in range(4):
            for slot in range(2):
                for t, ref in enumerate((q_ref, k_ref, v_ref)):
                    out_ref[z, j, t, slot] = ref[frame_of(z, j, slot), :, columns(head_of(z, False))]


def split_first_kernel(in_ref, *outs):
    *part_refs, other_ref, rows_ref = outs
    y, x, core = lax.axis_index("y"), lax.axis_index("x"), lax.axis_index("core")
    for zl in range(4):
        for half in range(2):
            other_ref[zl, half] = in_ref[zl * 4 + 2 - 2 * core + half, :12]
    for z in range(16):
        for t in range(2):
            for middle in range(2):
                at = (t * 2 + middle) * 4
                rows_ref[t, middle, z * 3 : z * 3 + 3] = in_ref[z, 12, at : at + 3]
    rows = rows_ref[...].reshape(12, 16, HD)
    for k, part_ref in enumerate(part_refs):
        zl = lax.rem(y + k, 4)
        for m in range(4):
            j = lax.rem(x + m, 4)
            for zh in range(4):
                for t in range(3):
                    part_ref[m, zh * 3 + t] = in_ref[zl * 4 + zh, t * 4 + j]
        part_ref[4] = rows


def send_kernel(first_ref, got_ref, out_ref):
    core, half = lax.axis_index("core"), 1 - lax.axis_index("zl0")
    for zl in range(4):
        out_ref[0, zl] = first_ref[zl * 4 + 2 * core + half, :12]
        out_ref[1, zl] = got_ref[zl, half]


def split_second_kernel(in_ref, frame_ref):
    for zl in range(4):
        for zh in range(4):
            for j in range(4):
                frame_ref[zl * 4 + j, zh] = in_ref[zl, zh, j]


def other_kernel(in_ref, other_ref):
    core = lax.axis_index("core")
    for zl in range(4):
        for half in range(2):
            other_ref[zl, half] = in_ref[zl, 2 - 2 * core + half]


def token_bias(bias_ref):
    rows = lax.broadcasted_iota(jnp.int32, bias_ref.shape, 0)
    columns = lax.broadcasted_iota(jnp.int32, bias_ref.shape, 1)
    bias_ref[...] = jnp.where(((rows ^ columns) & 15) == 0, 0.0, -1e30)


def attend_tokens(queries, keys, values, bias_ref):
    scale = LOG2E / math.sqrt(HD)
    key, value = jnp.concatenate(keys), jnp.concatenate(values)
    for query in queries:
        scores = lax.dot_general(
            query, key, (((1,), (1,)), ((), ())), preferred_element_type=jnp.float32
        )
        scores += bias_ref[...]
        highest = jnp.max(scores, axis=1, keepdims=True)
        weights = jnp.exp2((scores - highest) * scale)
        totals = jnp.sum(weights, axis=1, keepdims=True)
        result = jnp.dot(weights.astype(jnp.bfloat16), value, preferred_element_type=jnp.float32)
        yield (result / totals).astype(jnp.bfloat16).reshape(16, 16, HD)


def temporal_middle_kernel(first_ref, got_ref, recv_ref, keep_ref, send_ref, bias_ref):
    core, half = lax.axis_index("core"), lax.axis_index("zl0")
    token_bias(bias_ref)

    def block(part, t):
        at = slice(t * 4, t * 4 + 4)
        if part == 0:
            tiles = [first_ref[zl * 4 + 2 * core + half, at] for zl in range(4)]
        elif part == 1:
            tiles = [got_ref[zl, half, at] for zl in range(4)]
        else:
            tiles = [recv_ref[part - 2, zl, at] for zl in range(4)]
        return jnp.concatenate(tiles).reshape(256, HD)

    tensors = [[block(part, t) for part in range(4)] for t in range(3)]
    for part, result in enumerate(attend_tokens(*tensors, bias_ref)):
        (keep_ref if part < 2 else send_ref)[part % 2] = result


def temporal_own_kernel(in_ref, got_ref, mine_ref, other_ref, bias_ref):
    core = lax.axis_index("core")
    token_bias(bias_ref)
    for half in range(2):

        def block(part, slot, t):
            if part == 0:
                tiles = [in_ref[zl, 2 * core + half, :, t * 2 + slot] for zl in range(4)]
            else:
                tiles = [got_ref[zl, half, :, t * 2 + slot] for zl in range(4)]
            return jnp.concatenate(tiles).reshape(256, HD)

        blocks = [(part, slot) for part in range(2) for slot in range(2)]
        tensors = [[block(part, slot, t) for part, slot in blocks] for t in range(3)]
        for (part, slot), result in zip(blocks, attend_tokens(*tensors, bias_ref)):
            (other_ref if part else mine_ref)[slot, :, half] = result


def attend(query, own_k, ref_k, values):
    scale = LOG2E / math.sqrt(HD)
    nt = (((1,), (1,)), ((), ()))
    own = lax.dot_general(query, own_k, nt, preferred_element_type=jnp.float32)
    ref = lax.dot_general(query, ref_k, nt, preferred_element_type=jnp.float32)
    highest = jnp.maximum(jnp.max(own, axis=1, keepdims=True), jnp.max(ref, axis=1, keepdims=True))
    own = jnp.exp2((own - highest) * scale).astype(jnp.bfloat16)
    ref = jnp.exp2((ref - highest) * scale).astype(jnp.bfloat16)
    own_v, ref_v = values()
    result = jnp.dot(own, own_v, preferred_element_type=jnp.float32)
    result += jnp.dot(ref, ref_v, preferred_element_type=jnp.float32)
    return (result[:, :HD] / result[:, HD:]).astype(jnp.bfloat16)


def with_ones(value):
    return jnp.concatenate((value, jnp.ones_like(value)), axis=1)


def ref_rows(mine_ref, other_ref, t, middle):
    at = t * 6 + middle * 3
    parts = [ref[:, :, at : at + 3].reshape(768, HD) for ref in (mine_ref, other_ref)]
    return jnp.concatenate(parts)


def spatial_first_kernel(*refs):
    *parts, mine_ref, other_ref, out_ref = refs
    y, x = lax.axis_index("y"), lax.axis_index("x")

    def tensor(part, t):
        return jnp.stack([part[0, :, zh * 3 + t] for zh in range(4)], axis=1).reshape(256, HD)

    own_k = jnp.concatenate([tensor(part, 1) for part in parts])
    own_v = with_ones(jnp.concatenate([tensor(part, 2) for part in parts]))
    ref_k = ref_rows(mine_ref, other_ref, 0, 1)
    ref_v = with_ones(ref_rows(mine_ref, other_ref, 1, 1))
    for m, part in enumerate(parts):
        result = attend(tensor(part, 0), own_k, ref_k, lambda: (own_v, ref_v))
        result = result.reshape(4, 4, 16, HD)
        for k in range(4):
            out_ref[lax.rem(y + 4 - k, 4) * 4 + lax.rem(x + 4 - m, 4)] = result[k]


def spatial_second_kernel(x_hbm, mine_hbm, other_hbm, first_hbm, out_ref, x_ref, mine_ref, other_ref, sems):
    moves = [(first_hbm, out_ref.at[:, :, 2])]
    for start, blocks, source, target in (
        (0, 4, x_hbm, x_ref),
        (0, 3, mine_hbm, mine_ref),
        (0, 3, other_hbm, other_ref),
        (4, 2, x_hbm, x_ref),
        (6, 3, mine_hbm, mine_ref),
        (6, 3, other_hbm, other_ref),
    ):
        at = pl.ds(start, blocks)
        moves.append((source.at[:, :, at], target.at[:, :, at]))
    passed, *copies = [pltpu.make_async_copy(*move, sems.at[i]) for i, move in enumerate(moves)]
    for copy in copies:
        copy.start()
    passed.start()
    for copy in copies[:3]:
        copy.wait()
    ref_k = ref_rows(mine_ref, other_ref, 0, 0)
    held = {}

    def values(slot):
        if not held:
            for copy in copies[3:]:
                copy.wait()
            held["ref"] = with_ones(ref_rows(mine_ref, other_ref, 1, 0))
        if slot not in held:
            held[slot] = with_ones(x_ref[:, :, 4 + slot].reshape(1024, HD))
        return held[slot], held["ref"]

    for slot in range(2):
        own_k = x_ref[:, :, 2 + slot].reshape(1024, HD)
        for block in range(4):
            at = slice(block * 4, block * 4 + 4)
            query = x_ref[at, :, slot].reshape(256, HD)
            result = attend(query, own_k, ref_k, lambda: values(slot))
            out_ref[at, :, slot] = result.reshape(4, 4, 16, HD)
    passed.wait()


def sum_kernel(spatial_ref, mine_ref, other_ref, keep_ref, back_ref, middle_ref, out_ref):
    core, zl0 = lax.axis_index("core"), lax.axis_index("zl0")

    def add(group, zh, slot, temporal):
        both = spatial_ref[group, zh, slot].astype(jnp.float32) + temporal.astype(jnp.float32)
        out_ref[group // 4, zh, group % 4, slot] = both.astype(jnp.bfloat16)

    for group in range(16):
        for half in range(2):
            for slot in range(2):
                add(group, 2 * core + half, slot, mine_ref[slot, group, half])
                add(group, 2 - 2 * core + half, slot, other_ref[slot, group, half])
        add(group, 2 * core + zl0, 2, keep_ref[0, group])
        add(group, 2 * core + 1 - zl0, 2, back_ref[0, group])
        add(group, 2 - 2 * core + zl0, 2, middle_ref[0, group])
        add(group, 2 - 2 * core + 1 - zl0, 2, middle_ref[1, group])


def unpack_kernel(in_ref, out_ref):
    for z in range(16):
        for j in range(4):
            for slot in range(3):
                out_ref[frame_of(z, j, slot), :, columns(head_of(z, slot == 2))] = in_ref[z, j, slot]


def call(kernel, out_shapes, *args, flops=0, scratch=(), in_spec=VMEM, vmem=32):
    several = isinstance(out_shapes, list)
    shapes = [jax.ShapeDtypeStruct(s, jnp.bfloat16) for s in (out_shapes if several else [out_shapes])]
    size = sum(a.size * 2 for a in args) + sum(2 * math.prod(s.shape) for s in shapes)
    cost = pl.CostEstimate(flops=flops, bytes_accessed=size, transcendentals=0)
    return pl.pallas_call(
        kernel,
        out_shape=shapes if several else shapes[0],
        in_specs=[in_spec] * len(args),
        out_specs=[VMEM] * len(shapes) if several else VMEM,
        scratch_shapes=scratch,
        compiler_params=pltpu.CompilerParams(vmem_limit_bytes=vmem * 1024 * 1024),
        cost_estimate=cost,
    )(*args)


def swap(tensor, mask):
    return lax.ppermute(tensor, ("zl0", "core"), [(i, i ^ mask) for i in range(4)])


def shift(tensor, axis, step):
    return lax.ppermute(tensor, axis, [(i, (i + step) % 4) for i in range(4)])


def local(queries, keys, values, ref_keys, ref_values):
    first = call(
        pack_first_kernel,
        (16, 13, 16, HD),
        queries,
        keys,
        values,
        ref_keys,
        ref_values,
        in_spec=HBM,
        vmem=62,
        scratch=[
            pltpu.VMEM(ref_keys.shape, jnp.bfloat16),
            pltpu.VMEM(ref_keys.shape, jnp.bfloat16),
            pltpu.SemaphoreType.DMA((50,)),
        ],
    )
    first = lax.all_to_all(first, Z, split_axis=0, concat_axis=0, tiled=True)
    second = call(pack_second_kernel, (16, 4, 3, 2, 16, HD), queries, keys, values)
    first, second = lax.optimization_barrier((first, second))
    second = lax.all_to_all(second, Z, split_axis=0, concat_axis=0, tiled=True)

    *parts, other = call(
        split_first_kernel,
        [(5, 12, 16, HD)] * 4 + [(4, 2, 12, 16, HD)],
        first,
        scratch=[pltpu.VMEM((2, 2, 48, HD), jnp.bfloat16)],
    )
    parts = [parts[0]] + [shift(parts[step], "y", step) for step in (1, 2, 3)]
    rows = [part[4] for part in parts]
    parts = [jnp.stack([part[m] for part in parts] + rows).reshape(2, 4, 12, 16, HD) for m in range(4)]
    parts = [parts[0]] + [shift(parts[step], "x", step) for step in (1, 2, 3)]
    my_refs = jnp.stack([part[1] for part in parts])
    refs = (my_refs, lax.ppermute(my_refs, "core", [(0, 1), (1, 0)]))
    middle = call(
        spatial_first_kernel, (16, 4, 16, HD), *parts, *refs, flops=4 * 1024 * 2560 * HD
    )
    got = swap(other, 1)

    send = call(send_kernel, (2, 4, 12, 16, HD), first, got)

    second, middle, refs, send = lax.optimization_barrier((second, middle, refs, send))
    second = second.reshape(4, 4, 4, 6, 16, HD)
    by_frame = call(split_second_kernel, (16, 4, 6, 16, HD), second)
    other = call(other_kernel, (4, 2, 4, 6, 16, HD), second)

    by_frame = lax.all_to_all(by_frame, YX, split_axis=0, concat_axis=0, tiled=True)

    bias = [pltpu.VMEM((256, 1024), jnp.float32)]
    mine, other = call(
        temporal_own_kernel, [(2, 16, 2, 16, HD)] * 2, second, swap(other, 1), scratch=bias
    )
    recv, mine, other = lax.optimization_barrier((swap(send, 2), mine, other))
    keep, send = call(
        temporal_middle_kernel, [(2, 16, 16, HD)] * 2, first, got, recv, scratch=bias
    )
    by_frame, other, send = lax.optimization_barrier((by_frame, other, send))
    back = swap(send, 2)
    other = swap(other, 1)
    middle_other = swap(jnp.stack((keep[1], back[1])), 1)

    spatial = call(
        spatial_second_kernel,
        (16, 4, 3, 16, HD),
        by_frame,
        *refs,
        middle,
        flops=8 * 1024 * 2560 * HD,
        in_spec=HBM,
        vmem=62,
        scratch=[
            pltpu.VMEM((16, 4, 6, 16, HD), jnp.bfloat16),
            pltpu.VMEM((4, 4, 12, 16, HD), jnp.bfloat16),
            pltpu.VMEM((4, 4, 12, 16, HD), jnp.bfloat16),
            pltpu.SemaphoreType.DMA((7,)),
        ],
    )
    spatial = lax.all_to_all(spatial, YX, split_axis=0, concat_axis=0, tiled=True)

    attended = call(
        sum_kernel, (4, 4, 4, 3, 16, HD), spatial, mine, other, keep, back, middle_other
    )
    attended = attended.reshape(16, 4, 3, 16, HD)
    attended = lax.all_to_all(attended, Z, split_axis=0, concat_axis=0, tiled=True)
    return call(unpack_kernel, queries.shape, attended)


def solution(mesh):
    split = Mesh(mesh.devices.reshape(2, 2, 2, 4, 4, 4), ("zl1", "zl0", "core", "y", "zh", "x"))
    rows = P(("zl1", "zl0", "core"), ("y", "zh", "x"), None)
    refs = P(("zl1", "zl0", "core", "y", "zh", "x"), None)
    return jax.shard_map(
        local,
        mesh=split,
        in_specs=(rows, rows, rows, refs, refs),
        out_specs=rows,
        check_vma=False,
    )
```

time: 261 us -> 251 us (0.962)
  starting transfers between devices: 87.1 us -> 75.5 us
  local copies, waits for them, and re-layouts: 12.3 us -> 5.01 us
  waiting for transfers between devices: 86.1 us -> 90.9 us
  Pallas kernels: 19.9 us -> 24.4 us
    ppermute x12 -> x6, starting transfers between devices: 40.8 us -> 22.9 us  [shift(): return lax.ppermute(tensor, axis, [(i, (i + step) % 4) for i in range(4)])]
    all_to_all x1, waiting for transfers between devices: 0.79 us -> 16.1 us  [local(): second = lax.all_to_all(second, Z, split_axis=0, concat_axis=0, tiled=True)]
    all_to_all x1, waiting for transfers between devices: 10.2 us -> 4.13 us  [local(): lax.all_to_all(spatial, YX, split_axis=0, concat_axis=0, tiled=True)]
    all_to_all x1, waiting for transfers between devices: 6.8 us -> 1.74 us  [local(): lax.all_to_all(by_frame, YX, split_axis=0, concat_axis=0, tiled=True)]
    pallas_call x8 -> x12, Pallas kernels: 19.9 us -> 24.4 us  [call(): pl.pallas_call(kernel, out_shape=shapes if several else shapes[0], in_spe...]
    ppermute x4 -> x6, starting transfers between devices: 10.7 us -> 15.1 us  [swap(): lax.ppermute(tensor, ('zl0', 'core'), [(i, i ^ mask) for i in range(4)])]
    unnamed x34 -> x24, local copies, waits for them, and re-layouts: 7.52 us -> 4.73 us
    ppermute x4 -> x6, waiting for transfers between devices: 7.51 us -> 9.47 us  [swap(): lax.ppermute(tensor, ('zl0', 'core'), [(i, i ^ mask) for i in range(4)])]
  transfers between devices with their start and end apart: 21 -> 17, of which waited for: 12 -> 13; matrix products, arithmetic and copies ran while one was open for 3% -> 0% of each run, Pallas kernels for 5% -> 4%
where the time goes in v3:
time: 251 us; the launch traced here: 250 us
  waiting for transfers between devices  90.9 us (36%)
  starting transfers between devices  75.5 us (30%)
  blocking collectives  53.3 us (21%)
  Pallas kernels  24.4 us (10%)
  local copies, waits for them, and re-layouts  5.01 us (2%)
    all_to_all x1, blocking collectives, local(): lax.all_to_all(attended, Z, split_axis=0, concat_axis=0, tiled=True)  53.3 us
    all_to_all x1, waiting for transfers between devices, local(): first = lax.all_to_all(first, Z, split_axis=0, concat_axis=0, tiled=True)  40.4 us
    pallas_call x12, Pallas kernels, call(): pl.pallas_call(kernel, out_shape=shapes if several else shapes[0], in_spe...  24.4 us
    ppermute x6, starting transfers between devices, shift(): return lax.ppermute(tensor, axis, [(i, (i + step) % 4) for i in range(4)])  22.9 us
    ppermute x6, waiting for transfers between devices, shift(): return lax.ppermute(tensor, axis, [(i, (i + step) % 4) for i in range(4)])  19.1 us
    all_to_all x1, waiting for transfers between devices, local(): second = lax.all_to_all(second, Z, split_axis=0, concat_axis=0, tiled=True)  16.1 us
    all_to_all x1, starting transfers between devices, local(): first = lax.all_to_all(first, Z, split_axis=0, concat_axis=0, tiled=True)  15.4 us
    ppermute x6, starting transfers between devices, swap(): lax.ppermute(tensor, ('zl0', 'core'), [(i, i ^ mask) for i in range(4)])  15.1 us
  transfers between devices with their start and end apart: 17, of which 13 were waited for; matrix products, arithmetic and copies ran while one was open for 0% of the time, Pallas kernels for 4%

profile of v3, /device:TPU:32, one launch (start us, length us, event | category | flops | bytes accessed | tf_op | source)
XLA Modules:
  0.0 249.7 jit_solution(15622187842444960094)
XLA Ops:
  2.6 15.4 %all-to-all-start = ((bf16[16,13,16,128]{3,2,1,0:T(8,128)(2,1)}), bf16[16,13,16,128]{3,2,1,0:T(8,128)(2,1)S(1)}, u32[]{:S(2)}, u32[]{:S(2)}) async-start(bf16[16,13,16,128]{3,2,1,0:T(8,128)(2,1)} %shard_map.55), calls=%async_computation | async-start | bytes 1703936 | tf_op jit(solution)/shard_map/all_to_all | solution.py:314
  19.4 40.4 %all-to-all-done.in_ref.first_ref = bf16[16,13,16,128]{3,2,1,0:T(8,128)(2,1)S(1)} async-done(((bf16[16,13,16,128]{3,2,1,0:T(8,128)(2,1)}), bf16[16,13,16,128]{3,2,1,0:T(8,128)(2,1)S(1)}, u32[]{:S(2)}, u32[]{:S(2)}) %all-to-all-start) | async-done | bytes 852000 | tf_op jit(solution)/shard_map/all_to_all | solution.py:314
  59.8 7.6 %all-to-all-start.1 = ((bf16[16,4,3,2,16,128]{5,4,3,2,1,0:T(8,128)(2,1)}), bf16[16,4,3,2,16,128]{5,4,3,2,1,0:T(8,128)(2,1)S(1)}, u32[]{:S(2)}, u32[]{:S(2)}) async-start(bf16[16,4,3,2,16,128]{5,4,3,2,1,0:T(8,128)(2,1)} %copy-done.1), calls=%async_computation.1 | async-start | bytes 3145728 | tf_op jit(solution)/shard_map/all_to_all | solution.py:317
  67.5 3.5 %collective-permute-start = (bf16[5,12,16,128]{3,2,1,0:T(8,128)(2,1)S(1)}, bf16[5,12,16,128]{3,2,1,0:T(8,128)(2,1)S(1)}, u32[]{:S(2)}, u32[]{:S(2)}) collective-permute-start(bf16[5,12,16,128]{3,2,1,0:T(8,128)(2,1)S(1)} %get-tuple-element.30), channel_id=1, source_target_pairs={{0,16},{16,32},{32,48},{48,0},{1,17},{17,33},{33,49},{49,1},{2,18}... | collective-permute-start | bytes 737288 | tf_op jit(solution)/shard_map/ppermute | solution.py:294
  71.0 4.8 %collective-permute-start.1 = (bf16[5,12,16,128]{3,2,1,0:T(8,128)(2,1)S(1)}, bf16[5,12,16,128]{3,2,1,0:T(8,128)(2,1)S(1)}, u32[]{:S(2)}, u32[]{:S(2)}) collective-permute-start(bf16[5,12,16,128]{3,2,1,0:T(8,128)(2,1)S(1)} %get-tuple-element.31), channel_id=1, source_target_pairs={{0,32},{16,48},{32,0},{48,16},{1,33},{17,49},{33,1},{49,17},{2,34}... | collective-permute-start | bytes 737288 | tf_op jit(solution)/shard_map/ppermute | solution.py:294
  75.9 3.3 %collective-permute-start.2 = (bf16[5,12,16,128]{3,2,1,0:T(8,128)(2,1)S(1)}, bf16[5,12,16,128]{3,2,1,0:T(8,128)(2,1)S(1)}, u32[]{:S(2)}, u32[]{:S(2)}) collective-permute-start(bf16[5,12,16,128]{3,2,1,0:T(8,128)(2,1)S(1)} %get-tuple-element.32), channel_id=1, source_target_pairs={{0,48},{16,0},{32,16},{48,32},{1,49},{17,1},{33,17},{49,33},{2,50}... | collective-permute-start | bytes 737288 | tf_op jit(solution)/shard_map/ppermute | solution.py:294
  79.2 5.3 %collective-permute-done.1 = bf16[5,12,16,128]{3,2,1,0:T(8,128)(2,1)S(1)} collective-permute-done((bf16[5,12,16,128]{3,2,1,0:T(8,128)(2,1)S(1)}, bf16[5,12,16,128]{3,2,1,0:T(8,128)(2,1)S(1)}, u32[]{:S(2)}, u32[]{:S(2)}) %collective-permute-start.1) | collective-permute-done | bytes 245792 | tf_op jit(solution)/shard_map/ppermute | solution.py:294
  86.0 3.4 %collective-permute-start.3 = (bf16[2,4,12,16,128]{4,3,2,1,0:T(8,128)(2,1)S(1)}, bf16[2,4,12,16,128]{4,3,2,1,0:T(8,128)(2,1)S(1)}, u32[]{:S(2)}, u32[]{:S(2)}) collective-permute-start(bf16[2,4,12,16,128]{4,3,2,1,0:T(8,128)(2,1)S(1)} %bitcast.15), channel_id=1, source_target_pairs={{0,1},{1,2},{2,3},{3,0},{4,5},{5,6},{6,7},{7,4},{8,9},{9,10},{10,1... | collective-permute-start | bytes 1179656 | tf_op jit(solution)/shard_map/ppermute | solution.py:294
  89.4 4.6 %collective-permute-start.4 = (bf16[2,4,12,16,128]{4,3,2,1,0:T(8,128)(2,1)S(1)}, bf16[2,4,12,16,128]{4,3,2,1,0:T(8,128)(2,1)S(1)}, u32[]{:S(2)}, u32[]{:S(2)}) collective-permute-start(bf16[2,4,12,16,128]{4,3,2,1,0:T(8,128)(2,1)S(1)} %bitcast.14), channel_id=1, source_target_pairs={{0,2},{1,3},{2,0},{3,1},{4,6},{5,7},{6,4},{7,5},{8,10},{9,11},{10,... | collective-permute-start | bytes 1179656 | tf_op jit(solution)/shard_map/ppermute | solution.py:294
  94.1 3.3 %collective-permute-start.5 = (bf16[2,4,12,16,128]{4,3,2,1,0:T(8,128)(2,1)S(1)}, bf16[2,4,12,16,128]{4,3,2,1,0:T(8,128)(2,1)S(1)}, u32[]{:S(2)}, u32[]{:S(2)}) collective-permute-start(bf16[2,4,12,16,128]{4,3,2,1,0:T(8,128)(2,1)S(1)} %bitcast.13), channel_id=1, source_target_pairs={{0,3},{1,0},{2,1},{3,2},{4,7},{5,4},{6,5},{7,6},{8,11},{9,8},{10,9... | collective-permute-start | bytes 1179656 | tf_op jit(solution)/shard_map/ppermute | solution.py:294
  97.5 2.7 %collective-permute-done.3.refs_1_ = bf16[2,4,12,16,128]{4,3,2,1,0:T(8,128)(2,1)S(1)} collective-permute-done((bf16[2,4,12,16,128]{4,3,2,1,0:T(8,128)(2,1)S(1)}, bf16[2,4,12,16,128]{4,3,2,1,0:T(8,128)(2,1)S(1)}, u32[]{:S(2)}, u32[]{:S(2)}) %collective-permute-start.3) | collective-permute-done | bytes 393248 | tf_op jit(solution)/shard_map/ppermute | solution.py:294
  100.2 8.3 %collective-permute-done.4.refs_2_ = bf16[2,4,12,16,128]{4,3,2,1,0:T(8,128)(2,1)S(1)} collective-permute-done((bf16[2,4,12,16,128]{4,3,2,1,0:T(8,128)(2,1)S(1)}, bf16[2,4,12,16,128]{4,3,2,1,0:T(8,128)(2,1)S(1)}, u32[]{:S(2)}, u32[]{:S(2)}) %collective-permute-start.4) | collective-permute-done | bytes 393248 | tf_op jit(solution)/shard_map/ppermute | solution.py:294
  115.9 3.8 %shard_map.58.first_hbm = bf16[16,4,16,128]{3,2,1,0:T(8,128)(2,1)S(1)} custom-call(bf16[2,4,12,16,128]{4,3,2,1,0:T(8,128)(2,1)S(1)} %bitcast.12, bf16[2,4,12,16,128]{4,3,2,1,0:T(8,128)(2,1)S(1)} %collective-permute-done.3.refs_1_, bf16[2,4,12,16,128]{4,3,2,1,0:T(8,128)(2,1)S(1)} %collective-permute-done.4.refs_2_, ...), custom_call_target="tpu_custom_call" | custom-call | flops 1342177280 | bytes 3407872 | tf_op jit(solution)/shard_map/pallas_call | solution.py:278
  121.3 16.1 %all-to-all-done.1 = bf16[16,4,3,2,16,128]{5,4,3,2,1,0:T(8,128)(2,1)S(1)} async-done(((bf16[16,4,3,2,16,128]{5,4,3,2,1,0:T(8,128)(2,1)}), bf16[16,4,3,2,16,128]{5,4,3,2,1,0:T(8,128)(2,1)S(1)}, u32[]{:S(2)}, u32[]{:S(2)}) %all-to-all-start.1) | async-done | bytes 1572896 | tf_op jit(solution)/shard_map/all_to_all | solution.py:317
  138.6 7.1 %all-to-all-start.2 = ((bf16[16,4,6,16,128]{4,3,2,1,0:T(8,128)(2,1)}), bf16[16,4,6,16,128]{4,3,2,1,0:T(8,128)(2,1)}, u32[]{:S(2)}, u32[]{:S(2)}) async-start(bf16[16,4,6,16,128]{4,3,2,1,0:T(8,128)(2,1)} %copy-done), calls=%async_computation.2 | async-start | bytes 3145728 | tf_op jit(solution)/shard_map/all_to_all | solution.py:343
  147.7 3.5 %collective-permute-start.8 = (bf16[2,4,12,16,128]{4,3,2,1,0:T(8,128)(2,1)S(1)}, bf16[2,4,12,16,128]{4,3,2,1,0:T(8,128)(2,1)S(1)}, u32[]{:S(2)}, u32[]{:S(2)}) collective-permute-start(bf16[2,4,12,16,128]{4,3,2,1,0:T(8,128)(2,1)S(1)} %shard_map.59), channel_id=1, source_target_pairs={{0,128},{64,192},{128,0},{192,64},{1,129},{65,193},{129,1},{193,65... | collective-permute-start | bytes 1179656 | tf_op jit(solution)/shard_map/ppermute | solution.py:290
  151.3 4.1 %shard_map.62 = (bf16[2,16,2,16,128]{4,3,2,1,0:T(8,128)(2,1)S(1)}, bf16[2,16,2,16,128]{4,3,2,1,0:T(8,128)(2,1)S(1)}) custom-call(bf16[4,4,4,6,16,128]{5,4,3,2,1,0:T(8,128)(2,1)S(1)} %bitcast.10, bf16[4,2,4,6,16,128]{5,4,3,2,1,0:T(8,128)(2,1)S(1)} %collective-permute-done.9.got_ref), custom_call_target="tpu_custom_call" | custom-call | bytes 2883584 | tf_op jit(solution)/shard_map/pallas_call | solution.py:278
  156.1 5.1 %collective-permute-done.8.recv_ref = bf16[2,4,12,16,128]{4,3,2,1,0:T(8,128)(2,1)S(1)} collective-permute-done((bf16[2,4,12,16,128]{4,3,2,1,0:T(8,128)(2,1)S(1)}, bf16[2,4,12,16,128]{4,3,2,1,0:T(8,128)(2,1)S(1)}, u32[]{:S(2)}, u32[]{:S(2)}) %collective-permute-start.8) | collective-permute-done | bytes 393248 | tf_op jit(solution)/shard_map/ppermute | solution.py:290
  161.1 2.7 %shard_map.63 = (bf16[2,16,16,128]{3,2,1,0:T(8,128)(2,1)S(1)}, bf16[2,16,16,128]{3,2,1,0:T(8,128)(2,1)}) custom-call(bf16[16,13,16,128]{3,2,1,0:T(8,128)(2,1)S(1)} %all-to-all-done.in_ref.first_ref, bf16[4,2,12,16,128]{4,3,2,1,0:T(8,128)(2,1)S(1)} %collective-permute-done.7.got_ref, bf16[2,4,12,16,128]{4,3,2,1,0:T(8,128)(2,1)S(1)} %collective-permute-done.8.recv_ref), custom_call_target="tpu_custom_call" | custom-call | bytes 1900544 | tf_op jit(solution)/shard_map/pallas_call | solution.py:278
  165.6 9.4 %shard_map.64 = bf16[16,4,3,16,128]{4,3,2,1,0:T(8,128)(2,1)} custom-call(bf16[16,4,6,16,128]{4,3,2,1,0:T(8,128)(2,1)} %all-to-all-done.2.x_hbm, bf16[4,4,12,16,128]{4,3,2,1,0:T(8,128)(2,1)} %copy-done.5, bf16[4,4,12,16,128]{4,3,2,1,0:T(8,128)(2,1)} %copy-done.6, bf16[16,4,16,128]{3,2,1,0:T(8,128)(2,1)} %copy-done.9), custom_call_target="tpu_custom_call" | custom-call | flops 2684354560 | bytes 4194304 | tf_op jit(solution)/shard_map/pallas_call | solution.py:278
  175.0 5.6 %all-to-all-start.3 = ((bf16[16,4,3,16,128]{4,3,2,1,0:T(8,128)(2,1)}), bf16[16,4,3,16,128]{4,3,2,1,0:T(8,128)(2,1)S(1)}, u32[]{:S(2)}, u32[]{:S(2)}) async-start(bf16[16,4,3,16,128]{4,3,2,1,0:T(8,128)(2,1)} %shard_map.64), calls=%async_computation.3 | async-start | bytes 1572864 | tf_op jit(solution)/shard_map/all_to_all | solution.py:374
  180.6 3.4 %collective-permute-start.11 = (bf16[2,16,16,128]{3,2,1,0:T(8,128)(2,1)}, bf16[2,16,16,128]{3,2,1,0:T(8,128)(2,1)S(1)}, u32[]{:S(2)}, u32[]{:S(2)}) collective-permute-start(bf16[2,16,16,128]{3,2,1,0:T(8,128)(2,1)} %get-tuple-element.48), channel_id=1, source_target_pairs={{0,128},{64,192},{128,0},{192,64},{1,129},{65,193},{129,1},{193,65... | collective-permute-start | bytes 393224 | tf_op jit(solution)/shard_map/ppermute | solution.py:290
  191.0 4.1 %all-to-all-done.3.spatial_ref = bf16[16,4,3,16,128]{4,3,2,1,0:T(8,128)(2,1)S(1)} async-done(((bf16[16,4,3,16,128]{4,3,2,1,0:T(8,128)(2,1)}), bf16[16,4,3,16,128]{4,3,2,1,0:T(8,128)(2,1)S(1)}, u32[]{:S(2)}, u32[]{:S(2)}) %all-to-all-start.3) | async-done | bytes 786464 | tf_op jit(solution)/shard_map/all_to_all | solution.py:374
  195.3 53.3 %all_to_all.25.in_ref = bf16[16,4,3,16,128]{4,3,2,1,0:T(8,128)(2,1)S(1)} all-to-all(bf16[16,4,3,16,128]{4,3,2,1,0:T(8,128)(2,1)S(1)} %bitcast.11), channel_id=1, replica_groups=mesh['zl1'=2,'zl0'=2,'core'=2,'y'=4,'zh'=4,'x'=4] {'zl1','zl0','zh'}, dimensions={0} | all-to-all | bytes 1572864 | tf_op jit(solution)/shard_map/all_to_all | solution.py:380
  (59 shorter events, 28.6 us)
Async XLA Ops:
  0.0 17.9 %copy-start.4 = (bf16[8,16,3072]{2,1,0:T(8,128)(2,1)S(1)}, bf16[8,16,3072]{2,1,0:T(8,128)(2,1)}, u32[]{:S(2)}) copy-start(bf16[8,16,3072]{2,1,0:T(8,128)(2,1)} %v_ref.3) | copy-start | bytes 2359300
  2.5 15.4 %copy-start.2 = (bf16[8,16,3072]{2,1,0:T(8,128)(2,1)S(1)}, bf16[8,16,3072]{2,1,0:T(8,128)(2,1)}, u32[]{:S(2)}) copy-start(bf16[8,16,3072]{2,1,0:T(8,128)(2,1)} %q_ref.3) | copy-start | bytes 2359300
  2.5 15.4 %copy-start.3 = (bf16[8,16,3072]{2,1,0:T(8,128)(2,1)S(1)}, bf16[8,16,3072]{2,1,0:T(8,128)(2,1)}, u32[]{:S(2)}) copy-start(bf16[8,16,3072]{2,1,0:T(8,128)(2,1)} %k_ref.3) | copy-start | bytes 2359300
  2.6 57.2 %all-to-all-start = ((bf16[16,13,16,128]{3,2,1,0:T(8,128)(2,1)}), bf16[16,13,16,128]{3,2,1,0:T(8,128)(2,1)S(1)}, u32[]{:S(2)}, u32[]{:S(2)}) async-start(bf16[16,13,16,128]{3,2,1,0:T(8,128)(2,1)} %shard_map.55), calls=%async_computation | async-start | bytes 1703936 | tf_op jit(solution)/shard_map/all_to_all | solution.py:314
  18.2 1.2 copy-start.1
  59.8 77.6 %all-to-all-start.1 = ((bf16[16,4,3,2,16,128]{5,4,3,2,1,0:T(8,128)(2,1)}), bf16[16,4,3,2,16,128]{5,4,3,2,1,0:T(8,128)(2,1)S(1)}, u32[]{:S(2)}, u32[]{:S(2)}) async-start(bf16[16,4,3,2,16,128]{5,4,3,2,1,0:T(8,128)(2,1)} %copy-done.1), calls=%async_computation.1 | async-start | bytes 3145728 | tf_op jit(solution)/shard_map/all_to_all | solution.py:317
  67.5 11.6 %collective-permute-start = (bf16[5,12,16,128]{3,2,1,0:T(8,128)(2,1)S(1)}, bf16[5,12,16,128]{3,2,1,0:T(8,128)(2,1)S(1)}, u32[]{:S(2)}, u32[]{:S(2)}) collective-permute-start(bf16[5,12,16,128]{3,2,1,0:T(8,128)(2,1)S(1)} %get-tuple-element.30), channel_id=1, source_target_pairs={{0,16},{16,32},{32,48},{48,0},{1,17},{17,33},{33,49},{49,1},{2,18}... | collective-permute-start | bytes 737288 | tf_op jit(solution)/shard_map/ppermute | solution.py:294
  71.0 13.4 %collective-permute-start.1 = (bf16[5,12,16,128]{3,2,1,0:T(8,128)(2,1)S(1)}, bf16[5,12,16,128]{3,2,1,0:T(8,128)(2,1)S(1)}, u32[]{:S(2)}, u32[]{:S(2)}) collective-permute-start(bf16[5,12,16,128]{3,2,1,0:T(8,128)(2,1)S(1)} %get-tuple-element.31), channel_id=1, source_target_pairs={{0,32},{16,48},{32,0},{48,16},{1,33},{17,49},{33,1},{49,17},{2,34}... | collective-permute-start | bytes 737288 | tf_op jit(solution)/shard_map/ppermute | solution.py:294
  75.9 9.9 %collective-permute-start.2 = (bf16[5,12,16,128]{3,2,1,0:T(8,128)(2,1)S(1)}, bf16[5,12,16,128]{3,2,1,0:T(8,128)(2,1)S(1)}, u32[]{:S(2)}, u32[]{:S(2)}) collective-permute-start(bf16[5,12,16,128]{3,2,1,0:T(8,128)(2,1)S(1)} %get-tuple-element.32), channel_id=1, source_target_pairs={{0,48},{16,0},{32,16},{48,32},{1,49},{17,1},{33,17},{49,33},{2,50}... | collective-permute-start | bytes 737288 | tf_op jit(solution)/shard_map/ppermute | solution.py:294
  86.0 14.2 %collective-permute-start.3 = (bf16[2,4,12,16,128]{4,3,2,1,0:T(8,128)(2,1)S(1)}, bf16[2,4,12,16,128]{4,3,2,1,0:T(8,128)(2,1)S(1)}, u32[]{:S(2)}, u32[]{:S(2)}) collective-permute-start(bf16[2,4,12,16,128]{4,3,2,1,0:T(8,128)(2,1)S(1)} %bitcast.15), channel_id=1, source_target_pairs={{0,1},{1,2},{2,3},{3,0},{4,5},{5,6},{6,7},{7,4},{8,9},{9,10},{10,1... | collective-permute-start | bytes 1179656 | tf_op jit(solution)/shard_map/ppermute | solution.py:294
  89.4 19.0 %collective-permute-start.4 = (bf16[2,4,12,16,128]{4,3,2,1,0:T(8,128)(2,1)S(1)}, bf16[2,4,12,16,128]{4,3,2,1,0:T(8,128)(2,1)S(1)}, u32[]{:S(2)}, u32[]{:S(2)}) collective-permute-start(bf16[2,4,12,16,128]{4,3,2,1,0:T(8,128)(2,1)S(1)} %bitcast.14), channel_id=1, source_target_pairs={{0,2},{1,3},{2,0},{3,1},{4,6},{5,7},{6,4},{7,5},{8,10},{9,11},{10,... | collective-permute-start | bytes 1179656 | tf_op jit(solution)/shard_map/ppermute | solution.py:294
  94.1 15.9 %collective-permute-start.5 = (bf16[2,4,12,16,128]{4,3,2,1,0:T(8,128)(2,1)S(1)}, bf16[2,4,12,16,128]{4,3,2,1,0:T(8,128)(2,1)S(1)}, u32[]{:S(2)}, u32[]{:S(2)}) collective-permute-start(bf16[2,4,12,16,128]{4,3,2,1,0:T(8,128)(2,1)S(1)} %bitcast.13), channel_id=1, source_target_pairs={{0,3},{1,0},{2,1},{3,2},{4,7},{5,4},{6,5},{7,6},{8,11},{9,8},{10,9... | collective-permute-start | bytes 1179656 | tf_op jit(solution)/shard_map/ppermute | solution.py:294
  110.1 5.7 %copy-start.5 = (bf16[4,4,12,16,128]{4,3,2,1,0:T(8,128)(2,1)}, bf16[4,4,12,16,128]{4,3,2,1,0:T(8,128)(2,1)S(1)}, u32[]{:S(2)}) copy-start(bf16[4,4,12,16,128]{4,3,2,1,0:T(8,128)(2,1)S(1)} %pad_maximum_fusion.refs_4_.mine_hbm) | copy-start | bytes 2359300
  110.2 5.7 %collective-permute-start.6 = (bf16[4,4,12,16,128]{4,3,2,1,0:T(8,128)(2,1)S(1)}, bf16[4,4,12,16,128]{4,3,2,1,0:T(8,128)(2,1)S(1)}, u32[]{:S(2)}, u32[]{:S(2)}) collective-permute-start(bf16[4,4,12,16,128]{4,3,2,1,0:T(8,128)(2,1)S(1)} %pad_maximum_fusion.refs_4_.mine_hbm), channel_id=1, source_target_pairs={{0,64},{64,0},{1,65},{65,1},{2,66},{66,2},{3,67},{67,3},{4,68},{68... | collective-permute-start | bytes 2359304 | tf_op jit(solution)/shard_map/ppermute | solution.py:330
  112.1 3.7 %collective-permute-start.7 = (bf16[4,2,12,16,128]{4,3,2,1,0:T(8,128)(2,1)S(1)}, bf16[4,2,12,16,128]{4,3,2,1,0:T(8,128)(2,1)S(1)}, u32[]{:S(2)}, u32[]{:S(2)}) collective-permute-start(bf16[4,2,12,16,128]{4,3,2,1,0:T(8,128)(2,1)S(1)} %get-tuple-element.33), channel_id=1, source_target_pairs={{0,64},{64,0},{128,192},{192,128},{1,65},{65,1},{129,193},{193,129... | collective-permute-start | bytes 1179656 | tf_op jit(solution)/shard_map/ppermute | solution.py:290
  137.5 1.2 copy-start
  138.6 27.0 %all-to-all-start.2 = ((bf16[16,4,6,16,128]{4,3,2,1,0:T(8,128)(2,1)}), bf16[16,4,6,16,128]{4,3,2,1,0:T(8,128)(2,1)}, u32[]{:S(2)}, u32[]{:S(2)}) async-start(bf16[16,4,6,16,128]{4,3,2,1,0:T(8,128)(2,1)} %copy-done), calls=%async_computation.2 | async-start | bytes 3145728 | tf_op jit(solution)/shard_map/all_to_all | solution.py:343
  145.8 5.5 %collective-permute-start.9 = (bf16[4,2,4,6,16,128]{5,4,3,2,1,0:T(8,128)(2,1)S(1)}, bf16[4,2,4,6,16,128]{5,4,3,2,1,0:T(8,128)(2,1)S(1)}, u32[]{:S(2)}, u32[]{:S(2)}) collective-permute-start(bf16[4,2,4,6,16,128]{5,4,3,2,1,0:T(8,128)(2,1)S(1)} %shard_map.61), channel_id=1, source_target_pairs={{0,64},{64,0},{128,192},{192,128},{1,65},{65,1},{129,193},{193,129... | collective-permute-start | bytes 2359304 | tf_op jit(solution)/shard_map/ppermute | solution.py:290
  147.7 13.4 %collective-permute-start.8 = (bf16[2,4,12,16,128]{4,3,2,1,0:T(8,128)(2,1)S(1)}, bf16[2,4,12,16,128]{4,3,2,1,0:T(8,128)(2,1)S(1)}, u32[]{:S(2)}, u32[]{:S(2)}) collective-permute-start(bf16[2,4,12,16,128]{4,3,2,1,0:T(8,128)(2,1)S(1)} %shard_map.59), channel_id=1, source_target_pairs={{0,128},{64,192},{128,0},{192,64},{1,129},{65,193},{129,1},{193,65... | collective-permute-start | bytes 1179656 | tf_op jit(solution)/shard_map/ppermute | solution.py:290
  175.0 9.0 %copy-start.8 = (bf16[2,16,2,16,128]{4,3,2,1,0:T(8,128)(2,1)S(1)}, bf16[2,16,2,16,128]{4,3,2,1,0:T(8,128)(2,1)}, u32[]{:S(2)}) copy-start(bf16[2,16,2,16,128]{4,3,2,1,0:T(8,128)(2,1)} %copy-done.7) | copy-start | bytes 786436
  175.0 20.1 %all-to-all-start.3 = ((bf16[16,4,3,16,128]{4,3,2,1,0:T(8,128)(2,1)}), bf16[16,4,3,16,128]{4,3,2,1,0:T(8,128)(2,1)S(1)}, u32[]{:S(2)}, u32[]{:S(2)}) async-start(bf16[16,4,3,16,128]{4,3,2,1,0:T(8,128)(2,1)} %shard_map.64), calls=%async_computation.3 | async-start | bytes 1572864 | tf_op jit(solution)/shard_map/all_to_all | solution.py:374
  180.6 7.1 %collective-permute-start.11 = (bf16[2,16,16,128]{3,2,1,0:T(8,128)(2,1)}, bf16[2,16,16,128]{3,2,1,0:T(8,128)(2,1)S(1)}, u32[]{:S(2)}, u32[]{:S(2)}) collective-permute-start(bf16[2,16,16,128]{3,2,1,0:T(8,128)(2,1)} %get-tuple-element.48), channel_id=1, source_target_pairs={{0,128},{64,192},{128,0},{192,64},{1,129},{65,193},{129,1},{193,65... | collective-permute-start | bytes 393224 | tf_op jit(solution)/shard_map/ppermute | solution.py:290
  184.0 7.0 %collective-permute-start.10 = (bf16[2,16,2,16,128]{4,3,2,1,0:T(8,128)(2,1)S(1)}, bf16[2,16,2,16,128]{4,3,2,1,0:T(8,128)(2,1)S(1)}, u32[]{:S(2)}, u32[]{:S(2)}) collective-permute-start(bf16[2,16,2,16,128]{4,3,2,1,0:T(8,128)(2,1)S(1)} %copy-done.8), channel_id=1, source_target_pairs={{0,64},{64,0},{128,192},{192,128},{1,65},{65,1},{129,193},{193,129... | collective-permute-start | bytes 786440 | tf_op jit(solution)/shard_map/ppermute | solution.py:290
  187.7 3.2 %collective-permute-start.12 = (bf16[2,16,16,128]{3,2,1,0:T(8,128)(2,1)S(1)}, bf16[2,16,16,128]{3,2,1,0:T(8,128)(2,1)S(1)}, u32[]{:S(2)}, u32[]{:S(2)}) collective-permute-start(bf16[2,16,16,128]{3,2,1,0:T(8,128)(2,1)S(1)} %pad_maximum_fusion.1), channel_id=1, source_target_pairs={{0,64},{64,0},{128,192},{192,128},{1,65},{65,1},{129,193},{193,129... | collective-permute-start | bytes 393224 | tf_op jit(solution)/shard_map/ppermute | solution.py:290
  (3 other events, 2.3 us)

commit v4 on v3

--- a/solution.py
+++ b/solution.py
@@ -9,48 +9,61 @@
 
 HD = 128
 LOG2E = 1.4426950408889634
-Z = ("zl1", "zl0", "zh")
+Z = ("zh1", "zl1", "zl0", "zh0")
 YX = ("y", "x")
 VMEM = pl.BlockSpec(memory_space=pltpu.VMEM)
 HBM = pl.BlockSpec(memory_space=pltpu.HBM)
 
 
-def head_of(z_index, middle):
-    zl1, zl0, zh = z_index // 8, (z_index // 4) % 2, z_index % 4
-    pair = zh * 2 + zl1
-    return pair * 3 + (1 if middle else 2 * zl0)
-
-
-def frame_of(z_index, j, slot):
-    zl0 = (z_index // 4) % 2
-    return 4 * zl0 + j if slot == 2 else 2 * j + slot
+def z_index(zl, zh1, zh0):
+    at = {"zl1": zl // 2, "zl0": zl % 2, "zh1": zh1, "zh0": zh0}
+    return at[Z[0]] * 8 + at[Z[1]] * 4 + at[Z[2]] * 2 + at[Z[3]]
+
+
+def chip_of(index):
+    at = {axis: index >> (3 - i) & 1 for i, axis in enumerate(Z)}
+    return at["zl1"], at["zl0"], at["zh1"] * 2 + at["zh0"]
+
+
+def head_of(index, middle):
+    zl1, zl0, zh = chip_of(index)
+    return (zh * 2 + zl1) * 3 + (1 if middle else 2 * zl0)
+
+
+def frame_of(index, j, slot):
+    return 4 * chip_of(index)[1] + j if slot == 2 else 2 * j + slot
 
 
 def columns(head):
     return slice(head * HD, (head + 1) * HD)
 
 
-def pack_first_kernel(q_ref, k_ref, v_ref, ref_key_ref, ref_value_ref, out_ref, key_rows, value_rows, sems):
-    copies = [
-        pltpu.make_async_copy(ref_key_ref, key_rows, sems.at[48]),
-        pltpu.make_async_copy(ref_value_ref, value_rows, sems.at[49]),
+def pack_first_kernel(q_ref, k_ref, v_ref, ref_key_ref, ref_value_ref, out_hbm, out_ref, key_rows, value_rows, sems):
+    rows = [
+        pltpu.make_async_copy(ref_key_ref, key_rows, sems.at[64]),
+        pltpu.make_async_copy(ref_value_ref, value_rows, sems.at[65]),
     ]
+    reads, writes = [], []
     for z in range(16):
         for t, ref in enumerate((q_ref, k_ref, v_ref)):
             frames = pl.ds(frame_of(z, 0, 2), 4)
             source = ref.at[frames, :, pl.ds(head_of(z, True) * HD, HD)]
             target = out_ref.at[z, pl.ds(t * 4, 4)]
-            copies.append(pltpu.make_async_copy(source, target, sems.at[z * 3 + t]))
-    for copy in copies:
+            reads.append(pltpu.make_async_copy(source, target, sems.at[z * 4 + t]))
+        writes.append(pltpu.make_async_copy(out_ref.at[z], out_hbm.at[z], sems.at[z * 4 + 3]))
+    for copy in rows + reads:
         copy.start()
-    for copy in copies[:2]:
+    for copy in rows:
         copy.wait()
     for z in range(16):
         for t, ref in enumerate((key_rows, value_rows)):
             for middle in range(2):
                 at = (t * 2 + middle) * 4
                 out_ref[z, 12, at : at + 3] = ref[:, columns(head_of(z, middle))]
-    for copy in copies[2:]:
+        for copy in reads[z * 3 : z * 3 + 3]:
+            copy.wait()
+        writes[z].start()
+    for copy in writes:
         copy.wait()
 
 
@@ -67,7 +80,7 @@
     y, x, core = lax.axis_index("y"), lax.axis_index("x"), lax.axis_index("core")
     for zl in range(4):
         for half in range(2):
-            other_ref[zl, half] = in_ref[zl * 4 + 2 - 2 * core + half, :12]
+            other_ref[zl, half] = in_ref[z_index(zl, 1 - core, half), :12]
     for z in range(16):
         for t in range(2):
             for middle in range(2):
@@ -80,14 +93,14 @@
             j = lax.rem(x + m, 4)
             for zh in range(4):
                 for t in range(3):
-                    part_ref[m, zh * 3 + t] = in_ref[zl * 4 + zh, t * 4 + j]
+                    part_ref[m, zh * 3 + t] = in_ref[z_index(zl, zh // 2, zh % 2), t * 4 + j]
         part_ref[4] = rows
 
 
 def send_kernel(first_ref, got_ref, out_ref):
     core, half = lax.axis_index("core"), 1 - lax.axis_index("zl0")
     for zl in range(4):
-        out_ref[0, zl] = first_ref[zl * 4 + 2 * core + half, :12]
+        out_ref[0, zl] = first_ref[z_index(zl, core, half), :12]
         out_ref[1, zl] = got_ref[zl, half]
 
 
@@ -95,14 +108,14 @@
     for zl in range(4):
         for zh in range(4):
             for j in range(4):
-                frame_ref[zl * 4 + j, zh] = in_ref[zl, zh, j]
+                frame_ref[zl * 4 + j, zh] = in_ref[z_index(zl, zh // 2, zh % 2), j]
 
 
 def other_kernel(in_ref, other_ref):
     core = lax.axis_index("core")
     for zl in range(4):
         for half in range(2):
-            other_ref[zl, half] = in_ref[zl, 2 - 2 * core + half]
+            other_ref[zl, half] = in_ref[z_index(zl, 1 - core, half)]
 
 
 def token_bias(bias_ref):
@@ -133,7 +146,7 @@
     def block(part, t):
         at = slice(t * 4, t * 4 + 4)
         if part == 0:
-            tiles = [first_ref[zl * 4 + 2 * core + half, at] for zl in range(4)]
+            tiles = [first_ref[z_index(zl, core, half), at] for zl in range(4)]
         elif part == 1:
             tiles = [got_ref[zl, half, at] for zl in range(4)]
         else:
@@ -152,7 +165,7 @@
 
         def block(part, slot, t):
             if part == 0:
-                tiles = [in_ref[zl, 2 * core + half, :, t * 2 + slot] for zl in range(4)]
+                tiles = [in_ref[z_index(zl, core, half), :, t * 2 + slot] for zl in range(4)]
             else:
                 tiles = [got_ref[zl, half, :, t * 2 + slot] for zl in range(4)]
             return jnp.concatenate(tiles).reshape(256, HD)
@@ -163,17 +176,21 @@
             (other_ref if part else mine_ref)[slot, :, half] = result
 
 
-def attend(query, own_k, ref_k, values):
+def score(query, keys):
+    nt = (((1,), (1,)), ((), ()))
+    return [lax.dot_general(query, key, nt, preferred_element_type=jnp.float32) for key in keys]
+
+
+def weigh(scores, values):
     scale = LOG2E / math.sqrt(HD)
-    nt = (((1,), (1,)), ((), ()))
-    own = lax.dot_general(query, own_k, nt, preferred_element_type=jnp.float32)
-    ref = lax.dot_general(query, ref_k, nt, preferred_element_type=jnp.float32)
-    highest = jnp.maximum(jnp.max(own, axis=1, keepdims=True), jnp.max(ref, axis=1, keepdims=True))
-    own = jnp.exp2((own - highest) * scale).astype(jnp.bfloat16)
-    ref = jnp.exp2((ref - highest) * scale).astype(jnp.bfloat16)
-    own_v, ref_v = values()
-    result = jnp.dot(own, own_v, preferred_element_type=jnp.float32)
-    result += jnp.dot(ref, ref_v, preferred_element_type=jnp.float32)
+    highest = [jnp.max(part, axis=1, keepdims=True) for part in scores]
+    highest = jnp.maximum(*highest)
+    weights = [jnp.exp2((part - highest) * scale).astype(jnp.bfloat16) for part in scores]
+    result = [
+        jnp.dot(part, value, preferred_element_type=jnp.float32)
+        for part, value in zip(weights, values)
+    ]
+    result = result[0] + result[1]
     return (result[:, :HD] / result[:, HD:]).astype(jnp.bfloat16)
 
 
@@ -196,17 +213,17 @@
 
     own_k = jnp.concatenate([tensor(part, 1) for part in parts])
     own_v = with_ones(jnp.concatenate([tensor(part, 2) for part in parts]))
-    ref_k = ref_rows(mine_ref, other_ref, 0, 1)
-    ref_v = with_ones(ref_rows(mine_ref, other_ref, 1, 1))
+    keys = own_k, ref_rows(mine_ref, other_ref, 0, 1)
+    values = own_v, with_ones(ref_rows(mine_ref, other_ref, 1, 1))
     for m, part in enumerate(parts):
-        result = attend(tensor(part, 0), own_k, ref_k, lambda: (own_v, ref_v))
+        result = weigh(score(tensor(part, 0), keys), values)
         result = result.reshape(4, 4, 16, HD)
         for k in range(4):
             out_ref[lax.rem(y + 4 - k, 4) * 4 + lax.rem(x + 4 - m, 4)] = result[k]
 
 
-def spatial_second_kernel(x_hbm, mine_hbm, other_hbm, first_hbm, out_ref, x_ref, mine_ref, other_ref, sems):
-    moves = [(first_hbm, out_ref.at[:, :, 2])]
+def spatial_second_kernel(x_hbm, mine_hbm, other_hbm, first_hbm, out_hbm, x_ref, mine_ref, other_ref, out_ref, sems):
+    moves = [(first_hbm, out_ref.at[2])]
     for start, blocks, source, target in (
         (0, 4, x_hbm, x_ref),
         (0, 3, mine_hbm, mine_ref),
@@ -224,43 +241,46 @@
     for copy in copies[:3]:
         copy.wait()
     ref_k = ref_rows(mine_ref, other_ref, 0, 0)
-    held = {}
-
-    def values(slot):
-        if not held:
-            for copy in copies[3:]:
-                copy.wait()
-            held["ref"] = with_ones(ref_rows(mine_ref, other_ref, 1, 0))
-        if slot not in held:
-            held[slot] = with_ones(x_ref[:, :, 4 + slot].reshape(1024, HD))
-        return held[slot], held["ref"]
-
-    for slot in range(2):
-        own_k = x_ref[:, :, 2 + slot].reshape(1024, HD)
-        for block in range(4):
-            at = slice(block * 4, block * 4 + 4)
-            query = x_ref[at, :, slot].reshape(256, HD)
-            result = attend(query, own_k, ref_k, lambda: values(slot))
-            out_ref[at, :, slot] = result.reshape(4, 4, 16, HD)
+    blocks = [(slot, slice(at, at + 4)) for slot in range(2) for at in range(0, 16, 4)]
+
+    def scores(slot, at):
+        keys = x_ref[:, :, 2 + slot].reshape(1024, HD), ref_k
+        return score(x_ref[at, :, slot].reshape(256, HD), keys)
+
+    later = scores(*blocks[0])
+    for copy in copies[3:]:
+        copy.wait()
+    ref_v = with_ones(ref_rows(mine_ref, other_ref, 1, 0))
     passed.wait()
+    writes = [pltpu.make_async_copy(out_ref.at[2], out_hbm.at[:, :, 2], sems.at[15])]
+    writes[0].start()
+    for i, (slot, at) in enumerate(blocks):
+        now, later = later, scores(*blocks[i + 1]) if i < 7 else None
+        result = weigh(now, (with_ones(x_ref[:, :, 4 + slot].reshape(1024, HD)), ref_v))
+        out_ref[slot, at] = result.reshape(4, 4, 16, HD)
+        target = out_hbm.at[pl.ds(at.start, 4), :, slot]
+        writes.append(pltpu.make_async_copy(out_ref.at[slot, pl.ds(at.start, 4)], target, sems.at[7 + i]))
+        writes[-1].start()
+    for write in writes:
+        write.wait()
 
 
 def sum_kernel(spatial_ref, mine_ref, other_ref, keep_ref, back_ref, middle_ref, out_ref):
     core, zl0 = lax.axis_index("core"), lax.axis_index("zl0")
 
-    def add(group, zh, slot, temporal):
-        both = spatial_ref[group, zh, slot].astype(jnp.float32) + temporal.astype(jnp.float32)
-        out_ref[group // 4, zh, group % 4, slot] = both.astype(jnp.bfloat16)
+    def add(group, zh1, zh0, slot, temporal):
+        both = spatial_ref[group, zh1 * 2 + zh0, slot].astype(jnp.float32) + temporal.astype(jnp.float32)
+        out_ref[z_index(group // 4, zh1, zh0), group % 4, slot] = both.astype(jnp.bfloat16)
 
     for group in range(16):
         for half in range(2):
             for slot in range(2):
-                add(group, 2 * core + half, slot, mine_ref[slot, group, half])
-                add(group, 2 - 2 * core + half, slot, other_ref[slot, group, half])
-        add(group, 2 * core + zl0, 2, keep_ref[0, group])
-        add(group, 2 * core + 1 - zl0, 2, back_ref[0, group])
-        add(group, 2 - 2 * core + zl0, 2, middle_ref[0, group])
-        add(group, 2 - 2 * core + 1 - zl0, 2, middle_ref[1, group])
+                add(group, core, half, slot, mine_ref[slot, group, half])
+                add(group, 1 - core, half, slot, other_ref[slot, group, half])
+        add(group, core, zl0, 2, keep_ref[0, group])
+        add(group, core, 1 - zl0, 2, back_ref[0, group])
+        add(group, 1 - core, zl0, 2, middle_ref[0, group])
+        add(group, 1 - core, 1 - zl0, 2, middle_ref[1, group])
 
 
 def unpack_kernel(in_ref, out_ref):
@@ -270,7 +290,7 @@
                 out_ref[frame_of(z, j, slot), :, columns(head_of(z, slot == 2))] = in_ref[z, j, slot]
 
 
-def call(kernel, out_shapes, *args, flops=0, scratch=(), in_spec=VMEM, vmem=32):
+def call(kernel, out_shapes, *args, flops=0, scratch=(), in_spec=VMEM, out_spec=VMEM, vmem=32):
     several = isinstance(out_shapes, list)
     shapes = [jax.ShapeDtypeStruct(s, jnp.bfloat16) for s in (out_shapes if several else [out_shapes])]
     size = sum(a.size * 2 for a in args) + sum(2 * math.prod(s.shape) for s in shapes)
@@ -279,7 +299,7 @@
         kernel,
         out_shape=shapes if several else shapes[0],
         in_specs=[in_spec] * len(args),
-        out_specs=[VMEM] * len(shapes) if several else VMEM,
+        out_specs=[VMEM] * len(shapes) if several else out_spec,
         scratch_shapes=scratch,
         compiler_params=pltpu.CompilerParams(vmem_limit_bytes=vmem * 1024 * 1024),
         cost_estimate=cost,
@@ -304,11 +324,13 @@
         ref_keys,
         ref_values,
         in_spec=HBM,
+        out_spec=HBM,
         vmem=62,
         scratch=[
+            pltpu.VMEM((16, 13, 16, HD), jnp.bfloat16),
             pltpu.VMEM(ref_keys.shape, jnp.bfloat16),
             pltpu.VMEM(ref_keys.shape, jnp.bfloat16),
-            pltpu.SemaphoreType.DMA((50,)),
+            pltpu.SemaphoreType.DMA((66,)),
         ],
     )
     first = lax.all_to_all(first, Z, split_axis=0, concat_axis=0, tiled=True)
@@ -336,7 +358,7 @@
     send = call(send_kernel, (2, 4, 12, 16, HD), first, got)
 
     second, middle, refs, send = lax.optimization_barrier((second, middle, refs, send))
-    second = second.reshape(4, 4, 4, 6, 16, HD)
+    second = second.reshape(16, 4, 6, 16, HD)
     by_frame = call(split_second_kernel, (16, 4, 6, 16, HD), second)
     other = call(other_kernel, (4, 2, 4, 6, 16, HD), second)
 
@@ -363,28 +385,30 @@
         middle,
         flops=8 * 1024 * 2560 * HD,
         in_spec=HBM,
+        out_spec=HBM,
         vmem=62,
         scratch=[
             pltpu.VMEM((16, 4, 6, 16, HD), jnp.bfloat16),
             pltpu.VMEM((4, 4, 12, 16, HD), jnp.bfloat16),
             pltpu.VMEM((4, 4, 12, 16, HD), jnp.bfloat16),
-            pltpu.SemaphoreType.DMA((7,)),
+            pltpu.VMEM((3, 16, 4, 16, HD), jnp.bfloat16),
+            pltpu.SemaphoreType.DMA((16,)),
         ],
     )
     spatial = lax.all_to_all(spatial, YX, split_axis=0, concat_axis=0, tiled=True)
 
     attended = call(
-        sum_kernel, (4, 4, 4, 3, 16, HD), spatial, mine, other, keep, back, middle_other
-    )
-    attended = attended.reshape(16, 4, 3, 16, HD)
+        sum_kernel, (16, 4, 3, 16, HD), spatial, mine, other, keep, back, middle_other
+    )
     attended = lax.all_to_all(attended, Z, split_axis=0, concat_axis=0, tiled=True)
     return call(unpack_kernel, queries.shape, attended)
 
 
 def solution(mesh):
-    split = Mesh(mesh.devices.reshape(2, 2, 2, 4, 4, 4), ("zl1", "zl0", "core", "y", "zh", "x"))
-    rows = P(("zl1", "zl0", "core"), ("y", "zh", "x"), None)
-    refs = P(("zl1", "zl0", "core", "y", "zh", "x"), None)
+    axes = ("zl1", "zl0", "core", "y", "zh1", "zh0", "x")
+    split = Mesh(mesh.devices.reshape(2, 2, 2, 4, 2, 2, 4), axes)
+    rows = P(axes[:3], axes[3:], None)
+    refs = P(axes, None)
     return jax.shard_map(
         local,
         mesh=split,

time: 251 us -> 248 us (0.988)
  the two profiles are of different devices: /device:TPU:32 before, /device:TPU:2 now
where the time goes in v4:
time: 248 us; the launch traced here: 247 us
  waiting for transfers between devices  98.9 us (40%)
  starting transfers between devices  70.8 us (29%)
  blocking collectives  48.1 us (19%)
  Pallas kernels  23.4 us (9%)
  local copies, waits for them, and re-layouts  5.01 us (2%)
    all_to_all x1, blocking collectives, local(): lax.all_to_all(attended, Z, split_axis=0, concat_axis=0, tiled=True)  48.1 us
    all_to_all x1, waiting for transfers between devices, local(): first = lax.all_to_all(first, Z, split_axis=0, concat_axis=0, tiled=True)  41.9 us
    pallas_call x12, Pallas kernels, call(): pl.pallas_call(kernel, out_shape=shapes if several else shapes[0], in_spe...  23.4 us
    ppermute x6, starting transfers between devices, shift(): return lax.ppermute(tensor, axis, [(i, (i + step) % 4) for i in range(4)])  22 us
    ppermute x6, waiting for transfers between devices, shift(): return lax.ppermute(tensor, axis, [(i, (i + step) % 4) for i in range(4)])  21.1 us
    all_to_all x1, waiting for transfers between devices, local(): second = lax.all_to_all(second, Z, split_axis=0, concat_axis=0, tiled=True)  18.3 us
    all_to_all x1, starting transfers between devices, local(): first = lax.all_to_all(first, Z, split_axis=0, concat_axis=0, tiled=True)  15.3 us
    ppermute x6, waiting for transfers between devices, swap(): lax.ppermute(tensor, ('zl0', 'core'), [(i, i ^ mask) for i in range(4)])  12.4 us
  transfers between devices with their start and end apart: 17, of which 14 were waited for; matrix products, arithmetic and copies ran while one was open for 0% of the time, Pallas kernels for 5%

profile of v4, /device:TPU:2, one launch (start us, length us, event | category | flops | bytes accessed | tf_op | source)
XLA Modules:
  0.0 246.7 jit_solution(17200483987415459293)
XLA Ops:
  2.4 15.3 %all-to-all-start = ((bf16[16,13,16,128]{3,2,1,0:T(8,128)(2,1)}), bf16[16,13,16,128]{3,2,1,0:T(8,128)(2,1)S(1)}, u32[]{:S(2)}, u32[]{:S(2)}) async-start(bf16[16,13,16,128]{3,2,1,0:T(8,128)(2,1)} %shard_map.55), calls=%async_computation | async-start | bytes 1703936 | tf_op jit(solution)/shard_map/all_to_all | solution.py:336
  19.3 41.9 %all-to-all-done.in_ref.first_ref = bf16[16,13,16,128]{3,2,1,0:T(8,128)(2,1)S(1)} async-done(((bf16[16,13,16,128]{3,2,1,0:T(8,128)(2,1)}), bf16[16,13,16,128]{3,2,1,0:T(8,128)(2,1)S(1)}, u32[]{:S(2)}, u32[]{:S(2)}) %all-to-all-start) | async-done | bytes 852000 | tf_op jit(solution)/shard_map/all_to_all | solution.py:336
  61.2 6.0 %all-to-all-start.1 = ((bf16[16,4,3,2,16,128]{5,4,3,2,1,0:T(8,128)(2,1)}), bf16[16,4,3,2,16,128]{5,4,3,2,1,0:T(8,128)(2,1)S(1)}, u32[]{:S(2)}, u32[]{:S(2)}) async-start(bf16[16,4,3,2,16,128]{5,4,3,2,1,0:T(8,128)(2,1)} %copy-done.1), calls=%async_computation.1 | async-start | bytes 3145728 | tf_op jit(solution)/shard_map/all_to_all | solution.py:339
  67.4 3.5 %collective-permute-start = (bf16[5,12,16,128]{3,2,1,0:T(8,128)(2,1)S(1)}, bf16[5,12,16,128]{3,2,1,0:T(8,128)(2,1)S(1)}, u32[]{:S(2)}, u32[]{:S(2)}) collective-permute-start(bf16[5,12,16,128]{3,2,1,0:T(8,128)(2,1)S(1)} %get-tuple-element.30), channel_id=1, source_target_pairs={{0,16},{16,32},{32,48},{48,0},{1,17},{17,33},{33,49},{49,1},{2,18}... | collective-permute-start | bytes 737288 | tf_op jit(solution)/shard_map/ppermute | solution.py:314
  70.9 4.8 %collective-permute-start.1 = (bf16[5,12,16,128]{3,2,1,0:T(8,128)(2,1)S(1)}, bf16[5,12,16,128]{3,2,1,0:T(8,128)(2,1)S(1)}, u32[]{:S(2)}, u32[]{:S(2)}) collective-permute-start(bf16[5,12,16,128]{3,2,1,0:T(8,128)(2,1)S(1)} %get-tuple-element.31), channel_id=1, source_target_pairs={{0,32},{16,48},{32,0},{48,16},{1,33},{17,49},{33,1},{49,17},{2,34}... | collective-permute-start | bytes 737288 | tf_op jit(solution)/shard_map/ppermute | solution.py:314
  75.7 3.3 %collective-permute-start.2 = (bf16[5,12,16,128]{3,2,1,0:T(8,128)(2,1)S(1)}, bf16[5,12,16,128]{3,2,1,0:T(8,128)(2,1)S(1)}, u32[]{:S(2)}, u32[]{:S(2)}) collective-permute-start(bf16[5,12,16,128]{3,2,1,0:T(8,128)(2,1)S(1)} %get-tuple-element.32), channel_id=1, source_target_pairs={{0,48},{16,0},{32,16},{48,32},{1,49},{17,1},{33,17},{49,33},{2,50}... | collective-permute-start | bytes 737288 | tf_op jit(solution)/shard_map/ppermute | solution.py:314
  79.0 5.6 %collective-permute-done.1 = bf16[5,12,16,128]{3,2,1,0:T(8,128)(2,1)S(1)} collective-permute-done((bf16[5,12,16,128]{3,2,1,0:T(8,128)(2,1)S(1)}, bf16[5,12,16,128]{3,2,1,0:T(8,128)(2,1)S(1)}, u32[]{:S(2)}, u32[]{:S(2)}) %collective-permute-start.1) | collective-permute-done | bytes 245792 | tf_op jit(solution)/shard_map/ppermute | solution.py:314
  86.2 3.4 %collective-permute-start.3 = (bf16[2,4,12,16,128]{4,3,2,1,0:T(8,128)(2,1)S(1)}, bf16[2,4,12,16,128]{4,3,2,1,0:T(8,128)(2,1)S(1)}, u32[]{:S(2)}, u32[]{:S(2)}) collective-permute-start(bf16[2,4,12,16,128]{4,3,2,1,0:T(8,128)(2,1)S(1)} %bitcast.13), channel_id=1, source_target_pairs={{0,1},{1,2},{2,3},{3,0},{4,5},{5,6},{6,7},{7,4},{8,9},{9,10},{10,1... | collective-permute-start | bytes 1179656 | tf_op jit(solution)/shard_map/ppermute | solution.py:314
  89.6 3.0 %collective-permute-start.4 = (bf16[2,4,12,16,128]{4,3,2,1,0:T(8,128)(2,1)S(1)}, bf16[2,4,12,16,128]{4,3,2,1,0:T(8,128)(2,1)S(1)}, u32[]{:S(2)}, u32[]{:S(2)}) collective-permute-start(bf16[2,4,12,16,128]{4,3,2,1,0:T(8,128)(2,1)S(1)} %bitcast.12), channel_id=1, source_target_pairs={{0,2},{1,3},{2,0},{3,1},{4,6},{5,7},{6,4},{7,5},{8,10},{9,11},{10,... | collective-permute-start | bytes 1179656 | tf_op jit(solution)/shard_map/ppermute | solution.py:314
  92.6 4.1 %collective-permute-start.5 = (bf16[2,4,12,16,128]{4,3,2,1,0:T(8,128)(2,1)S(1)}, bf16[2,4,12,16,128]{4,3,2,1,0:T(8,128)(2,1)S(1)}, u32[]{:S(2)}, u32[]{:S(2)}) collective-permute-start(bf16[2,4,12,16,128]{4,3,2,1,0:T(8,128)(2,1)S(1)} %bitcast.11), channel_id=1, source_target_pairs={{0,3},{1,0},{2,1},{3,2},{4,7},{5,4},{6,5},{7,6},{8,11},{9,8},{10,9... | collective-permute-start | bytes 1179656 | tf_op jit(solution)/shard_map/ppermute | solution.py:314
  96.7 3.4 %collective-permute-done.3.refs_1_ = bf16[2,4,12,16,128]{4,3,2,1,0:T(8,128)(2,1)S(1)} collective-permute-done((bf16[2,4,12,16,128]{4,3,2,1,0:T(8,128)(2,1)S(1)}, bf16[2,4,12,16,128]{4,3,2,1,0:T(8,128)(2,1)S(1)}, u32[]{:S(2)}, u32[]{:S(2)}) %collective-permute-start.3) | collective-permute-done | bytes 393248 | tf_op jit(solution)/shard_map/ppermute | solution.py:314
  100.2 4.9 %collective-permute-done.4.refs_2_ = bf16[2,4,12,16,128]{4,3,2,1,0:T(8,128)(2,1)S(1)} collective-permute-done((bf16[2,4,12,16,128]{4,3,2,1,0:T(8,128)(2,1)S(1)}, bf16[2,4,12,16,128]{4,3,2,1,0:T(8,128)(2,1)S(1)}, u32[]{:S(2)}, u32[]{:S(2)}) %collective-permute-start.4) | collective-permute-done | bytes 393248 | tf_op jit(solution)/shard_map/ppermute | solution.py:314
  105.1 6.0 %collective-permute-done.5.refs_3_ = bf16[2,4,12,16,128]{4,3,2,1,0:T(8,128)(2,1)S(1)} collective-permute-done((bf16[2,4,12,16,128]{4,3,2,1,0:T(8,128)(2,1)S(1)}, bf16[2,4,12,16,128]{4,3,2,1,0:T(8,128)(2,1)S(1)}, u32[]{:S(2)}, u32[]{:S(2)}) %collective-permute-start.5) | collective-permute-done | bytes 393248 | tf_op jit(solution)/shard_map/ppermute | solution.py:314
  116.9 3.8 %shard_map.58.first_hbm = bf16[16,4,16,128]{3,2,1,0:T(8,128)(2,1)S(1)} custom-call(bf16[2,4,12,16,128]{4,3,2,1,0:T(8,128)(2,1)S(1)} %bitcast.10, bf16[2,4,12,16,128]{4,3,2,1,0:T(8,128)(2,1)S(1)} %collective-permute-done.3.refs_1_, bf16[2,4,12,16,128]{4,3,2,1,0:T(8,128)(2,1)S(1)} %collective-permute-done.4.refs_2_, ...), custom_call_target="tpu_custom_call" | custom-call | flops 1342177280 | bytes 3407872 | tf_op jit(solution)/shard_map/pallas_call | solution.py:298
  122.3 18.3 %all-to-all-done.1 = bf16[16,4,3,2,16,128]{5,4,3,2,1,0:T(8,128)(2,1)S(1)} async-done(((bf16[16,4,3,2,16,128]{5,4,3,2,1,0:T(8,128)(2,1)}), bf16[16,4,3,2,16,128]{5,4,3,2,1,0:T(8,128)(2,1)S(1)}, u32[]{:S(2)}, u32[]{:S(2)}) %all-to-all-start.1) | async-done | bytes 1572896 | tf_op jit(solution)/shard_map/all_to_all | solution.py:339
  141.9 7.5 %all-to-all-start.2 = ((bf16[16,4,6,16,128]{4,3,2,1,0:T(8,128)(2,1)}), bf16[16,4,6,16,128]{4,3,2,1,0:T(8,128)(2,1)}, u32[]{:S(2)}, u32[]{:S(2)}) async-start(bf16[16,4,6,16,128]{4,3,2,1,0:T(8,128)(2,1)} %copy-done), calls=%async_computation.2 | async-start | bytes 3145728 | tf_op jit(solution)/shard_map/all_to_all | solution.py:365
  153.6 4.1 %shard_map.62 = (bf16[2,16,2,16,128]{4,3,2,1,0:T(8,128)(2,1)S(1)}, bf16[2,16,2,16,128]{4,3,2,1,0:T(8,128)(2,1)S(1)}) custom-call(bf16[16,4,6,16,128]{4,3,2,1,0:T(8,128)(2,1)S(1)} %bitcast.9, bf16[4,2,4,6,16,128]{5,4,3,2,1,0:T(8,128)(2,1)S(1)} %collective-permute-done.9.got_ref), custom_call_target="tpu_custom_call" | custom-call | bytes 2883584 | tf_op jit(solution)/shard_map/pallas_call | solution.py:298
  158.4 6.4 %collective-permute-done.8.recv_ref = bf16[2,4,12,16,128]{4,3,2,1,0:T(8,128)(2,1)S(1)} collective-permute-done((bf16[2,4,12,16,128]{4,3,2,1,0:T(8,128)(2,1)S(1)}, bf16[2,4,12,16,128]{4,3,2,1,0:T(8,128)(2,1)S(1)}, u32[]{:S(2)}, u32[]{:S(2)}) %collective-permute-start.8) | collective-permute-done | bytes 393248 | tf_op jit(solution)/shard_map/ppermute | solution.py:310
  164.7 2.7 %shard_map.63 = (bf16[2,16,16,128]{3,2,1,0:T(8,128)(2,1)S(1)}, bf16[2,16,16,128]{3,2,1,0:T(8,128)(2,1)}) custom-call(bf16[16,13,16,128]{3,2,1,0:T(8,128)(2,1)S(1)} %all-to-all-done.in_ref.first_ref, bf16[4,2,12,16,128]{4,3,2,1,0:T(8,128)(2,1)S(1)} %collective-permute-done.7.got_ref, bf16[2,4,12,16,128]{4,3,2,1,0:T(8,128)(2,1)S(1)} %collective-permute-done.8.recv_ref), custom_call_target="tpu_custom_call" | custom-call | bytes 1900544 | tf_op jit(solution)/shard_map/pallas_call | solution.py:298
  167.5 2.7 %all-to-all-done.2.x_hbm = bf16[16,4,6,16,128]{4,3,2,1,0:T(8,128)(2,1)} async-done(((bf16[16,4,6,16,128]{4,3,2,1,0:T(8,128)(2,1)}), bf16[16,4,6,16,128]{4,3,2,1,0:T(8,128)(2,1)}, u32[]{:S(2)}, u32[]{:S(2)}) %all-to-all-start.2) | async-done | bytes 1572896 | tf_op jit(solution)/shard_map/all_to_all | solution.py:365
  170.2 8.5 %shard_map.64 = bf16[16,4,3,16,128]{4,3,2,1,0:T(8,128)(2,1)} custom-call(bf16[16,4,6,16,128]{4,3,2,1,0:T(8,128)(2,1)} %all-to-all-done.2.x_hbm, bf16[4,4,12,16,128]{4,3,2,1,0:T(8,128)(2,1)} %copy-done.5, bf16[4,4,12,16,128]{4,3,2,1,0:T(8,128)(2,1)} %copy-done.6, bf16[16,4,16,128]{3,2,1,0:T(8,128)(2,1)} %copy-done.9), custom_call_target="tpu_custom_call" | custom-call | flops 2684354560 | bytes 4194304 | tf_op jit(solution)/shard_map/pallas_call | solution.py:298
  178.7 5.8 %all-to-all-start.3 = ((bf16[16,4,3,16,128]{4,3,2,1,0:T(8,128)(2,1)}), bf16[16,4,3,16,128]{4,3,2,1,0:T(8,128)(2,1)S(1)}, u32[]{:S(2)}, u32[]{:S(2)}) async-start(bf16[16,4,3,16,128]{4,3,2,1,0:T(8,128)(2,1)} %shard_map.64), calls=%async_computation.3 | async-start | bytes 1572864 | tf_op jit(solution)/shard_map/all_to_all | solution.py:398
  188.5 3.2 %collective-permute-done.11.back_ref = bf16[2,16,16,128]{3,2,1,0:T(8,128)(2,1)S(1)} collective-permute-done((bf16[2,16,16,128]{3,2,1,0:T(8,128)(2,1)}, bf16[2,16,16,128]{3,2,1,0:T(8,128)(2,1)S(1)}, u32[]{:S(2)}, u32[]{:S(2)}) %collective-permute-start.11) | collective-permute-done | bytes 131104 | tf_op jit(solution)/shard_map/ppermute | solution.py:310
  197.5 48.1 %all_to_all.25.in_ref = bf16[16,4,3,16,128]{4,3,2,1,0:T(8,128)(2,1)S(1)} all-to-all(bf16[16,4,3,16,128]{4,3,2,1,0:T(8,128)(2,1)S(1)} %shard_map.65), channel_id=1, replica_groups=mesh['zl1'=2,'zl0'=2,'core'=2,'y'=4,'zh1'=2,'zh0'=2,'x'=4] {'zh1','zl1',..., dimensions={0} | all-to-all | bytes 1572864 | tf_op jit(solution)/shard_map/all_to_all | solution.py:403
  (59 shorter events, 30.0 us)
Async XLA Ops:
  0.0 17.8 %copy-start.4 = (bf16[8,16,3072]{2,1,0:T(8,128)(2,1)S(1)}, bf16[8,16,3072]{2,1,0:T(8,128)(2,1)}, u32[]{:S(2)}) copy-start(bf16[8,16,3072]{2,1,0:T(8,128)(2,1)} %v_ref.3) | copy-start | bytes 2359300
  2.4 15.4 %copy-start.2 = (bf16[8,16,3072]{2,1,0:T(8,128)(2,1)S(1)}, bf16[8,16,3072]{2,1,0:T(8,128)(2,1)}, u32[]{:S(2)}) copy-start(bf16[8,16,3072]{2,1,0:T(8,128)(2,1)} %q_ref.3) | copy-start | bytes 2359300
  2.4 15.4 %copy-start.3 = (bf16[8,16,3072]{2,1,0:T(8,128)(2,1)S(1)}, bf16[8,16,3072]{2,1,0:T(8,128)(2,1)}, u32[]{:S(2)}) copy-start(bf16[8,16,3072]{2,1,0:T(8,128)(2,1)} %k_ref.3) | copy-start | bytes 2359300
  2.4 58.8 %all-to-all-start = ((bf16[16,13,16,128]{3,2,1,0:T(8,128)(2,1)}), bf16[16,13,16,128]{3,2,1,0:T(8,128)(2,1)S(1)}, u32[]{:S(2)}, u32[]{:S(2)}) async-start(bf16[16,13,16,128]{3,2,1,0:T(8,128)(2,1)} %shard_map.55), calls=%async_computation | async-start | bytes 1703936 | tf_op jit(solution)/shard_map/all_to_all | solution.py:336
  18.1 1.2 copy-start.1
  61.2 79.4 %all-to-all-start.1 = ((bf16[16,4,3,2,16,128]{5,4,3,2,1,0:T(8,128)(2,1)}), bf16[16,4,3,2,16,128]{5,4,3,2,1,0:T(8,128)(2,1)S(1)}, u32[]{:S(2)}, u32[]{:S(2)}) async-start(bf16[16,4,3,2,16,128]{5,4,3,2,1,0:T(8,128)(2,1)} %copy-done.1), calls=%async_computation.1 | async-start | bytes 3145728 | tf_op jit(solution)/shard_map/all_to_all | solution.py:339
  67.4 11.6 %collective-permute-start = (bf16[5,12,16,128]{3,2,1,0:T(8,128)(2,1)S(1)}, bf16[5,12,16,128]{3,2,1,0:T(8,128)(2,1)S(1)}, u32[]{:S(2)}, u32[]{:S(2)}) collective-permute-start(bf16[5,12,16,128]{3,2,1,0:T(8,128)(2,1)S(1)} %get-tuple-element.30), channel_id=1, source_target_pairs={{0,16},{16,32},{32,48},{48,0},{1,17},{17,33},{33,49},{49,1},{2,18}... | collective-permute-start | bytes 737288 | tf_op jit(solution)/shard_map/ppermute | solution.py:314
  70.9 13.7 %collective-permute-start.1 = (bf16[5,12,16,128]{3,2,1,0:T(8,128)(2,1)S(1)}, bf16[5,12,16,128]{3,2,1,0:T(8,128)(2,1)S(1)}, u32[]{:S(2)}, u32[]{:S(2)}) collective-permute-start(bf16[5,12,16,128]{3,2,1,0:T(8,128)(2,1)S(1)} %get-tuple-element.31), channel_id=1, source_target_pairs={{0,32},{16,48},{32,0},{48,16},{1,33},{17,49},{33,1},{49,17},{2,34}... | collective-permute-start | bytes 737288 | tf_op jit(solution)/shard_map/ppermute | solution.py:314
  75.7 10.2 %collective-permute-start.2 = (bf16[5,12,16,128]{3,2,1,0:T(8,128)(2,1)S(1)}, bf16[5,12,16,128]{3,2,1,0:T(8,128)(2,1)S(1)}, u32[]{:S(2)}, u32[]{:S(2)}) collective-permute-start(bf16[5,12,16,128]{3,2,1,0:T(8,128)(2,1)S(1)} %get-tuple-element.32), channel_id=1, source_target_pairs={{0,48},{16,0},{32,16},{48,32},{1,49},{17,1},{33,17},{49,33},{2,50}... | collective-permute-start | bytes 737288 | tf_op jit(solution)/shard_map/ppermute | solution.py:314
  86.2 13.9 %collective-permute-start.3 = (bf16[2,4,12,16,128]{4,3,2,1,0:T(8,128)(2,1)S(1)}, bf16[2,4,12,16,128]{4,3,2,1,0:T(8,128)(2,1)S(1)}, u32[]{:S(2)}, u32[]{:S(2)}) collective-permute-start(bf16[2,4,12,16,128]{4,3,2,1,0:T(8,128)(2,1)S(1)} %bitcast.13), channel_id=1, source_target_pairs={{0,1},{1,2},{2,3},{3,0},{4,5},{5,6},{6,7},{7,4},{8,9},{9,10},{10,1... | collective-permute-start | bytes 1179656 | tf_op jit(solution)/shard_map/ppermute | solution.py:314
  89.6 15.5 %collective-permute-start.4 = (bf16[2,4,12,16,128]{4,3,2,1,0:T(8,128)(2,1)S(1)}, bf16[2,4,12,16,128]{4,3,2,1,0:T(8,128)(2,1)S(1)}, u32[]{:S(2)}, u32[]{:S(2)}) collective-permute-start(bf16[2,4,12,16,128]{4,3,2,1,0:T(8,128)(2,1)S(1)} %bitcast.12), channel_id=1, source_target_pairs={{0,2},{1,3},{2,0},{3,1},{4,6},{5,7},{6,4},{7,5},{8,10},{9,11},{10,... | collective-permute-start | bytes 1179656 | tf_op jit(solution)/shard_map/ppermute | solution.py:314
  92.6 18.4 %collective-permute-start.5 = (bf16[2,4,12,16,128]{4,3,2,1,0:T(8,128)(2,1)S(1)}, bf16[2,4,12,16,128]{4,3,2,1,0:T(8,128)(2,1)S(1)}, u32[]{:S(2)}, u32[]{:S(2)}) collective-permute-start(bf16[2,4,12,16,128]{4,3,2,1,0:T(8,128)(2,1)S(1)} %bitcast.11), channel_id=1, source_target_pairs={{0,3},{1,0},{2,1},{3,2},{4,7},{5,4},{6,5},{7,6},{8,11},{9,8},{10,9... | collective-permute-start | bytes 1179656 | tf_op jit(solution)/shard_map/ppermute | solution.py:314
  111.2 5.7 %copy-start.5 = (bf16[4,4,12,16,128]{4,3,2,1,0:T(8,128)(2,1)}, bf16[4,4,12,16,128]{4,3,2,1,0:T(8,128)(2,1)S(1)}, u32[]{:S(2)}) copy-start(bf16[4,4,12,16,128]{4,3,2,1,0:T(8,128)(2,1)S(1)} %pad_maximum_fusion.refs_4_.mine_hbm) | copy-start | bytes 2359300
  111.2 5.7 %collective-permute-start.6 = (bf16[4,4,12,16,128]{4,3,2,1,0:T(8,128)(2,1)S(1)}, bf16[4,4,12,16,128]{4,3,2,1,0:T(8,128)(2,1)S(1)}, u32[]{:S(2)}, u32[]{:S(2)}) collective-permute-start(bf16[4,4,12,16,128]{4,3,2,1,0:T(8,128)(2,1)S(1)} %pad_maximum_fusion.refs_4_.mine_hbm), channel_id=1, source_target_pairs={{0,64},{64,0},{1,65},{65,1},{2,66},{66,2},{3,67},{67,3},{4,68},{68... | collective-permute-start | bytes 2359304 | tf_op jit(solution)/shard_map/ppermute | solution.py:352
  113.1 3.7 %collective-permute-start.7 = (bf16[4,2,12,16,128]{4,3,2,1,0:T(8,128)(2,1)S(1)}, bf16[4,2,12,16,128]{4,3,2,1,0:T(8,128)(2,1)S(1)}, u32[]{:S(2)}, u32[]{:S(2)}) collective-permute-start(bf16[4,2,12,16,128]{4,3,2,1,0:T(8,128)(2,1)S(1)} %get-tuple-element.33), channel_id=1, source_target_pairs={{0,64},{64,0},{128,192},{192,128},{1,65},{65,1},{129,193},{193,129... | collective-permute-start | bytes 1179656 | tf_op jit(solution)/shard_map/ppermute | solution.py:310
  140.7 1.2 copy-start
  141.9 28.3 %all-to-all-start.2 = ((bf16[16,4,6,16,128]{4,3,2,1,0:T(8,128)(2,1)}), bf16[16,4,6,16,128]{4,3,2,1,0:T(8,128)(2,1)}, u32[]{:S(2)}, u32[]{:S(2)}) async-start(bf16[16,4,6,16,128]{4,3,2,1,0:T(8,128)(2,1)} %copy-done), calls=%async_computation.2 | async-start | bytes 3145728 | tf_op jit(solution)/shard_map/all_to_all | solution.py:365
  149.4 4.2 %collective-permute-start.9 = (bf16[4,2,4,6,16,128]{5,4,3,2,1,0:T(8,128)(2,1)S(1)}, bf16[4,2,4,6,16,128]{5,4,3,2,1,0:T(8,128)(2,1)S(1)}, u32[]{:S(2)}, u32[]{:S(2)}) collective-permute-start(bf16[4,2,4,6,16,128]{5,4,3,2,1,0:T(8,128)(2,1)S(1)} %shard_map.61), channel_id=1, source_target_pairs={{0,64},{64,0},{128,192},{192,128},{1,65},{65,1},{129,193},{193,129... | collective-permute-start | bytes 2359304 | tf_op jit(solution)/shard_map/ppermute | solution.py:310
  151.3 13.4 %collective-permute-start.8 = (bf16[2,4,12,16,128]{4,3,2,1,0:T(8,128)(2,1)S(1)}, bf16[2,4,12,16,128]{4,3,2,1,0:T(8,128)(2,1)S(1)}, u32[]{:S(2)}, u32[]{:S(2)}) collective-permute-start(bf16[2,4,12,16,128]{4,3,2,1,0:T(8,128)(2,1)S(1)} %shard_map.59), channel_id=1, source_target_pairs={{0,128},{64,192},{128,0},{192,64},{1,129},{65,193},{129,1},{193,65... | collective-permute-start | bytes 1179656 | tf_op jit(solution)/shard_map/ppermute | solution.py:310
  178.7 7.8 %copy-start.8 = (bf16[2,16,2,16,128]{4,3,2,1,0:T(8,128)(2,1)S(1)}, bf16[2,16,2,16,128]{4,3,2,1,0:T(8,128)(2,1)}, u32[]{:S(2)}) copy-start(bf16[2,16,2,16,128]{4,3,2,1,0:T(8,128)(2,1)} %copy-done.7) | copy-start | bytes 786436
  178.7 18.6 %all-to-all-start.3 = ((bf16[16,4,3,16,128]{4,3,2,1,0:T(8,128)(2,1)}), bf16[16,4,3,16,128]{4,3,2,1,0:T(8,128)(2,1)S(1)}, u32[]{:S(2)}, u32[]{:S(2)}) async-start(bf16[16,4,3,16,128]{4,3,2,1,0:T(8,128)(2,1)} %shard_map.64), calls=%async_computation.3 | async-start | bytes 1572864 | tf_op jit(solution)/shard_map/all_to_all | solution.py:398
  184.6 7.1 %collective-permute-start.11 = (bf16[2,16,16,128]{3,2,1,0:T(8,128)(2,1)}, bf16[2,16,16,128]{3,2,1,0:T(8,128)(2,1)S(1)}, u32[]{:S(2)}, u32[]{:S(2)}) collective-permute-start(bf16[2,16,16,128]{3,2,1,0:T(8,128)(2,1)} %get-tuple-element.48), channel_id=1, source_target_pairs={{0,128},{64,192},{128,0},{192,64},{1,129},{65,193},{129,1},{193,65... | collective-permute-start | bytes 393224 | tf_op jit(solution)/shard_map/ppermute | solution.py:310
  186.5 8.4 %collective-permute-start.10 = (bf16[2,16,2,16,128]{4,3,2,1,0:T(8,128)(2,1)S(1)}, bf16[2,16,2,16,128]{4,3,2,1,0:T(8,128)(2,1)S(1)}, u32[]{:S(2)}, u32[]{:S(2)}) collective-permute-start(bf16[2,16,2,16,128]{4,3,2,1,0:T(8,128)(2,1)S(1)} %copy-done.8), channel_id=1, source_target_pairs={{0,64},{64,0},{128,192},{192,128},{1,65},{65,1},{129,193},{193,129... | collective-permute-start | bytes 786440 | tf_op jit(solution)/shard_map/ppermute | solution.py:310
  191.7 3.2 %collective-permute-start.12 = (bf16[2,16,16,128]{3,2,1,0:T(8,128)(2,1)S(1)}, bf16[2,16,16,128]{3,2,1,0:T(8,128)(2,1)S(1)}, u32[]{:S(2)}, u32[]{:S(2)}) collective-permute-start(bf16[2,16,16,128]{3,2,1,0:T(8,128)(2,1)S(1)} %pad_maximum_fusion.1), channel_id=1, source_target_pairs={{0,64},{64,0},{128,192},{192,128},{1,65},{65,1},{129,193},{193,129... | collective-permute-start | bytes 393224 | tf_op jit(solution)/shard_map/ppermute | solution.py:310
  (3 other events, 2.3 us)

commit v5 on v4

--- a/solution.py
+++ b/solution.py
@@ -368,13 +368,12 @@
     mine, other = call(
         temporal_own_kernel, [(2, 16, 2, 16, HD)] * 2, second, swap(other, 1), scratch=bias
     )
-    recv, mine, other = lax.optimization_barrier((swap(send, 2), mine, other))
+    recv, mine, other = lax.optimization_barrier((swap(send, 2), mine, swap(other, 1)))
     keep, send = call(
         temporal_middle_kernel, [(2, 16, 16, HD)] * 2, first, got, recv, scratch=bias
     )
-    by_frame, other, send = lax.optimization_barrier((by_frame, other, send))
+    by_frame, send = lax.optimization_barrier((by_frame, send))
     back = swap(send, 2)
-    other = swap(other, 1)
     middle_other = swap(jnp.stack((keep[1], back[1])), 1)
 
     spatial = call(

time: 248 us -> 248 us (level)
    unnamed x24 -> x28, local copies, waits for them, and re-layouts: 4.73 us -> 5.39 us
  transfers between devices with their start and end apart: 17 -> 17, of which waited for: 14 -> 14; matrix products, arithmetic and copies ran while one was open for 0% -> 0% of each run, Pallas kernels for 5% -> 4%
where the time goes in v5:
time: 248 us; the launch traced here: 247 us
  waiting for transfers between devices  98.6 us (40%)
  starting transfers between devices  71 us (29%)
  blocking collectives  48.1 us (19%)
  Pallas kernels  22.8 us (9%)
  local copies, waits for them, and re-layouts  5.66 us (2%)
    all_to_all x1, blocking collectives, local(): lax.all_to_all(attended, Z, split_axis=0, concat_axis=0, tiled=True)  48.1 us
    all_to_all x1, waiting for transfers between devices, local(): first = lax.all_to_all(first, Z, split_axis=0, concat_axis=0, tiled=True)  41.9 us
    pallas_call x12, Pallas kernels, call(): pl.pallas_call(kernel, out_shape=shapes if several else shapes[0], in_spe...  22.8 us
    ppermute x6, starting transfers between devices, shift(): return lax.ppermute(tensor, axis, [(i, (i + step) % 4) for i in range(4)])  22 us
    ppermute x6, waiting for transfers between devices, shift(): return lax.ppermute(tensor, axis, [(i, (i + step) % 4) for i in range(4)])  21.1 us
    all_to_all x1, waiting for transfers between devices, local(): second = lax.all_to_all(second, Z, split_axis=0, concat_axis=0, tiled=True)  18.3 us
    all_to_all x1, starting transfers between devices, local(): first = lax.all_to_all(first, Z, split_axis=0, concat_axis=0, tiled=True)  15.3 us
    ppermute x6, waiting for transfers between devices, swap(): lax.ppermute(tensor, ('zl0', 'core'), [(i, i ^ mask) for i in range(4)])  12.7 us
  transfers between devices with their start and end apart: 17, of which 14 were waited for; matrix products, arithmetic and copies ran while one was open for 0% of the time, Pallas kernels for 4%

profile of v5, /device:TPU:2, one launch (start us, length us, event | category | flops | bytes accessed | tf_op | source)
XLA Modules:
  0.0 246.7 jit_solution(9038827172504215828)
XLA Ops:
  0.0 2.4 shard_map.55
  2.4 15.3 %all-to-all-start = ((bf16[16,13,16,128]{3,2,1,0:T(8,128)(2,1)}), bf16[16,13,16,128]{3,2,1,0:T(8,128)(2,1)S(1)}, u32[]{:S(2)}, u32[]{:S(2)}) async-start(bf16[16,13,16,128]{3,2,1,0:T(8,128)(2,1)} %shard_map.55), calls=%async_computation | async-start | bytes 1703936 | tf_op jit(solution)/shard_map/all_to_all | solution.py:336
  19.3 41.9 %all-to-all-done.in_ref.first_ref = bf16[16,13,16,128]{3,2,1,0:T(8,128)(2,1)S(1)} async-done(((bf16[16,13,16,128]{3,2,1,0:T(8,128)(2,1)}), bf16[16,13,16,128]{3,2,1,0:T(8,128)(2,1)S(1)}, u32[]{:S(2)}, u32[]{:S(2)}) %all-to-all-start) | async-done | bytes 852000 | tf_op jit(solution)/shard_map/all_to_all | solution.py:336
  61.2 6.0 %all-to-all-start.1 = ((bf16[16,4,3,2,16,128]{5,4,3,2,1,0:T(8,128)(2,1)}), bf16[16,4,3,2,16,128]{5,4,3,2,1,0:T(8,128)(2,1)S(1)}, u32[]{:S(2)}, u32[]{:S(2)}) async-start(bf16[16,4,3,2,16,128]{5,4,3,2,1,0:T(8,128)(2,1)} %copy-done.1), calls=%async_computation.1 | async-start | bytes 3145728 | tf_op jit(solution)/shard_map/all_to_all | solution.py:339
  67.4 3.5 %collective-permute-start = (bf16[5,12,16,128]{3,2,1,0:T(8,128)(2,1)S(1)}, bf16[5,12,16,128]{3,2,1,0:T(8,128)(2,1)S(1)}, u32[]{:S(2)}, u32[]{:S(2)}) collective-permute-start(bf16[5,12,16,128]{3,2,1,0:T(8,128)(2,1)S(1)} %get-tuple-element.29), channel_id=1, source_target_pairs={{0,16},{16,32},{32,48},{48,0},{1,17},{17,33},{33,49},{49,1},{2,18}... | collective-permute-start | bytes 737288 | tf_op jit(solution)/shard_map/ppermute | solution.py:314
  70.9 4.8 %collective-permute-start.1 = (bf16[5,12,16,128]{3,2,1,0:T(8,128)(2,1)S(1)}, bf16[5,12,16,128]{3,2,1,0:T(8,128)(2,1)S(1)}, u32[]{:S(2)}, u32[]{:S(2)}) collective-permute-start(bf16[5,12,16,128]{3,2,1,0:T(8,128)(2,1)S(1)} %get-tuple-element.30), channel_id=1, source_target_pairs={{0,32},{16,48},{32,0},{48,16},{1,33},{17,49},{33,1},{49,17},{2,34}... | collective-permute-start | bytes 737288 | tf_op jit(solution)/shard_map/ppermute | solution.py:314
  75.7 3.3 %collective-permute-start.2 = (bf16[5,12,16,128]{3,2,1,0:T(8,128)(2,1)S(1)}, bf16[5,12,16,128]{3,2,1,0:T(8,128)(2,1)S(1)}, u32[]{:S(2)}, u32[]{:S(2)}) collective-permute-start(bf16[5,12,16,128]{3,2,1,0:T(8,128)(2,1)S(1)} %get-tuple-element.31), channel_id=1, source_target_pairs={{0,48},{16,0},{32,16},{48,32},{1,49},{17,1},{33,17},{49,33},{2,50}... | collective-permute-start | bytes 737288 | tf_op jit(solution)/shard_map/ppermute | solution.py:314
  79.1 5.6 %collective-permute-done.1 = bf16[5,12,16,128]{3,2,1,0:T(8,128)(2,1)S(1)} collective-permute-done((bf16[5,12,16,128]{3,2,1,0:T(8,128)(2,1)S(1)}, bf16[5,12,16,128]{3,2,1,0:T(8,128)(2,1)S(1)}, u32[]{:S(2)}, u32[]{:S(2)}) %collective-permute-start.1) | collective-permute-done | bytes 245792 | tf_op jit(solution)/shard_map/ppermute | solution.py:314
  86.2 3.4 %collective-permute-start.3 = (bf16[2,4,12,16,128]{4,3,2,1,0:T(8,128)(2,1)S(1)}, bf16[2,4,12,16,128]{4,3,2,1,0:T(8,128)(2,1)S(1)}, u32[]{:S(2)}, u32[]{:S(2)}) collective-permute-start(bf16[2,4,12,16,128]{4,3,2,1,0:T(8,128)(2,1)S(1)} %bitcast.13), channel_id=1, source_target_pairs={{0,1},{1,2},{2,3},{3,0},{4,5},{5,6},{6,7},{7,4},{8,9},{9,10},{10,1... | collective-permute-start | bytes 1179656 | tf_op jit(solution)/shard_map/ppermute | solution.py:314
  89.6 3.0 %collective-permute-start.4 = (bf16[2,4,12,16,128]{4,3,2,1,0:T(8,128)(2,1)S(1)}, bf16[2,4,12,16,128]{4,3,2,1,0:T(8,128)(2,1)S(1)}, u32[]{:S(2)}, u32[]{:S(2)}) collective-permute-start(bf16[2,4,12,16,128]{4,3,2,1,0:T(8,128)(2,1)S(1)} %bitcast.12), channel_id=1, source_target_pairs={{0,2},{1,3},{2,0},{3,1},{4,6},{5,7},{6,4},{7,5},{8,10},{9,11},{10,... | collective-permute-start | bytes 1179656 | tf_op jit(solution)/shard_map/ppermute | solution.py:314
  92.6 4.1 %collective-permute-start.5 = (bf16[2,4,12,16,128]{4,3,2,1,0:T(8,128)(2,1)S(1)}, bf16[2,4,12,16,128]{4,3,2,1,0:T(8,128)(2,1)S(1)}, u32[]{:S(2)}, u32[]{:S(2)}) collective-permute-start(bf16[2,4,12,16,128]{4,3,2,1,0:T(8,128)(2,1)S(1)} %bitcast.11), channel_id=1, source_target_pairs={{0,3},{1,0},{2,1},{3,2},{4,7},{5,4},{6,5},{7,6},{8,11},{9,8},{10,9... | collective-permute-start | bytes 1179656 | tf_op jit(solution)/shard_map/ppermute | solution.py:314
  96.7 3.4 %collective-permute-done.3.refs_1_ = bf16[2,4,12,16,128]{4,3,2,1,0:T(8,128)(2,1)S(1)} collective-permute-done((bf16[2,4,12,16,128]{4,3,2,1,0:T(8,128)(2,1)S(1)}, bf16[2,4,12,16,128]{4,3,2,1,0:T(8,128)(2,1)S(1)}, u32[]{:S(2)}, u32[]{:S(2)}) %collective-permute-start.3) | collective-permute-done | bytes 393248 | tf_op jit(solution)/shard_map/ppermute | solution.py:314
  100.2 4.9 %collective-permute-done.4.refs_2_ = bf16[2,4,12,16,128]{4,3,2,1,0:T(8,128)(2,1)S(1)} collective-permute-done((bf16[2,4,12,16,128]{4,3,2,1,0:T(8,128)(2,1)S(1)}, bf16[2,4,12,16,128]{4,3,2,1,0:T(8,128)(2,1)S(1)}, u32[]{:S(2)}, u32[]{:S(2)}) %collective-permute-start.4) | collective-permute-done | bytes 393248 | tf_op jit(solution)/shard_map/ppermute | solution.py:314
  105.1 6.0 %collective-permute-done.5.refs_3_ = bf16[2,4,12,16,128]{4,3,2,1,0:T(8,128)(2,1)S(1)} collective-permute-done((bf16[2,4,12,16,128]{4,3,2,1,0:T(8,128)(2,1)S(1)}, bf16[2,4,12,16,128]{4,3,2,1,0:T(8,128)(2,1)S(1)}, u32[]{:S(2)}, u32[]{:S(2)}) %collective-permute-start.5) | collective-permute-done | bytes 393248 | tf_op jit(solution)/shard_map/ppermute | solution.py:314
  116.9 3.8 %shard_map.58.first_hbm = bf16[16,4,16,128]{3,2,1,0:T(8,128)(2,1)S(1)} custom-call(bf16[2,4,12,16,128]{4,3,2,1,0:T(8,128)(2,1)S(1)} %bitcast.10, bf16[2,4,12,16,128]{4,3,2,1,0:T(8,128)(2,1)S(1)} %collective-permute-done.3.refs_1_, bf16[2,4,12,16,128]{4,3,2,1,0:T(8,128)(2,1)S(1)} %collective-permute-done.4.refs_2_, ...), custom_call_target="tpu_custom_call" | custom-call | flops 1342177280 | bytes 3407872 | tf_op jit(solution)/shard_map/pallas_call | solution.py:298
  122.3 18.3 %all-to-all-done.1 = bf16[16,4,3,2,16,128]{5,4,3,2,1,0:T(8,128)(2,1)S(1)} async-done(((bf16[16,4,3,2,16,128]{5,4,3,2,1,0:T(8,128)(2,1)}), bf16[16,4,3,2,16,128]{5,4,3,2,1,0:T(8,128)(2,1)S(1)}, u32[]{:S(2)}, u32[]{:S(2)}) %all-to-all-start.1) | async-done | bytes 1572896 | tf_op jit(solution)/shard_map/all_to_all | solution.py:339
  141.9 7.5 %all-to-all-start.2 = ((bf16[16,4,6,16,128]{4,3,2,1,0:T(8,128)(2,1)}), bf16[16,4,6,16,128]{4,3,2,1,0:T(8,128)(2,1)}, u32[]{:S(2)}, u32[]{:S(2)}) async-start(bf16[16,4,6,16,128]{4,3,2,1,0:T(8,128)(2,1)} %copy-done), calls=%async_computation.2 | async-start | bytes 3145728 | tf_op jit(solution)/shard_map/all_to_all | solution.py:365
  153.6 4.1 %shard_map.62 = (bf16[2,16,2,16,128]{4,3,2,1,0:T(8,128)(2,1)S(1)}, bf16[2,16,2,16,128]{4,3,2,1,0:T(8,128)(2,1)S(1)}) custom-call(bf16[16,4,6,16,128]{4,3,2,1,0:T(8,128)(2,1)S(1)} %bitcast.9, bf16[4,2,4,6,16,128]{5,4,3,2,1,0:T(8,128)(2,1)S(1)} %collective-permute-done.9.got_ref), custom_call_target="tpu_custom_call" | custom-call | bytes 2883584 | tf_op jit(solution)/shard_map/pallas_call | solution.py:298
  160.0 4.8 %collective-permute-done.8.recv_ref = bf16[2,4,12,16,128]{4,3,2,1,0:T(8,128)(2,1)S(1)} collective-permute-done((bf16[2,4,12,16,128]{4,3,2,1,0:T(8,128)(2,1)S(1)}, bf16[2,4,12,16,128]{4,3,2,1,0:T(8,128)(2,1)S(1)}, u32[]{:S(2)}, u32[]{:S(2)}) %collective-permute-start.8) | collective-permute-done | bytes 393248 | tf_op jit(solution)/shard_map/ppermute | solution.py:310
  170.2 8.6 %shard_map.64 = bf16[16,4,3,16,128]{4,3,2,1,0:T(8,128)(2,1)} custom-call(bf16[16,4,6,16,128]{4,3,2,1,0:T(8,128)(2,1)} %all-to-all-done.2.x_hbm, bf16[4,4,12,16,128]{4,3,2,1,0:T(8,128)(2,1)} %copy-done.5, bf16[4,4,12,16,128]{4,3,2,1,0:T(8,128)(2,1)} %copy-done.8, bf16[16,4,16,128]{3,2,1,0:T(8,128)(2,1)} %copy-done.11), custom_call_target="tpu_custom_call" | custom-call | flops 2684354560 | bytes 4194304 | tf_op jit(solution)/shard_map/pallas_call | solution.py:298
  178.8 5.8 %all-to-all-start.3 = ((bf16[16,4,3,16,128]{4,3,2,1,0:T(8,128)(2,1)}), bf16[16,4,3,16,128]{4,3,2,1,0:T(8,128)(2,1)S(1)}, u32[]{:S(2)}, u32[]{:S(2)}) async-start(bf16[16,4,3,16,128]{4,3,2,1,0:T(8,128)(2,1)} %shard_map.64), calls=%async_computation.3 | async-start | bytes 1572864 | tf_op jit(solution)/shard_map/all_to_all | solution.py:397
  186.6 4.9 %collective-permute-done.11.back_ref = bf16[2,16,16,128]{3,2,1,0:T(8,128)(2,1)S(1)} collective-permute-done((bf16[2,16,16,128]{3,2,1,0:T(8,128)(2,1)S(1)}, bf16[2,16,16,128]{3,2,1,0:T(8,128)(2,1)S(1)}, u32[]{:S(2)}, u32[]{:S(2)}) %collective-permute-start.11) | collective-permute-done | bytes 131104 | tf_op jit(solution)/shard_map/ppermute | solution.py:310
  194.8 2.6 %all-to-all-done.3.spatial_ref = bf16[16,4,3,16,128]{4,3,2,1,0:T(8,128)(2,1)S(1)} async-done(((bf16[16,4,3,16,128]{4,3,2,1,0:T(8,128)(2,1)}), bf16[16,4,3,16,128]{4,3,2,1,0:T(8,128)(2,1)S(1)}, u32[]{:S(2)}, u32[]{:S(2)}) %all-to-all-start.3) | async-done | bytes 786464 | tf_op jit(solution)/shard_map/all_to_all | solution.py:397
  197.6 48.1 %all_to_all.25.in_ref = bf16[16,4,3,16,128]{4,3,2,1,0:T(8,128)(2,1)S(1)} all-to-all(bf16[16,4,3,16,128]{4,3,2,1,0:T(8,128)(2,1)S(1)} %shard_map.65), channel_id=1, replica_groups=mesh['zl1'=2,'zl0'=2,'core'=2,'y'=4,'zh1'=2,'zh0'=2,'x'=4] {'zh1','zl1',..., dimensions={0} | all-to-all | bytes 1572864 | tf_op jit(solution)/shard_map/all_to_all | solution.py:402
  (63 shorter events, 30.3 us)
Async XLA Ops:
  0.0 17.8 %copy-start.4 = (bf16[8,16,3072]{2,1,0:T(8,128)(2,1)S(1)}, bf16[8,16,3072]{2,1,0:T(8,128)(2,1)}, u32[]{:S(2)}) copy-start(bf16[8,16,3072]{2,1,0:T(8,128)(2,1)} %v_ref.3) | copy-start | bytes 2359300
  2.4 15.4 %copy-start.2 = (bf16[8,16,3072]{2,1,0:T(8,128)(2,1)S(1)}, bf16[8,16,3072]{2,1,0:T(8,128)(2,1)}, u32[]{:S(2)}) copy-start(bf16[8,16,3072]{2,1,0:T(8,128)(2,1)} %q_ref.3) | copy-start | bytes 2359300
  2.4 15.4 %copy-start.3 = (bf16[8,16,3072]{2,1,0:T(8,128)(2,1)S(1)}, bf16[8,16,3072]{2,1,0:T(8,128)(2,1)}, u32[]{:S(2)}) copy-start(bf16[8,16,3072]{2,1,0:T(8,128)(2,1)} %k_ref.3) | copy-start | bytes 2359300
  2.4 58.8 %all-to-all-start = ((bf16[16,13,16,128]{3,2,1,0:T(8,128)(2,1)}), bf16[16,13,16,128]{3,2,1,0:T(8,128)(2,1)S(1)}, u32[]{:S(2)}, u32[]{:S(2)}) async-start(bf16[16,13,16,128]{3,2,1,0:T(8,128)(2,1)} %shard_map.55), calls=%async_computation | async-start | bytes 1703936 | tf_op jit(solution)/shard_map/all_to_all | solution.py:336
  18.1 1.2 copy-start.1
  61.2 79.4 %all-to-all-start.1 = ((bf16[16,4,3,2,16,128]{5,4,3,2,1,0:T(8,128)(2,1)}), bf16[16,4,3,2,16,128]{5,4,3,2,1,0:T(8,128)(2,1)S(1)}, u32[]{:S(2)}, u32[]{:S(2)}) async-start(bf16[16,4,3,2,16,128]{5,4,3,2,1,0:T(8,128)(2,1)} %copy-done.1), calls=%async_computation.1 | async-start | bytes 3145728 | tf_op jit(solution)/shard_map/all_to_all | solution.py:339
  67.4 11.6 %collective-permute-start = (bf16[5,12,16,128]{3,2,1,0:T(8,128)(2,1)S(1)}, bf16[5,12,16,128]{3,2,1,0:T(8,128)(2,1)S(1)}, u32[]{:S(2)}, u32[]{:S(2)}) collective-permute-start(bf16[5,12,16,128]{3,2,1,0:T(8,128)(2,1)S(1)} %get-tuple-element.29), channel_id=1, source_target_pairs={{0,16},{16,32},{32,48},{48,0},{1,17},{17,33},{33,49},{49,1},{2,18}... | collective-permute-start | bytes 737288 | tf_op jit(solution)/shard_map/ppermute | solution.py:314
  70.9 13.7 %collective-permute-start.1 = (bf16[5,12,16,128]{3,2,1,0:T(8,128)(2,1)S(1)}, bf16[5,12,16,128]{3,2,1,0:T(8,128)(2,1)S(1)}, u32[]{:S(2)}, u32[]{:S(2)}) collective-permute-start(bf16[5,12,16,128]{3,2,1,0:T(8,128)(2,1)S(1)} %get-tuple-element.30), channel_id=1, source_target_pairs={{0,32},{16,48},{32,0},{48,16},{1,33},{17,49},{33,1},{49,17},{2,34}... | collective-permute-start | bytes 737288 | tf_op jit(solution)/shard_map/ppermute | solution.py:314
  75.7 10.2 %collective-permute-start.2 = (bf16[5,12,16,128]{3,2,1,0:T(8,128)(2,1)S(1)}, bf16[5,12,16,128]{3,2,1,0:T(8,128)(2,1)S(1)}, u32[]{:S(2)}, u32[]{:S(2)}) collective-permute-start(bf16[5,12,16,128]{3,2,1,0:T(8,128)(2,1)S(1)} %get-tuple-element.31), channel_id=1, source_target_pairs={{0,48},{16,0},{32,16},{48,32},{1,49},{17,1},{33,17},{49,33},{2,50}... | collective-permute-start | bytes 737288 | tf_op jit(solution)/shard_map/ppermute | solution.py:314
  86.2 13.9 %collective-permute-start.3 = (bf16[2,4,12,16,128]{4,3,2,1,0:T(8,128)(2,1)S(1)}, bf16[2,4,12,16,128]{4,3,2,1,0:T(8,128)(2,1)S(1)}, u32[]{:S(2)}, u32[]{:S(2)}) collective-permute-start(bf16[2,4,12,16,128]{4,3,2,1,0:T(8,128)(2,1)S(1)} %bitcast.13), channel_id=1, source_target_pairs={{0,1},{1,2},{2,3},{3,0},{4,5},{5,6},{6,7},{7,4},{8,9},{9,10},{10,1... | collective-permute-start | bytes 1179656 | tf_op jit(solution)/shard_map/ppermute | solution.py:314
  89.6 15.5 %collective-permute-start.4 = (bf16[2,4,12,16,128]{4,3,2,1,0:T(8,128)(2,1)S(1)}, bf16[2,4,12,16,128]{4,3,2,1,0:T(8,128)(2,1)S(1)}, u32[]{:S(2)}, u32[]{:S(2)}) collective-permute-start(bf16[2,4,12,16,128]{4,3,2,1,0:T(8,128)(2,1)S(1)} %bitcast.12), channel_id=1, source_target_pairs={{0,2},{1,3},{2,0},{3,1},{4,6},{5,7},{6,4},{7,5},{8,10},{9,11},{10,... | collective-permute-start | bytes 1179656 | tf_op jit(solution)/shard_map/ppermute | solution.py:314
  92.6 18.4 %collective-permute-start.5 = (bf16[2,4,12,16,128]{4,3,2,1,0:T(8,128)(2,1)S(1)}, bf16[2,4,12,16,128]{4,3,2,1,0:T(8,128)(2,1)S(1)}, u32[]{:S(2)}, u32[]{:S(2)}) collective-permute-start(bf16[2,4,12,16,128]{4,3,2,1,0:T(8,128)(2,1)S(1)} %bitcast.11), channel_id=1, source_target_pairs={{0,3},{1,0},{2,1},{3,2},{4,7},{5,4},{6,5},{7,6},{8,11},{9,8},{10,9... | collective-permute-start | bytes 1179656 | tf_op jit(solution)/shard_map/ppermute | solution.py:314
  111.2 5.7 %copy-start.5 = (bf16[4,4,12,16,128]{4,3,2,1,0:T(8,128)(2,1)}, bf16[4,4,12,16,128]{4,3,2,1,0:T(8,128)(2,1)S(1)}, u32[]{:S(2)}) copy-start(bf16[4,4,12,16,128]{4,3,2,1,0:T(8,128)(2,1)S(1)} %pad_maximum_fusion.refs_4_.mine_hbm) | copy-start | bytes 2359300
  111.2 5.7 %collective-permute-start.6 = (bf16[4,4,12,16,128]{4,3,2,1,0:T(8,128)(2,1)S(1)}, bf16[4,4,12,16,128]{4,3,2,1,0:T(8,128)(2,1)S(1)}, u32[]{:S(2)}, u32[]{:S(2)}) collective-permute-start(bf16[4,4,12,16,128]{4,3,2,1,0:T(8,128)(2,1)S(1)} %pad_maximum_fusion.refs_4_.mine_hbm), channel_id=1, source_target_pairs={{0,64},{64,0},{1,65},{65,1},{2,66},{66,2},{3,67},{67,3},{4,68},{68... | collective-permute-start | bytes 2359304 | tf_op jit(solution)/shard_map/ppermute | solution.py:352
  113.2 3.7 %collective-permute-start.7 = (bf16[4,2,12,16,128]{4,3,2,1,0:T(8,128)(2,1)S(1)}, bf16[4,2,12,16,128]{4,3,2,1,0:T(8,128)(2,1)S(1)}, u32[]{:S(2)}, u32[]{:S(2)}) collective-permute-start(bf16[4,2,12,16,128]{4,3,2,1,0:T(8,128)(2,1)S(1)} %get-tuple-element.32), channel_id=1, source_target_pairs={{0,64},{64,0},{128,192},{192,128},{1,65},{65,1},{129,193},{193,129... | collective-permute-start | bytes 1179656 | tf_op jit(solution)/shard_map/ppermute | solution.py:310
  141.9 28.3 %all-to-all-start.2 = ((bf16[16,4,6,16,128]{4,3,2,1,0:T(8,128)(2,1)}), bf16[16,4,6,16,128]{4,3,2,1,0:T(8,128)(2,1)}, u32[]{:S(2)}, u32[]{:S(2)}) async-start(bf16[16,4,6,16,128]{4,3,2,1,0:T(8,128)(2,1)} %copy-done), calls=%async_computation.2 | async-start | bytes 3145728 | tf_op jit(solution)/shard_map/all_to_all | solution.py:365
  149.4 4.2 %collective-permute-start.9 = (bf16[4,2,4,6,16,128]{5,4,3,2,1,0:T(8,128)(2,1)S(1)}, bf16[4,2,4,6,16,128]{5,4,3,2,1,0:T(8,128)(2,1)S(1)}, u32[]{:S(2)}, u32[]{:S(2)}) collective-permute-start(bf16[4,2,4,6,16,128]{5,4,3,2,1,0:T(8,128)(2,1)S(1)} %shard_map.61), channel_id=1, source_target_pairs={{0,64},{64,0},{128,192},{192,128},{1,65},{65,1},{129,193},{193,129... | collective-permute-start | bytes 2359304 | tf_op jit(solution)/shard_map/ppermute | solution.py:310
  151.3 13.4 %collective-permute-start.8 = (bf16[2,4,12,16,128]{4,3,2,1,0:T(8,128)(2,1)S(1)}, bf16[2,4,12,16,128]{4,3,2,1,0:T(8,128)(2,1)S(1)}, u32[]{:S(2)}, u32[]{:S(2)}) collective-permute-start(bf16[2,4,12,16,128]{4,3,2,1,0:T(8,128)(2,1)S(1)} %shard_map.59), channel_id=1, source_target_pairs={{0,128},{64,192},{128,0},{192,64},{1,129},{65,193},{129,1},{193,65... | collective-permute-start | bytes 1179656 | tf_op jit(solution)/shard_map/ppermute | solution.py:310
  157.7 7.1 %collective-permute-start.10 = (bf16[2,16,2,16,128]{4,3,2,1,0:T(8,128)(2,1)S(1)}, bf16[2,16,2,16,128]{4,3,2,1,0:T(8,128)(2,1)S(1)}, u32[]{:S(2)}, u32[]{:S(2)}) collective-permute-start(bf16[2,16,2,16,128]{4,3,2,1,0:T(8,128)(2,1)S(1)} %get-tuple-element.36), channel_id=1, source_target_pairs={{0,64},{64,0},{128,192},{192,128},{1,65},{65,1},{129,193},{193,129... | collective-permute-start | bytes 786440 | tf_op jit(solution)/shard_map/ppermute | solution.py:310
  178.8 5.9 %copy-start.10 = (bf16[2,16,16,128]{3,2,1,0:T(8,128)(2,1)S(1)}, bf16[2,16,16,128]{3,2,1,0:T(8,128)(2,1)}, u32[]{:S(2)}) copy-start(bf16[2,16,16,128]{3,2,1,0:T(8,128)(2,1)} %copy-done.9) | copy-start | bytes 393220
  178.8 18.6 %copy-start.7 = (bf16[2,16,2,16,128]{4,3,2,1,0:T(8,128)(2,1)S(1)}, bf16[2,16,2,16,128]{4,3,2,1,0:T(8,128)(2,1)}, u32[]{:S(2)}) copy-start(bf16[2,16,2,16,128]{4,3,2,1,0:T(8,128)(2,1)} %copy-done.6) | copy-start | bytes 786436
  178.8 18.6 %all-to-all-start.3 = ((bf16[16,4,3,16,128]{4,3,2,1,0:T(8,128)(2,1)}), bf16[16,4,3,16,128]{4,3,2,1,0:T(8,128)(2,1)S(1)}, u32[]{:S(2)}, u32[]{:S(2)}) async-start(bf16[16,4,3,16,128]{4,3,2,1,0:T(8,128)(2,1)} %shard_map.64), calls=%async_computation.3 | async-start | bytes 1572864 | tf_op jit(solution)/shard_map/all_to_all | solution.py:397
  184.6 6.9 %collective-permute-start.11 = (bf16[2,16,16,128]{3,2,1,0:T(8,128)(2,1)S(1)}, bf16[2,16,16,128]{3,2,1,0:T(8,128)(2,1)S(1)}, u32[]{:S(2)}, u32[]{:S(2)}) collective-permute-start(bf16[2,16,16,128]{3,2,1,0:T(8,128)(2,1)S(1)} %copy-done.10), channel_id=1, source_target_pairs={{0,128},{64,192},{128,0},{192,64},{1,129},{65,193},{129,1},{193,65... | collective-permute-start | bytes 393224 | tf_op jit(solution)/shard_map/ppermute | solution.py:310
  191.5 3.2 %collective-permute-start.12 = (bf16[2,16,16,128]{3,2,1,0:T(8,128)(2,1)S(1)}, bf16[2,16,16,128]{3,2,1,0:T(8,128)(2,1)S(1)}, u32[]{:S(2)}, u32[]{:S(2)}) collective-permute-start(bf16[2,16,16,128]{3,2,1,0:T(8,128)(2,1)S(1)} %pad_maximum_fusion.1), channel_id=1, source_target_pairs={{0,64},{64,0},{128,192},{192,128},{1,65},{65,1},{129,193},{193,129... | collective-permute-start | bytes 393224 | tf_op jit(solution)/shard_map/ppermute | solution.py:310
  (5 other events, 4.1 us)
